TPU v7x, 32 devices: a whole 2x2x4 slice. The times are simulated.
32 devices in a mesh: batch: 2 (over core), seq: 16 (over z, y, x).
Axes of the slice: x: 2, y: 2, z: 4, core: 2. Of those that a mesh axis runs over, the one named last changes fastest.
Arguments:
- tokens: float32 [4, 4096, 768], P('batch', 'seq'), may hold values from -6 to 6
- cotangent: float32 [4, 4096, 768], P('batch', 'seq'), may hold values from -6 to 6
- prefix_len: int32 [4], P('batch'), may hold values from 409 to 4096, as said below
- query_routes: int32 [4, 512], P('batch'), may hold values from 0 to 4095, as said below
- key_routes: int32 [4, 512], P('batch'), may hold values from 0 to 4095, as said below
- ffn_routes: int32 [4, 512], P('batch'), may hold values from 0 to 4095, as said below
- light_qkv: bfloat16 [768, 1536], P(('batch', 'seq')), may hold values from -0.21875 to 0.21875
- light_out: bfloat16 [768, 512], P(('batch', 'seq')), may hold values from -1 to 1
- heavy_qkv: bfloat16 [768, 2304], P(('batch', 'seq')), may hold values from -0.21875 to 0.21875
- heavy_out: bfloat16 [768, 768], P(('batch', 'seq')), may hold values from -0.875 to 0.875
- light_ff_in: bfloat16 [768, 2048], P(('batch', 'seq')), may hold values from -0.21875 to 0.21875
- light_ff_out: bfloat16 [768, 1024], P(('batch', 'seq')), may hold values from -0.1875 to 0.1875
- heavy_ff_in: bfloat16 [768, 8192], P(('batch', 'seq')), may hold values from -0.21875 to 0.21875
- heavy_ff_out: bfloat16 [768, 4096], P(('batch', 'seq')), may hold values from -0.1875 to 0.1875
- gains: bfloat16 [768, 2], P(('batch', 'seq')), may hold values from 0.099609375 to 1.8984375
- routers: bfloat16 [768, 3], P(('batch', 'seq')), may hold values from -0.21875 to 0.21875
Outputs:
- output: float32 [4, 4096, 768], P('batch', 'seq')
- grad_tokens: float32 [4, 4096, 768], P('batch', 'seq')
- grad_light_qkv: float32 [768, 1536], P(('batch', 'seq'))
- grad_light_out: float32 [768, 512], P(('batch', 'seq'))
- grad_heavy_qkv: float32 [768, 2304], P(('batch', 'seq'))
- grad_heavy_out: float32 [768, 768], P(('batch', 'seq'))
- grad_light_ff_in: float32 [768, 2048], P(('batch', 'seq'))
- grad_light_ff_out: float32 [768, 1024], P(('batch', 'seq'))
- grad_heavy_ff_in: float32 [768, 8192], P(('batch', 'seq'))
- grad_heavy_ff_out: float32 [768, 4096], P(('batch', 'seq'))
- grad_gains: float32 [768, 2], P(('batch', 'seq'))
- grad_routers: float32 [768, 3], P(('batch', 'seq'))
Inputs may be any that keep to these rules, and one draw needn't show every extreme that they name: `prefix_len`: in each aligned group of 2 sequences, one sequence has a prefix of 3904 tokens or more; all others have a prefix of 409 to 2048 tokens. `query_routes`: each row lists 512 distinct token positions of its sequence in increasing order, the first being 0 and the last 4095. At most 64 of them lie among the 256 positions of one device along seq, and in every row some device holds exactly 64. `key_routes`: each row lists 512 distinct token positions of its sequence in increasing order, the first being 0 and the last 4095. At most 64 of them lie among the 256 positions of one device along seq, and in every row some device holds exactly 64. `ffn_routes`: each row lists 512 distinct token positions of its sequence in increasing order, the first being 0 and the last 4095. At most 64 of them lie among the 256 positions of one device along seq, and in every row some device holds exactly 64.
All inputs are finite; a program needn't handle non-finite values.
Results may differ from a plain program's by a relative error of at most 0.0003.
Values may be sent and summed in bfloat16 or wider, within the bound.
No kernel may reach another device: no remote copies, remote signals or barrier semaphores. Data moves between devices by JAX's collectives and lax.ppermute only.
A program may use at most 320 MiB of HBM per device.

v0:
```python
import jax
import jax.numpy as jnp
from jax import lax
from jax.sharding import PartitionSpec as P

HL = 8
HH = 12
DH = 64
FL = 1024
FH = 4096
W = 128
IL = 512
IH = 768


precise_mode = lax.Precision.HIGHEST
eps = 1e-06


def extended(value, sides, width):
    for axis, dim in sides:
        size, length = (lax.axis_size(axis), value.shape[dim])
        up = [(i, (i + 1) % size) for i in range(size - 1)]
        down = [(j, i) for i, j in up]
        last = lax.slice_in_dim(value, length - width, length, axis=dim)
        initial = lax.slice_in_dim(value, 0, width, axis=dim)
        before = lax.ppermute(last, axis, up)
        after = lax.ppermute(initial, axis, down)
        value = jnp.concatenate([before, value, after], axis=dim)
    return value


def shifted(value, axis, by):
    length = lax.axis_size(axis)
    pairs = [(i, i + by) for i in range(length) if 0 <= i + by < length]
    return lax.ppermute(value, axis, pairs)


def rms_scale(values, gain_vec):
    return values * lax.rsqrt(jnp.mean(values * values, axis=-1, keepdims=True) + eps) * gain_vec


def gelu_tanh(values):
    return jax.nn.gelu(values, approximate=True)


def product(formula, left_side, right_side):
    return jnp.einsum(
        formula, left_side, right_side, precision=precise_mode, preferred_element_type=jnp.float32
    )


def masked_softmax(scores, allowed):
    return jax.nn.softmax(jnp.where(allowed, scores, -1e30), axis=-1)


def route_slots(route_row, row_begin, span_rows, capacity):
    count_below = jnp.sum((route_row < row_begin).astype(jnp.int32))
    count_upper = jnp.sum((route_row < row_begin + span_rows).astype(jnp.int32))
    slot_index = count_below + jnp.arange(capacity, dtype=jnp.int32)
    present = slot_index < count_upper
    positions = jnp.take(route_row, jnp.clip(slot_index, 0, route_row.shape[0] - 1))
    return (positions, present)


def local_picker(route_row, row_begin, span_rows, capacity):
    positions, present = route_slots(route_row, row_begin, span_rows, capacity)
    offsets = positions - row_begin
    matched = (offsets[:, None] == jnp.arange(span_rows, dtype=jnp.int32)[None, :]) & present[
        :, None
    ]
    return (positions, matched.astype(jnp.float32))


def every_slot(route_row, span_rows, devices, capacity):

    def one_device(row_begin):
        return route_slots(route_row, row_begin, span_rows, capacity)

    starts = jnp.arange(devices, dtype=jnp.int32) * span_rows
    positions, present = jax.vmap(one_device)(starts)
    return (positions.reshape(-1), present.reshape(-1))


def light_attend(queries, keys_values, query_pos, key_pos, prefix, full_len):
    seqs_here = queries.shape[0]
    rows_here = queries.shape[1]
    span_rows = keys_values.shape[1]
    query_heads = queries.reshape(seqs_here, rows_here, HL, DH)
    key_heads = keys_values[:, :, :IL].reshape(seqs_here, span_rows, HL, DH)
    value_heads = keys_values[:, :, IL:].reshape(seqs_here, span_rows, HL, DH)
    scores = product("sthd,suhd->shtu", query_heads, key_heads) * DH ** (-0.5)
    within_window = jnp.abs(query_pos[:, None] - key_pos[None, :]) < W
    inside = (key_pos >= 0) & (key_pos < full_len)
    causal = (key_pos[None, None, :] <= query_pos[None, :, None]) | (
        key_pos[None, None, :] < prefix[:, None, None]
    )
    allowed = causal & within_window[None] & inside[None, None, :]
    attn_probs = masked_softmax(scores, allowed[:, None])
    mixed_heads = product("shtu,suhd->sthd", attn_probs, value_heads)
    return mixed_heads.reshape(seqs_here, rows_here, IL)


def heavy_attend(queries, key_mat, value_mat, query_pos, key_pos, key_present, prefix):
    seqs_here = queries.shape[0]
    query_heads = queries.reshape(seqs_here, queries.shape[1], HH, DH)
    key_heads = key_mat.reshape(seqs_here, key_mat.shape[1], HH, DH)
    value_heads = value_mat.reshape(seqs_here, value_mat.shape[1], HH, DH)
    scores = product("schd,skhd->shck", query_heads, key_heads) * DH ** (-0.5)
    causal = (key_pos[:, None, :] <= query_pos[:, :, None]) | (
        key_pos[:, None, :] < prefix[:, None, None]
    )
    allowed = causal & key_present[:, None, :]
    attn_probs = masked_softmax(scores, allowed[:, None])
    mixed_heads = product("shck,skhd->schd", attn_probs, value_heads)
    return mixed_heads.reshape(seqs_here, queries.shape[1], IH)


def on_device(
    tokens,
    cotangent,
    prefix_len,
    query_routes,
    key_routes,
    ffn_routes,
    light_qkv,
    light_out,
    heavy_qkv,
    heavy_out,
    light_ff_in,
    light_ff_out,
    heavy_ff_in,
    heavy_ff_out,
    gains,
    routers,
):
    rows_here = tokens.shape[1]
    seq_devices = lax.axis_size("seq")
    row_begin = lax.axis_index("seq") * rows_here
    full_len = rows_here * seq_devices
    capacity = rows_here // 4
    query_pos_local = row_begin + jnp.arange(rows_here, dtype=jnp.int32)
    key_pos_local = row_begin - W + jnp.arange(rows_here + 2 * W, dtype=jnp.int32)

    def picker(route_row):
        return local_picker(route_row, row_begin, rows_here, capacity)

    def slots_all(route_row):
        return every_slot(route_row, rows_here, seq_devices, capacity)

    query_at, query_pick = jax.vmap(picker)(query_routes)
    _, key_pick = jax.vmap(picker)(key_routes)
    _, ffn_pick = jax.vmap(picker)(ffn_routes)
    key_all_at, key_all_present = jax.vmap(slots_all)(key_routes)

    def first_part(tokens_in, gain_pair, light_proj, heavy_proj, router_cols):
        normed = rms_scale(tokens_in, gain_pair[:, 0])
        light_kv = product("std,de->ste", normed, light_proj[:, IL:])
        key_rows = product("sct,std->scd", key_pick, normed)
        return (normed, light_kv, key_rows)

    def second_part(tokens_in, normed, kv_ext, heavy_all, weight_set):
        (
            light_qkv_full,
            light_out_full,
            heavy_qkv_full,
            heavy_out_full,
            light_ff_in_full,
            light_ff_out_full,
            heavy_ff_in_full,
            heavy_ff_out_full,
            gain_pair,
            router_cols,
        ) = weight_set
        light_query = product("std,de->ste", normed, light_qkv_full[:, :IL])
        attended = jax.checkpoint(light_attend)(
            light_query, kv_ext, query_pos_local, key_pos_local, prefix_len, jnp.int32(full_len)
        )
        light_branch = product("sti,di->std", attended, light_out_full)
        query_rows = product("sct,std->scd", query_pick, normed)
        query_score = jax.nn.sigmoid(product("scd,d->sc", query_rows, router_cols[:, 0]))
        heavy_query = product("scd,di->sci", query_rows, heavy_qkv_full[:, :IH])
        key_score = jax.nn.sigmoid(product("skd,d->sk", heavy_all, router_cols[:, 1]))
        key_value = product("skd,de->ske", heavy_all, heavy_qkv_full[:, IH:])
        heavy_keys = key_value[..., :IH]
        heavy_values = key_value[..., IH:] * key_score[..., None]
        heavy_mixed = jax.checkpoint(heavy_attend)(
            heavy_query, heavy_keys, heavy_values, query_at, key_all_at, key_all_present, prefix_len
        )
        heavy_rows = product("sci,di->scd", heavy_mixed, heavy_out_full) * query_score[..., None]
        hidden = tokens_in + light_branch + product("sct,scd->std", query_pick, heavy_rows)
        second = rms_scale(hidden, gain_pair[:, 1])
        gate_up = product("std,de->ste", second, light_ff_in_full)
        light_ff = product(
            "stf,df->std", gelu_tanh(gate_up[..., :FL]) * gate_up[..., FL:], light_ff_out_full
        )
        ffn_rows = product("sct,std->scd", ffn_pick, second)
        ffn_score = jax.nn.sigmoid(product("scd,d->sc", ffn_rows, router_cols[:, 2]))
        heavy_gate_up = product("scd,de->sce", ffn_rows, heavy_ff_in_full)
        heavy_ff = (
            product(
                "scf,df->scd",
                gelu_tanh(heavy_gate_up[..., :FH]) * heavy_gate_up[..., FH:],
                heavy_ff_out_full,
            )
            * ffn_score[..., None]
        )
        return hidden + light_ff + product("sct,scd->std", ffn_pick, heavy_ff)

    gathered = (
        lax.all_gather(light_qkv, ("batch", "seq"), axis=0, tiled=True),
        lax.all_gather(light_out, ("batch", "seq"), axis=0, tiled=True),
        lax.all_gather(heavy_qkv, ("batch", "seq"), axis=0, tiled=True),
        lax.all_gather(heavy_out, ("batch", "seq"), axis=0, tiled=True),
        lax.all_gather(light_ff_in, ("batch", "seq"), axis=0, tiled=True),
        lax.all_gather(light_ff_out, ("batch", "seq"), axis=0, tiled=True),
        lax.all_gather(heavy_ff_in, ("batch", "seq"), axis=0, tiled=True),
        lax.all_gather(heavy_ff_out, ("batch", "seq"), axis=0, tiled=True),
        lax.all_gather(gains, ("batch", "seq"), axis=0, tiled=True),
        lax.all_gather(routers, ("batch", "seq"), axis=0, tiled=True),
    )
    weight_set = tuple((piece.astype(jnp.float32) for piece in gathered))
    sent_parts = first_part(tokens, weight_set[8], weight_set[0], weight_set[2], weight_set[9])
    normed, light_kv, heavy_send = sent_parts
    kv_ext = extended(light_kv, (("seq", 1),), W)
    heavy_all = lax.all_gather(heavy_send, "seq", axis=1, tiled=True)
    output = second_part(tokens, normed, kv_ext, heavy_all, weight_set)
    regathered = (
        lax.all_gather(light_qkv, ("batch", "seq"), axis=0, tiled=True),
        lax.all_gather(light_out, ("batch", "seq"), axis=0, tiled=True),
        lax.all_gather(heavy_qkv, ("batch", "seq"), axis=0, tiled=True),
        lax.all_gather(heavy_out, ("batch", "seq"), axis=0, tiled=True),
        lax.all_gather(light_ff_in, ("batch", "seq"), axis=0, tiled=True),
        lax.all_gather(light_ff_out, ("batch", "seq"), axis=0, tiled=True),
        lax.all_gather(heavy_ff_in, ("batch", "seq"), axis=0, tiled=True),
        lax.all_gather(heavy_ff_out, ("batch", "seq"), axis=0, tiled=True),
        lax.all_gather(gains, ("batch", "seq"), axis=0, tiled=True),
        lax.all_gather(routers, ("batch", "seq"), axis=0, tiled=True),
    )
    weight_back = tuple((piece.astype(jnp.float32) for piece in regathered))
    _, first_back = jax.vjp(
        first_part, tokens, weight_back[8], weight_back[0], weight_back[2], weight_back[9]
    )
    _, second_back = jax.vjp(second_part, tokens, normed, kv_ext, heavy_all, weight_back)
    grad_tokens_late, grad_normed, grad_kv_ext, grad_heavy_all, grad_weights_late = second_back(
        cotangent
    )
    left_rim = grad_kv_ext[:, :W]
    right_rim = grad_kv_ext[:, W + rows_here :]
    from_next = shifted(left_rim, "seq", -1)
    from_prev = shifted(right_rim, "seq", 1)
    grad_light_kv = grad_kv_ext[:, W : W + rows_here]
    grad_light_kv = grad_light_kv.at[:, :W].add(from_prev).at[:, rows_here - W :].add(from_next)
    grad_heavy_send = lax.psum_scatter(grad_heavy_all, "seq", scatter_dimension=1, tiled=True)
    grad_tokens_early, grad_gains_early, grad_light_early, grad_heavy_early, grad_routers_early = (
        first_back((grad_normed, grad_light_kv, grad_heavy_send))
    )
    grad_tokens = grad_tokens_early + grad_tokens_late
    summed = (
        lax.psum_scatter(
            grad_weights_late[0] + grad_light_early,
            ("batch", "seq"),
            scatter_dimension=0,
            tiled=True,
        ),
        lax.psum_scatter(grad_weights_late[1], ("batch", "seq"), scatter_dimension=0, tiled=True),
        lax.psum_scatter(
            grad_weights_late[2] + grad_heavy_early,
            ("batch", "seq"),
            scatter_dimension=0,
            tiled=True,
        ),
        lax.psum_scatter(grad_weights_late[3], ("batch", "seq"), scatter_dimension=0, tiled=True),
        lax.psum_scatter(grad_weights_late[4], ("batch", "seq"), scatter_dimension=0, tiled=True),
        lax.psum_scatter(grad_weights_late[5], ("batch", "seq"), scatter_dimension=0, tiled=True),
        lax.psum_scatter(grad_weights_late[6], ("batch", "seq"), scatter_dimension=0, tiled=True),
        lax.psum_scatter(grad_weights_late[7], ("batch", "seq"), scatter_dimension=0, tiled=True),
        lax.psum_scatter(
            grad_weights_late[8] + grad_gains_early,
            ("batch", "seq"),
            scatter_dimension=0,
            tiled=True,
        ),
        lax.psum_scatter(
            grad_weights_late[9] + grad_routers_early,
            ("batch", "seq"),
            scatter_dimension=0,
            tiled=True,
        ),
    )
    return (
        output,
        grad_tokens,
        summed[0],
        summed[1],
        summed[2],
        summed[3],
        summed[4],
        summed[5],
        summed[6],
        summed[7],
        summed[8],
        summed[9],
    )


def solution(mesh):
    in_specs = (
        P("batch", "seq", None),
        P("batch", "seq", None),
        P("batch"),
        P("batch", None),
        P("batch", None),
        P("batch", None),
        P(("batch", "seq"), None),
        P(("batch", "seq"), None),
        P(("batch", "seq"), None),
        P(("batch", "seq"), None),
        P(("batch", "seq"), None),
        P(("batch", "seq"), None),
        P(("batch", "seq"), None),
        P(("batch", "seq"), None),
        P(("batch", "seq"), None),
        P(("batch", "seq"), None),
    )
    out_specs = (
        P("batch", "seq", None),
        P("batch", "seq", None),
        P(("batch", "seq"), None),
        P(("batch", "seq"), None),
        P(("batch", "seq"), None),
        P(("batch", "seq"), None),
        P(("batch", "seq"), None),
        P(("batch", "seq"), None),
        P(("batch", "seq"), None),
        P(("batch", "seq"), None),
        P(("batch", "seq"), None),
        P(("batch", "seq"), None),
    )
    return jax.shard_map(
        on_device, mesh=mesh, in_specs=in_specs, out_specs=out_specs, check_vma=False
    )
```

profile of v0, /device:TPU:0, one launch (start us, length us, event | category | flops | bytes accessed | tf_op | source)
XLA Modules:
  0.0 1992.0 jit_solution(646759785898077566)
XLA Ops:
  11.7 69.5 %all-gather = bf16[32,24,2]{1,2,0:T(2,128)(2,1)S(1)} all-gather(bf16[1,24,2]{1,2,0:T(2,128)(2,1)} %bitcast.276), channel_id=1, replica_groups=mesh['batch'=2,'seq'=16] {'batch','seq'}, dimensions={0}, use_global_device_ids=true | all-gather | bytes 3168 | tf_op jit(solution)/shard_map/all_gather | solution.py:219
  94.0 17.7 gather_fusion
  111.9 63.8 %all-gather.1 = bf16[32,24,3]{1,2,0:T(4,128)(2,1)S(1)} all-gather(bf16[1,24,3]{1,2,0:T(4,128)(2,1)S(1)} %bitcast.275), channel_id=1, replica_groups=mesh['batch'=2,'seq'=16] {'batch','seq'}, dimensions={0}, use_global_device_ids=true | all-gather | bytes 4752 | tf_op jit(solution)/shard_map/all_gather | solution.py:220
  195.1 132.8 %all_gather.45 = bf16[768,512]{1,0:T(8,128)(2,1)} all-gather(bf16[24,512]{1,0:T(8,128)(2,1)S(1)} %copy-done.81), channel_id=1, replica_groups=mesh['batch'=2,'seq'=16] {'batch','seq'}, dimensions={0}, use_global_device_ids=true | all-gather | bytes 811008 | tf_op jit(solution)/shard_map/all_gather | solution.py:212
  374.5 18.7 fusion.55
  466.9 77.7 %all-gather.23.cloned.1.call-done = bf16[768,8192]{1,0:T(8,128)(2,1)} async-done(((bf16[24,8192]{1,0:T(8,128)(2,1)}), bf16[768,8192]{1,0:T(8,128)(2,1)}) %all-gather.23.cloned.1.call-update) | async-done | bytes 12582928 | tf_op jit(solution)/shard_map/all_gather | solution.py:217
  555.0 60.3 %all-gather.25.cloned.1.call-done = bf16[768,4096]{1,0:T(8,128)(2,1)} async-done(((bf16[24,4096]{1,0:T(8,128)(2,1)}), bf16[768,4096]{1,0:T(8,128)(2,1)}) %all-gather.25.cloned.1.call-update) | async-done | bytes 6291472 | tf_op jit(solution)/shard_map/all_gather | solution.py:218
  629.9 17.0 fusion.66
  730.5 20.1 %multiply_add_fusion = f32[2,1024,768]{2,1,0:T(8,128)} fusion(f32[768]{0:T(1024)S(1)} %copy-done.113, f32[2,1024]{1,0:T(2,128)S(1)} %fusion.148, f32[2,1024,768]{2,1,0:T(8,128)} %copy.195, f32[2,1024,768]{2,1,0:T(8,128)} %get-tuple-element.154, bf16[768,2304]{1,0:T(8,128)(2,1)} %all-gather.15.cloned.1.call-done), kind=kOutput, calls=%fused_computation.31 | convolution fusion | flops 28997320704 | bytes 21244928 | tf_op jit(solution)/shard_map/transpose(jvp(skd,de->ske))/dot_general | solution.py:48
  765.8 14.2 convolution_bitcast_fusion.2
  825.3 14.9 multiply_reduce_fusion
  877.7 18.6 collective-permute-done.2
  898.0 11.0 fusion.198
  932.5 12.5 convolution_bitcast_fusion.9
  951.8 36.9 %fusion.30 = f32[768,1536]{1,0:T(8,128)S(1)} fusion(f32[2,1024,768]{2,1,0:T(8,128)} %all-gather.13.cloned.1.call-done, f32[2,1024,768]{2,1,0:T(8,128)} %copy.195, f32[2,1024,768]{2,1,0:T(8,128)} %get-tuple-element.154), kind=kOutput, calls=%fused_computation.63 | convolution fusion | flops 28994174976 | bytes 23592960 | tf_op jit(solution)/shard_map/transpose(jvp(skd,de->ske))/dot_general | solution.py:48
  993.0 14.9 convolution_bitcast_fusion.1
  1008.9 24.8 %convolution_bitcast_fusion = f32[768,8192]{1,0:T(8,128)} fusion(f32[2,64,768]{2,1,0:T(8,128)S(1)} %copy-done.22, f32[2,64,4096]{2,1,0:T(8,128)} %copy-done.32, f32[2,64,4096]{2,1,0:T(8,128)} %copy-done.31), kind=kOutput, calls=%fused_computation.4 | convolution fusion | flops 9664724992 | bytes 29753344 | tf_op jit(solution)/shard_map/transpose(jvp(scd,de->sce))/dot_general | solution.py:48
  1069.5 48.9 %all-reduce.19 = (f32[768,2]{0,1:T(2,128)S(1)}, f32[768,3]{0,1:T(4,128)S(1)}) all-reduce(f32[768,2]{0,1:T(2,128)S(1)} %pad_add_fusion.19, f32[768,3]{0,1:T(4,128)S(1)} %pad_add_fusion.18), channel_id=11, replica_groups=mesh['batch'=2,'seq'=16] {'batch','seq'}, use_global_device_ids=true, to_apply=%region_36.38.clone | all-reduce | flops 3840 | bytes 30720
  1126.7 102.7 %reduce-scatter.18.cloned.1.call-done = f32[24,512]{1,0:T(8,128)} async-done(((f32[768,512]{1,0:T(8,128)}), f32[24,512]{1,0:T(8,128)}) %reduce-scatter.18.cloned.1.call-update) | async-done | bytes 49168 | tf_op jit(solution)/shard_map/reduce_scatter | solution.py:266
  1229.4 104.9 %reduce-scatter.22.cloned.1.call-done = f32[24,768]{1,0:T(8,128)} async-done(((f32[768,768]{1,0:T(8,128)}), f32[24,768]{1,0:T(8,128)}) %reduce-scatter.22.cloned.1.call-update) | async-done | bytes 73744 | tf_op jit(solution)/shard_map/reduce_scatter | solution.py:273
  1334.2 111.9 %reduce-scatter.16.cloned.1.call-done = f32[24,1536]{1,0:T(8,128)} async-done(((f32[768,1536]{1,0:T(8,128)}), f32[24,1536]{1,0:T(8,128)}) %reduce-scatter.16.cloned.1.call-update) | async-done | bytes 147472 | tf_op jit(solution)/shard_map/reduce_scatter | solution.py:260
  1446.1 125.3 %reduce-scatter.20.cloned.1.call-done = f32[24,2304]{1,0:T(8,128)} async-done(((f32[768,2304]{1,0:T(8,128)}), f32[24,2304]{1,0:T(8,128)}) %reduce-scatter.20.cloned.1.call-update) | async-done | bytes 221200 | tf_op jit(solution)/shard_map/reduce_scatter | solution.py:267
  1571.4 161.2 %reduce-scatter.28.cloned.1.call-done = f32[24,4096]{1,0:T(8,128)} async-done(((f32[768,4096]{1,0:T(8,128)}), f32[24,4096]{1,0:T(8,128)}) %reduce-scatter.28.cloned.1.call-update) | async-done | bytes 393232 | tf_op jit(solution)/shard_map/reduce_scatter | solution.py:277
  1732.7 252.6 %reduce-scatter.26.cloned.1.call-done = f32[24,8192]{1,0:T(8,128)} async-done(((f32[768,8192]{1,0:T(8,128)}), f32[24,8192]{1,0:T(8,128)}) %reduce-scatter.26.cloned.1.call-update) | async-done | bytes 786448 | tf_op jit(solution)/shard_map/reduce_scatter | solution.py:276
  (472 shorter events, 443.2 us)
Async XLA Ops:
  7.2 172.0 %all-gather.11.cloned.1.call-start = ((), (), s32[]{:S(2)}) async-start(), calls=%async_computation.9 | async-start | bytes 2433024 | tf_op jit(solution)/shard_map/all_gather | solution.py:211
  7.9 358.5 %all-gather.15.cloned.1.call-start = ((), (), s32[]{:S(2)}) async-start(), calls=%async_computation.11 | async-start | bytes 3649536 | tf_op jit(solution)/shard_map/all_gather | solution.py:213
  8.7 359.9 %all-gather.13.cloned.1.call-start = ((), (), s32[]{:S(2)}) async-start(), calls=%async_computation.10 | async-start | bytes 6684672 | tf_op jit(solution)/shard_map/all_gather | solution.py:226
  82.0 245.9 %copy-start.56 = (f32[768]{0:T(1024)}, f32[768]{0:T(1024)S(1)}, u32[]{:S(2)}) copy-start(f32[768]{0:T(1024)S(1)} %get-tuple-element.135) | copy-start | bytes 9220
  83.8 244.1 %copy-start.58 = (f32[2,256]{1,0:T(2,128)}, f32[2,256]{1,0:T(2,128)S(1)}, u32[]{:S(2)}) copy-start(f32[2,256]{1,0:T(2,128)S(1)} %fusion.168) | copy-start | bytes 6148
  85.9 347.4 %all-gather.17.cloned.1.call-start = ((), (), s32[]{:S(2)}) async-start(), calls=%async_computation.12 | async-start | bytes 1216512 | tf_op jit(solution)/shard_map/all_gather | solution.py:214
  86.5 356.0 %all-gather.19.cloned.1.call-start = ((), (), s32[]{:S(2)}) async-start(), calls=%async_computation.13 | async-start | bytes 3244032 | tf_op jit(solution)/shard_map/all_gather | solution.py:215
  87.1 364.2 %all-gather.21.cloned.1.call-start = ((), (), s32[]{:S(2)}) async-start(), calls=%async_computation.14 | async-start | bytes 1622016 | tf_op jit(solution)/shard_map/all_gather | solution.py:216
  87.7 457.0 %all-gather.23.cloned.1.call-start = ((), (), s32[]{:S(2)}) async-start(), calls=%async_computation.15 | async-start | bytes 12976128 | tf_op jit(solution)/shard_map/all_gather | solution.py:217
  88.4 526.9 %all-gather.25.cloned.1.call-start = ((), (), s32[]{:S(2)}) async-start(), calls=%async_computation.16 | async-start | bytes 6488064 | tf_op jit(solution)/shard_map/all_gather | solution.py:218
  89.2 971.5 %reduce-scatter.14.cloned.1.call-start = ((), (), s32[]{:S(2)}) async-start(), calls=%async_computation.17 | async-start | bytes 6684672 | tf_op jit(solution)/shard_map/reduce_scatter | solution.py:254
  185.3 146.6 %collective-permute-start = (f32[2,128,1024]{2,1,0:T(8,128)}, f32[2,128,1024]{2,1,0:T(8,128)}, u32[]{:S(2)}, u32[]{:S(2)}) collective-permute-start(f32[2,128,1024]{2,1,0:T(8,128)} %get-tuple-element.166), channel_id=1, source_target_pairs={{0,1},{1,2},{2,3},{3,4},{4,5},{5,6},{6,7},{7,8},{8,9},{9,10},{10,1... | collective-permute-start | bytes 3145736 | tf_op jit(solution)/shard_map/ppermute | solution.py:27
  190.5 141.4 %collective-permute-start.1 = (f32[2,128,1024]{2,1,0:T(8,128)}, f32[2,128,1024]{2,1,0:T(8,128)}, u32[]{:S(2)}, u32[]{:S(2)}) collective-permute-start(f32[2,128,1024]{2,1,0:T(8,128)} %get-tuple-element.167), channel_id=1, source_target_pairs={{1,0},{2,1},{3,2},{4,3},{5,4},{6,5},{7,6},{8,7},{9,8},{10,9},{11,1... | collective-permute-start | bytes 3145736 | tf_op jit(solution)/shard_map/ppermute | solution.py:28
  441.2 209.2 %copy-start.16 = (f32[2,256,768]{2,1,0:T(8,128)}, f32[2,256,768]{2,1,0:T(8,128)S(1)}, u32[]{:S(2)}) copy-start(f32[2,256,768]{2,1,0:T(8,128)S(1)} %get-tuple-element.178) | copy-start | bytes 4718596
  750.7 372.0 %reduce-scatter.30.cloned.1.call-start = ((), (), s32[]{:S(2)}) async-start(), calls=%async_computation.25 | async-start | bytes 3244032
  764.4 362.3 %reduce-scatter.24.cloned.1.call-start = ((), (), s32[]{:S(2)}) async-start(), calls=%async_computation.22 | async-start | bytes 6488064 | tf_op jit(solution)/shard_map/reduce_scatter | solution.py:274
  780.0 449.4 %reduce-scatter.18.cloned.1.call-start = ((), (), s32[]{:S(2)}) async-start(), calls=%async_computation.19 | async-start | bytes 1622016 | tf_op jit(solution)/shard_map/reduce_scatter | solution.py:266
  846.4 487.8 %reduce-scatter.22.cloned.1.call-start = ((), (), s32[]{:S(2)}) async-start(), calls=%async_computation.21 | async-start | bytes 2433024 | tf_op jit(solution)/shard_map/reduce_scatter | solution.py:273
  866.9 29.5 %collective-permute-start.2 = (f32[2,128,1024]{2,1,0:T(8,128)}, f32[2,128,1024]{2,1,0:T(8,128)S(1)}, u32[]{:S(2)}, u32[]{:S(2)}) collective-permute-start(f32[2,128,1024]{2,1,0:T(8,128)} %fusion.73), channel_id=1, source_target_pairs={{0,1},{1,2},{2,3},{3,4},{4,5},{5,6},{6,7},{7,8},{8,9},{9,10},{10,1... | collective-permute-start | bytes 3145736 | tf_op jit(solution)/shard_map/ppermute | solution.py:36
  875.7 570.4 %reduce-scatter.16.cloned.1.call-start = ((), (), s32[]{:S(2)}) async-start(), calls=%async_computation.18 | async-start | bytes 4866048 | tf_op jit(solution)/shard_map/reduce_scatter | solution.py:260
  896.6 27.3 %collective-permute-start.3 = (f32[2,128,1024]{2,1,0:T(8,128)S(1)}, f32[2,128,1024]{2,1,0:T(8,128)S(1)}, u32[]{:S(2)}, u32[]{:S(2)}) collective-permute-start(f32[2,128,1024]{2,1,0:T(8,128)S(1)} %get-tuple-element.160), channel_id=1, source_target_pairs={{1,0},{2,1},{3,2},{4,3},{5,4},{6,5},{7,6},{8,7},{9,8},{10,9},{11,1... | collective-permute-start | bytes 3145736 | tf_op jit(solution)/shard_map/ppermute | solution.py:36
  932.4 639.0 %reduce-scatter.20.cloned.1.call-start = ((), (), s32[]{:S(2)}) async-start(), calls=%async_computation.20 | async-start | bytes 7299072 | tf_op jit(solution)/shard_map/reduce_scatter | solution.py:267
  992.0 740.6 %reduce-scatter.28.cloned.1.call-start = ((), (), s32[]{:S(2)}) async-start(), calls=%async_computation.24 | async-start | bytes 12976128 | tf_op jit(solution)/shard_map/reduce_scatter | solution.py:277
  1007.9 977.3 %reduce-scatter.26.cloned.1.call-start = ((), (), s32[]{:S(2)}) async-start(), calls=%async_computation.23 | async-start | bytes 25952256 | tf_op jit(solution)/shard_map/reduce_scatter | solution.py:276
  (124 other events, 2030.3 us)
Sparse Core Ops, SparseCore 0:
  10.9 59.9 all-gather.10
  73.8 59.0 all-gather.14
  136.2 122.2 all-gather.12
  261.2 67.5 all-gather.16
  331.5 58.6 all-gather.18
  393.0 53.8 all-gather.20
  449.7 94.8 all-gather.22
  547.5 67.7 all-gather.24
  750.8 147.9 reduce-scatter.13
  904.6 102.4 reduce-scatter.29
  1013.3 113.3 reduce-scatter.23
  1133.2 96.1 reduce-scatter.17
  1236.1 98.0 reduce-scatter.21
  1340.2 105.9 reduce-scatter.15
  1453.2 118.2 reduce-scatter.19
  1577.9 154.7 reduce-scatter.27
  1740.6 244.5 reduce-scatter.25
where the time goes:
time: 2000 us; the launch traced here: 1990 us
  waiting for transfers between devices  1030 us (52%)
  matrix products  433 us (22%)
  blocking collectives  315 us (16%)
  local copies, waits for them, and re-layouts  128 us (6%)
  other arithmetic  54.9 us (3%)
    dot_general x60, matrix products, product(): jnp.einsum(formula, left_side, right_side, precision=precise_mode, prefer...  433 us
    reduce_scatter x1, waiting for transfers between devices, on_device(): lax.psum_scatter(grad_weights_late[6], ('batch', 'seq'), scatter_dimensio...  253 us
    reduce_scatter x1, waiting for transfers between devices, on_device(): lax.psum_scatter(grad_weights_late[7], ('batch', 'seq'), scatter_dimensio...  161 us
    all_gather x1, blocking collectives, on_device(): lax.all_gather(light_out, ('batch', 'seq'), axis=0, tiled=True)  133 us
    reduce_scatter x1, waiting for transfers between devices, on_device(): lax.psum_scatter(grad_weights_late[2] + grad_heavy_early, ('batch', 'seq'...  125 us
    reduce_scatter x1, waiting for transfers between devices, on_device(): lax.psum_scatter(grad_weights_late[0] + grad_light_early, ('batch', 'seq'...  112 us
    reduce_scatter x1, waiting for transfers between devices, on_device(): lax.psum_scatter(grad_weights_late[3], ('batch', 'seq'), scatter_dimensio...  105 us
    reduce_scatter x1, waiting for transfers between devices, on_device(): lax.psum_scatter(grad_weights_late[1], ('batch', 'seq'), scatter_dimensio...  103 us
  transfers between devices with their start and end apart: 21, of which 11 were waited for; matrix products, arithmetic and copies ran while one was open for 23% of the time, Pallas kernels for 0%

commit v1 on v0

v1 whole, which is shorter than its diff:
```python
import jax
import jax.numpy as jnp
from jax import lax
from jax.sharding import PartitionSpec as P

HL = 8
HH = 12
DH = 64
FL = 1024
FH = 4096
W = 128
IL = 512
IH = 768
GROUP = 4

f32 = jnp.float32
bf16 = jnp.bfloat16
fine = lax.Precision.HIGH
eps = 1e-06
GELU_A = 0.7978845608
GELU_B = 0.044715


def bit_stages(axis):
    size, found, step = lax.axis_size(axis), [], 1
    while step < size:
        found.append((axis, step))
        step *= 2
    return found


def own_bit(stage):
    axis, step = stage
    return (lax.axis_index(axis) // step) % 2


def flip(value, axis, step):
    return lax.ppermute(value, axis, [(i, i ^ step) for i in range(lax.axis_size(axis))])


def swapped(order):
    order = list(order)
    order[0], order[1] = order[1], order[0]
    return order


def gather_blocks(value, order, canonical):
    shape, have = value.shape, []
    for stage in order:
        other = flip(value, *stage)
        mine = own_bit(stage) == 1
        at = sum(1 for s in have if canonical.index(s) < canonical.index(stage))
        low = jnp.where(mine, other, value)
        high = jnp.where(mine, value, other)
        value = jnp.stack([low, high], axis=at)
        have = sorted(have + [stage], key=canonical.index)
    return value.reshape((2 ** len(order),) + shape)


def scatter_blocks(value, order, canonical):
    have = [s for s in canonical if s in order]
    shape = value.shape[1:]
    value = value.reshape((2,) * len(have) + shape)
    for stage in order:
        at, mine = have.index(stage), own_bit(stage)
        sent = lax.dynamic_index_in_dim(value, 1 - mine, at, keepdims=False)
        kept = lax.dynamic_index_in_dim(value, mine, at, keepdims=False)
        value = kept + flip(sent, *stage)
        have.remove(stage)
    return value


def in_group_order(pieces):
    value = jnp.stack(pieces)
    value = value.reshape((2, 2) + value.shape[1:])
    place = lax.axis_index("seq") % GROUP
    value = jnp.where(place // 2 == 1, value[::-1], value)
    value = jnp.where(place % 2 == 1, value[:, ::-1], value)
    return value.reshape((GROUP,) + value.shape[2:])


def shifted(value, by):
    length = lax.axis_size("seq")
    pairs = [(i, i + by) for i in range(length) if 0 <= i + by < length]
    return lax.ppermute(value, "seq", pairs)


def product(formula, left_side, right_side):
    return jnp.einsum(
        formula,
        left_side.astype(f32),
        right_side.astype(f32),
        precision=fine,
        preferred_element_type=f32,
    )


def unit_rms(values):
    scale = lax.rsqrt(jnp.mean(values * values, axis=-1, keepdims=True) + eps)
    return values * scale, scale


def norm_back(unit, scale, scaled_grad):
    return scale * (scaled_grad - unit * jnp.mean(scaled_grad * unit, axis=-1, keepdims=True))


def gelu_both(values):
    squared = values * values
    bend = jnp.tanh(GELU_A * (values + GELU_B * squared * values))
    half = 0.5 * (1.0 + bend)
    slope = half + 0.5 * values * (1.0 - bend * bend) * GELU_A * (1.0 + 3.0 * GELU_B * squared)
    return values * half, slope


def local_slots(route_row, row_begin, span_rows, capacity):
    below = jnp.sum((route_row < row_begin).astype(jnp.int32))
    upper = jnp.sum((route_row < row_begin + span_rows).astype(jnp.int32))
    slot = below + jnp.arange(capacity, dtype=jnp.int32)
    index = jnp.arange(route_row.shape[0], dtype=jnp.int32)
    positions = jnp.sum(
        jnp.where(slot[:, None] == index[None, :], route_row[None, :], 0), axis=1
    )
    offsets = positions - row_begin
    matched = (offsets[:, None] == jnp.arange(span_rows, dtype=jnp.int32)[None, :]) & (
        slot < upper
    )[:, None]
    return positions, matched.astype(bf16)


def slot_table(route_row, span_rows, devices, capacity):
    home = route_row // span_rows
    before = jnp.sum((route_row[None, :] < (home * span_rows)[:, None]).astype(jnp.int32), axis=1)
    rank = jnp.arange(route_row.shape[0], dtype=jnp.int32) - before
    place = home * capacity + rank
    return (
        place[:, None] == jnp.arange(devices * capacity, dtype=jnp.int32)[None, :]
    ).astype(bf16)


def softmax(scores, allowed):
    scores = jnp.where(allowed, scores, -1e30)
    top = jnp.max(scores, axis=-1, keepdims=True)
    weights = jnp.exp(scores - top)
    return weights / jnp.sum(weights, axis=-1, keepdims=True)


def light_blocks(kv_ext, rows):
    seqs = kv_ext.shape[0]
    parts = kv_ext.reshape(seqs, rows // W + 2, W, 2, HL, DH)
    spans = jnp.stack([parts[:, b : b + 3] for b in range(rows // W)], axis=1)
    spans = spans.reshape(seqs, rows // W, 3 * W, 2, HL, DH)
    return spans[:, :, :, 0], spans[:, :, :, 1]


def on_device(
    tokens,
    cotangent,
    prefix_len,
    query_routes,
    key_routes,
    ffn_routes,
    light_qkv,
    light_out,
    heavy_qkv,
    heavy_out,
    light_ff_in,
    light_ff_out,
    heavy_ff_in,
    heavy_ff_out,
    gains,
    routers,
):
    seqs, rows, width = tokens.shape
    devices = lax.axis_size("seq")
    row_begin = lax.axis_index("seq") * rows
    full_len = rows * devices
    capacity = rows // 4
    place = lax.axis_index("seq") % GROUP
    units = FH // GROUP

    seq_bits = bit_stages("seq")
    batch_bits = bit_stages("batch")
    canonical = batch_bits[::-1] + seq_bits[::-1]
    down_a = batch_bits + seq_bits
    down_b = batch_bits + swapped(seq_bits)
    up_a = down_a[::-1]
    up_b = down_b[::-1]
    seq_canonical = seq_bits[::-1]
    seq_down = (seq_bits, swapped(seq_bits))
    group_bits = seq_bits[:2]
    far_bits = seq_bits[2:]

    def joined(*pieces):
        return jnp.concatenate(pieces, axis=1)

    def gather_weight(value, order):
        return gather_blocks(value, order, canonical).reshape(-1, value.shape[1])

    def scatter_weight(value, order):
        blocks = 2 ** len(canonical)
        return scatter_blocks(
            value.reshape(blocks, value.shape[0] // blocks, value.shape[1]), order, canonical
        )

    def group_gather(value):
        canon = group_bits[::-1]
        first = gather_blocks(value[0], canon, canon)
        second_ = gather_blocks(value[1], group_bits, canon)
        return jnp.stack([first, second_], axis=1)

    n_one, r_one = unit_rms(tokens)
    small = gather_weight(joined(gains, routers), up_a).astype(f32)
    gain_one, gain_two = small[:, 0], small[:, 1]
    router_q, router_k, router_f = small[:, 2], small[:, 3], small[:, 4]
    before = shifted(tokens[:, rows - W :], 1)
    after = shifted(tokens[:, :W], -1)

    def picker(route_row):
        return local_slots(route_row, row_begin, rows, capacity)

    query_at, query_pick = jax.vmap(picker)(query_routes)
    _, key_pick = jax.vmap(picker)(key_routes)
    _, ffn_pick = jax.vmap(picker)(ffn_routes)
    table = jax.vmap(lambda r: slot_table(r, rows, devices, capacity))(key_routes)

    picked = product("sct,std->scd", jnp.concatenate([query_pick, key_pick], axis=1), n_one)
    query_unit, key_unit_own = picked[:, :capacity], picked[:, capacity:]

    qkv_light = gather_weight(light_qkv, up_a)
    qkv_heavy = gather_weight(heavy_qkv, up_b)
    key_slots = jnp.stack(
        [
            gather_blocks(key_unit_own[s], seq_down[s % 2][::-1], seq_canonical).reshape(-1, width)
            for s in range(seqs)
        ]
    )
    outs = gather_weight(joined(light_out, heavy_out), up_a)
    out_light, out_heavy = outs[:, :IL], outs[:, IL:]
    ff_in = gather_weight(light_ff_in, up_b)
    ff_out = gather_weight(light_ff_out, up_a)

    def unit_slice(gate_up, down, who):
        return joined(
            lax.dynamic_slice_in_dim(gate_up, who * units, units, 1),
            lax.dynamic_slice_in_dim(gate_up, FH + who * units, units, 1),
            lax.dynamic_slice_in_dim(down, who * units, units, 1),
        )

    big = in_group_order(
        [unit_slice(heavy_ff_in, heavy_ff_out, place)]
        + [
            flip(unit_slice(heavy_ff_in, heavy_ff_out, place ^ j), "seq", j)
            for j in range(1, GROUP)
        ]
    )
    big = gather_blocks(big, (batch_bits + far_bits)[::-1], batch_bits[::-1] + far_bits[::-1])
    big = big.reshape(width, 3 * units)
    big_in, big_out = big[:, : 2 * units], big[:, 2 * units :]

    cot_rows = group_gather(product("sct,std->scd", ffn_pick, cotangent))
    cot_rows = cot_rows.reshape(-1, width)

    n_ext = unit_rms(jnp.concatenate([before, tokens, after], axis=1))[0]
    normed_ext = n_ext * gain_one
    normed = n_one * gain_one
    light_q = product("std,de->ste", normed, qkv_light[:, :IL])
    light_kv = product("std,de->ste", normed_ext, qkv_light[:, IL:])
    blocks = rows // W
    q_heads = light_q.reshape(seqs, blocks, W, HL, DH)
    k_heads, v_heads = light_blocks(light_kv, rows)
    query_pos = (row_begin + jnp.arange(rows, dtype=jnp.int32)).reshape(blocks, W)
    key_pos = (
        row_begin
        - W
        + W * jnp.arange(blocks, dtype=jnp.int32)[:, None]
        + jnp.arange(3 * W, dtype=jnp.int32)[None, :]
    )
    near = jnp.abs(query_pos[:, :, None] - key_pos[:, None, :]) < W
    inside = (key_pos >= 0) & (key_pos < full_len)
    causal = (key_pos[None, :, None, :] <= query_pos[None, :, :, None]) | (
        key_pos[None, :, None, :] < prefix_len[:, None, None, None]
    )
    allowed = causal & near[None] & inside[None, :, None, :]
    scale = DH**-0.5
    light_probs = softmax(
        product("sbthd,sbuhd->sbhtu", q_heads, k_heads) * scale, allowed[:, :, None]
    )
    attended = product("sbhtu,sbuhd->sbthd", light_probs, v_heads).reshape(seqs, rows, IL)
    light_branch = product("sti,di->std", attended, out_light)

    query_rows = query_unit * gain_one
    key_unit = product("skp,spd->skd", table, key_slots)
    key_rows = key_unit * gain_one
    query_score = jax.nn.sigmoid(jnp.sum(query_rows * router_q, axis=-1))
    key_score = jax.nn.sigmoid(jnp.sum(key_rows * router_k, axis=-1))
    heavy_q = product("scd,di->sci", query_rows, qkv_heavy[:, :IH])
    heavy_kv = product("skd,de->ske", key_rows, qkv_heavy[:, IH:])
    heavy_k, heavy_v_raw = heavy_kv[..., :IH], heavy_kv[..., IH:]
    heavy_v = heavy_v_raw * key_score[..., None]
    hq = heavy_q.reshape(seqs, capacity, HH, DH)
    hk = heavy_k.reshape(seqs, -1, HH, DH)
    hv = heavy_v.reshape(seqs, -1, HH, DH)
    heavy_allowed = (key_routes[:, None, :] <= query_at[:, :, None]) | (
        key_routes[:, None, :] < prefix_len[:, None, None]
    )
    heavy_probs = softmax(product("schd,skhd->shck", hq, hk) * scale, heavy_allowed[:, None])
    heavy_mixed = product("shck,skhd->schd", heavy_probs, hv).reshape(seqs, capacity, IH)
    heavy_plain = product("sci,di->scd", heavy_mixed, out_heavy)
    heavy_rows = heavy_plain * query_score[..., None]
    hidden = tokens + light_branch + product("sct,scd->std", query_pick, heavy_rows)

    n_two, r_two = unit_rms(hidden)
    second = n_two * gain_two
    ffn_rows = group_gather(product("sct,std->scd", ffn_pick, second)).reshape(-1, width)
    gate_up = product("std,de->ste", second, ff_in)
    gate, up = gate_up[..., :FL], gate_up[..., FL:]
    gate_act, gate_slope = gelu_both(gate)
    light_act = gate_act * up
    light_ff = product("stf,df->std", light_act, ff_out)
    d_act = product("std,df->stf", cotangent, ff_out)
    d_gate_up = jnp.concatenate([d_act * up * gate_slope, d_act * gate_act], axis=-1)
    d_second = product("ste,de->std", d_gate_up, ff_in)
    d_ff_in = scatter_weight(product("std,ste->de", second, d_gate_up), down_b)
    d_ff_out = scatter_weight(product("std,stf->df", cotangent, light_act), down_a)

    ffn_score = jax.nn.sigmoid(jnp.sum(ffn_rows * router_f, axis=-1, keepdims=True))
    big_gate_up = product("rd,de->re", ffn_rows, big_in)
    big_gate, big_up = big_gate_up[:, :units], big_gate_up[:, units:]
    big_act, big_slope = gelu_both(big_gate)
    big_mix = big_act * big_up
    big_rows = product("rf,df->rd", big_mix, big_out) * ffn_score
    cot_mix = product("rd,df->rf", cot_rows, big_out)
    d_score = jnp.sum(cot_mix * big_mix, axis=-1, keepdims=True)
    d_score_in = d_score * ffn_score * (1.0 - ffn_score)
    d_mix = cot_mix * ffn_score
    d_big = jnp.concatenate([d_mix * big_up * big_slope, d_mix * big_act], axis=-1)
    d_ffn_rows = product("re,de->rd", d_big, big_in) + d_score_in * router_f
    d_router_f = jnp.sum(d_score_in * ffn_rows, axis=0)

    def group_blocks(value):
        return value.reshape(GROUP, seqs, capacity, width)

    ffn_own = scatter_blocks(group_blocks(d_ffn_rows), group_bits, group_bits[::-1])
    out_own = scatter_blocks(group_blocks(big_rows), swapped(group_bits), group_bits[::-1])
    d_big_all = joined(
        product("rd,re->de", ffn_rows, d_big),
        product("rd,rf->df", cot_rows, big_mix * ffn_score),
    )
    far_order = batch_bits + far_bits
    d_big_all = scatter_blocks(
        d_big_all.reshape(
            2 ** len(far_order), GROUP, width // 2 ** len(far_order) // GROUP, 3 * units
        ),
        far_order,
        batch_bits[::-1] + far_bits[::-1],
    )
    mine = in_group_order(
        [lax.dynamic_index_in_dim(d_big_all, place, 0, keepdims=False)]
        + [
            flip(lax.dynamic_index_in_dim(d_big_all, place ^ j, 0, keepdims=False), "seq", j)
            for j in range(1, GROUP)
        ]
    )

    def spread(value):
        return jnp.swapaxes(value, 0, 1).reshape(value.shape[1], -1)

    d_heavy_ff_in = joined(spread(mine[..., :units]), spread(mine[..., units : 2 * units]))
    d_heavy_ff_out = spread(mine[..., 2 * units :])

    output = hidden + light_ff + product("sct,scd->std", ffn_pick, out_own)
    d_second = d_second + product("sct,scd->std", ffn_pick, ffn_own)
    d_gain_two = jnp.sum(d_second * n_two, axis=(0, 1))
    d_hidden = cotangent + norm_back(n_two, r_two, d_second * gain_two)

    d_heavy_rows = product("sct,std->scd", query_pick, d_hidden)
    d_query_score = jnp.sum(d_heavy_rows * heavy_plain, axis=-1)
    d_plain = d_heavy_rows * query_score[..., None]
    d_mixed = product("scd,di->sci", d_plain, out_heavy)
    d_attended = product("std,di->sti", d_hidden, out_light)
    d_outs = scatter_weight(
        joined(
            product("std,sti->di", d_hidden, attended),
            product("scd,sci->di", d_plain, heavy_mixed),
        ),
        down_a,
    )
    d_mixed_heads = d_mixed.reshape(seqs, capacity, HH, DH)
    row_dot = jnp.sum(d_mixed_heads * heavy_mixed.reshape(d_mixed_heads.shape), axis=-1)
    d_probs = product("schd,skhd->shck", d_mixed_heads, hv)
    d_scores = heavy_probs * (d_probs - jnp.swapaxes(row_dot, 1, 2)[..., None]) * scale
    d_hv = product("shck,schd->skhd", heavy_probs, d_mixed_heads).reshape(heavy_v.shape)
    d_hq = product("shck,skhd->schd", d_scores, hk).reshape(heavy_q.shape)
    d_hk = product("shck,schd->skhd", d_scores, hq).reshape(heavy_k.shape)
    d_key_score = jnp.sum(d_hv * heavy_v_raw, axis=-1)
    d_key_in = d_key_score * key_score * (1.0 - key_score)
    d_query_in = d_query_score * query_score * (1.0 - query_score)
    d_kv = jnp.concatenate([d_hk, d_hv * key_score[..., None]], axis=-1)
    d_key_rows = product("ske,de->skd", d_kv, qkv_heavy[:, IH:]) + d_key_in[..., None] * router_k
    d_query_rows = (
        product("sci,di->scd", d_hq, qkv_heavy[:, :IH]) + d_query_in[..., None] * router_q
    )
    d_router_k = jnp.sum(d_key_in[..., None] * key_rows, axis=(0, 1))
    d_router_q = jnp.sum(d_query_in[..., None] * query_rows, axis=(0, 1))
    d_key_slots = product("skp,skd->spd", table, d_key_rows)
    d_key_own = jnp.stack(
        [
            scatter_blocks(
                d_key_slots[s].reshape(devices, capacity, width), seq_down[s % 2], seq_canonical
            )
            for s in range(seqs)
        ]
    )
    d_heavy_q_w = product("scd,sci->di", query_rows, d_hq)
    d_heavy_kv_w = product("skd,ske->de", key_rows, d_kv)
    d_qkv_heavy = scatter_weight(joined(d_heavy_q_w, d_heavy_kv_w), down_b)

    d_att_heads = d_attended.reshape(seqs, blocks, W, HL, DH)
    light_dot = jnp.sum(d_att_heads * attended.reshape(d_att_heads.shape), axis=-1)
    dl_probs = product("sbthd,sbuhd->sbhtu", d_att_heads, v_heads)
    dl_scores = light_probs * (dl_probs - jnp.swapaxes(light_dot, 2, 3)[..., None]) * scale
    d_lv = product("sbhtu,sbthd->sbuhd", light_probs, d_att_heads)
    d_lq = product("sbhtu,sbuhd->sbthd", dl_scores, k_heads).reshape(seqs, rows, IL)
    d_lk = product("sbhtu,sbthd->sbuhd", dl_scores, q_heads)

    def overlapped(value):
        value = value.reshape(seqs, blocks, 3, W, IL)
        total = jnp.zeros((seqs, blocks + 2, W, IL), f32)
        for b in range(blocks):
            total = total.at[:, b : b + 3].add(value[:, b])
        return total.reshape(seqs, rows + 2 * W, IL)

    d_lkv = jnp.concatenate([overlapped(d_lk), overlapped(d_lv)], axis=-1)
    d_ext = product("ste,de->std", d_lkv, qkv_light[:, IL:])
    from_next = shifted(d_ext[:, :W], -1)
    from_prev = shifted(d_ext[:, W + rows :], 1)
    d_qkv_light = scatter_weight(
        joined(product("std,ste->de", normed, d_lq), product("std,ste->de", normed_ext, d_lkv)),
        down_a,
    )
    d_own = product("ste,de->std", d_lq, qkv_light[:, :IL]) + product(
        "sct,scd->std", query_pick, d_query_rows
    )
    d_gain_one = (
        jnp.sum(d_ext * n_ext, axis=(0, 1))
        + jnp.sum(d_own * n_one, axis=(0, 1))
        + jnp.sum(d_key_rows * key_unit, axis=(0, 1))
    )
    d_normed = d_own + d_ext[:, W : W + rows] + product("sct,scd->std", key_pick, d_key_own)
    d_normed = d_normed.at[:, :W].add(from_prev).at[:, rows - W :].add(from_next)
    grad_tokens = d_hidden + norm_back(n_one, r_one, d_normed * gain_one)

    vectors = jnp.stack([d_gain_one, d_gain_two, d_router_q, d_router_k, d_router_f])
    for stage in down_a:
        vectors = vectors + flip(vectors, *stage)
    per_device = width // (devices * lax.axis_size("batch"))
    start = (lax.axis_index("batch") * devices + lax.axis_index("seq")) * per_device
    vectors = lax.dynamic_slice_in_dim(vectors, start, per_device, 1).T

    return (
        output,
        grad_tokens,
        d_qkv_light,
        d_outs[:, :IL],
        d_qkv_heavy,
        d_outs[:, IL:],
        d_ff_in,
        d_ff_out,
        d_heavy_ff_in,
        d_heavy_ff_out,
        vectors[:, :2],
        vectors[:, 2:],
    )


def solution(mesh):
    rows = P("batch", "seq", None)
    routes = P("batch", None)
    weight = P(("batch", "seq"), None)
    return jax.shard_map(
        on_device,
        mesh=mesh,
        in_specs=(rows, rows, P("batch"), routes, routes, routes) + (weight,) * 10,
        out_specs=(rows, rows) + (weight,) * 10,
        check_vma=False,
    )
```

time: 2000 us -> 1130 us (0.56)
  waiting for transfers between devices: 1030 us -> 421 us
  blocking collectives: 315 us -> 0 us
  matrix products: 433 us -> 208 us
  starting transfers between devices: 12 us -> 146 us
  local copies, waits for them, and re-layouts: 128 us -> 227 us
  other arithmetic: 54.9 us -> 116 us
    reduce_scatter x8 -> x0, waiting for transfers between devices: 863 us -> none  [the longest x1 253 us: on_device(): lax.psum_scatter(grad_weights_late[6], ('batch', 'seq'), scatter_dimensio...]
    ppermute x4 -> x104, waiting for transfers between devices: 28.3 us -> 421 us  [the longest x100 421 us: flip(): lax.ppermute(value, axis, [(i, i ^ step) for i in range(lax.axis_size(axi...]
    all_gather x3 -> x0, blocking collectives: 266 us -> none  [the longest x1 133 us: on_device(): lax.all_gather(light_out, ('batch', 'seq'), axis=0, tiled=True)]
    dot_general x60 -> x53, matrix products: 433 us -> 208 us  [product(): jnp.einsum(formula, left_side.astype(f32), right_side.astype(f32), precis...]
    all_gather x8 -> x0, waiting for transfers between devices: 138 us -> none  [the longest x1 77.7 us: on_device(): lax.all_gather(heavy_ff_in, ('batch', 'seq'), axis=0, tiled=True)]
    ppermute x4 -> x104, starting transfers between devices: 11.4 us -> 146 us  [the longest x100 136 us: flip(): lax.ppermute(value, axis, [(i, i ^ step) for i in range(lax.axis_size(axi...]
    scatter-add x0 -> x6, local copies, waits for them, and re-layouts: none -> 66.1 us  [overlapped(): total = total.at[:, b:b + 3].add(value[:, b])]
    unnamed x1 -> x0, blocking collectives: 48.9 us -> none
  transfers between devices with their start and end apart: 21 -> 104, of which waited for: 11 -> 51; matrix products, arithmetic and copies ran while one was open for 23% -> 46% of each run, Pallas kernels for 0% -> 0%
where the time goes in v1:
time: 1130 us; the launch traced here: 1120 us
  waiting for transfers between devices  421 us (37%)
  local copies, waits for them, and re-layouts  227 us (20%)
  matrix products  208 us (18%)
  starting transfers between devices  146 us (13%)
  other arithmetic  116 us (10%)
    ppermute x100, waiting for transfers between devices, flip(): lax.ppermute(value, axis, [(i, i ^ step) for i in range(lax.axis_size(axi...  421 us
    dot_general x53, matrix products, product(): jnp.einsum(formula, left_side.astype(f32), right_side.astype(f32), precis...  208 us
    ppermute x100, starting transfers between devices, flip(): lax.ppermute(value, axis, [(i, i ^ step) for i in range(lax.axis_size(axi...  136 us
    scatter-add x6, local copies, waits for them, and re-layouts, overlapped(): total = total.at[:, b:b + 3].add(value[:, b])  66.1 us
    unnamed x341, local copies, waits for them, and re-layouts  34 us
    another operation x94, other arithmetic, gather_blocks(): value = jnp.stack([low, high], axis=at)  33.3 us
    add x36, other arithmetic, scatter_blocks(): value = kept + flip(sent, *stage)  25.6 us
  transfers between devices with their start and end apart: 104, of which 51 were waited for; matrix products, arithmetic and copies ran while one was open for 46% of the time, Pallas kernels for 0%

profile of v1, /device:TPU:0, one launch (start us, length us, event | category | flops | bytes accessed | tf_op | source)
XLA Modules:
  0.0 1121.7 jit_solution(8280613538633201267)
XLA Ops:
  81.1 15.1 %collective-permute-done.36 = bf16[2,24,1024]{2,1,0:T(8,128)(2,1)S(1)} collective-permute-done((bf16[2,24,1024]{2,1,0:T(8,128)(2,1)S(1)}, bf16[2,24,1024]{2,1,0:T(8,128)(2,1)S(1)}, u32[]{:S(2)}, u32[]{:S(2)}) %collective-permute-start.36) | collective-permute-done | bytes 98336 | tf_op jit(solution)/shard_map/ppermute | solution.py:38
  134.8 9.8 collective-permute-done.53
  154.6 13.6 %collective-permute-done.38 = bf16[2,2,2,24,1024]{4,3,0,1,2:T(8,128)(2,1)S(1)} collective-permute-done((bf16[2,2,2,24,1024]{4,3,0,1,2:T(8,128)(2,1)S(1)}, bf16[2,2,2,24,1024]{4,3,0,1,2:T(8,128)(2,1)S(1)}, u32[]{:S(2)}, u32[]{:S(2)}) %collective-permute-start.38) | collective-permute-done | bytes 393248 | tf_op jit(solution)/shard_map/ppermute | solution.py:38
  182.5 10.2 collective-permute-done.17
  198.8 39.5 %collective-permute-done.18 = f32[2,64,768]{2,1,0:T(8,128)S(1)} collective-permute-done((f32[2,64,768]{2,1,0:T(8,128)S(1)}, f32[2,64,768]{2,1,0:T(8,128)S(1)}, u32[]{:S(2)}, u32[]{:S(2)}) %collective-permute-start.18) | collective-permute-done | bytes 393248 | tf_op jit(solution)/shard_map/ppermute | solution.py:38
  242.8 17.1 %collective-permute-done.28 = bf16[2,2,2,24,2304]{4,3,0,1,2:T(8,128)(2,1)S(1)} collective-permute-done((bf16[2,2,2,24,2304]{4,3,0,1,2:T(8,128)(2,1)S(1)}, bf16[2,2,2,24,2304]{4,3,0,1,2:T(8,128)(2,1)S(1)}, u32[]{:S(2)}, u32[]{:S(2)}) %collective-permute-start.28) | collective-permute-done | bytes 884768 | tf_op jit(solution)/shard_map/ppermute | solution.py:38
  267.3 11.1 collective-permute-done.19
  302.3 9.0 fusion.181
  471.3 10.0 fusion.13
  601.4 28.3 %scatter-add.25 = f32[2,4,128,512]{2,1,3,0:T(4,128)} dynamic-update-slice(f32[2,4,128,512]{2,1,3,0:T(4,128)} %scatter-add.24, f32[2,3,128,512]{2,1,3,0:T(4,128)} %fusion.39, s32[]{:T(128)} %constant.894.clone.1, s32[]{:T(128)} %constant.895.clone.1, s32[]{:T(128)} %constant.894.clone.1, s32[]{:T(128)} %constant.894.clone.1) | dynamic-update-slice | bytes 3145732 | tf_op jit(solution)/shard_map/scatter-add | solution.py:430
  632.6 28.3 %scatter-add.21 = f32[2,4,128,512]{2,1,3,0:T(4,128)} dynamic-update-slice(f32[2,4,128,512]{2,1,3,0:T(4,128)} %scatter-add.20, f32[2,3,128,512]{2,1,3,0:T(4,128)} %fusion.40, s32[]{:T(128)} %constant.894.clone.1, s32[]{:T(128)} %constant.895.clone.1, s32[]{:T(128)} %constant.894.clone.1, s32[]{:T(128)} %constant.894.clone.1) | dynamic-update-slice | bytes 3145732 | tf_op jit(solution)/shard_map/scatter-add | solution.py:430
  664.1 8.9 multiply_reduce_fusion.2
  692.2 10.8 fusion.10
  778.7 15.5 %collective-permute-done.62 = f32[2,2,2,64,768]{4,3,1,0,2:T(8,128)S(1)} collective-permute-done((f32[2,2,2,64,768]{4,3,1,0,2:T(8,128)S(1)}, f32[2,2,2,64,768]{4,3,1,0,2:T(8,128)S(1)}, u32[]{:S(2)}, u32[]{:S(2)}) %collective-permute-start.62) | collective-permute-done | bytes 1572896 | tf_op jit(solution)/shard_map/ppermute | solution.py:38
  795.7 27.3 %collective-permute-done.58 = f32[2,2,2,64,768]{4,3,1,0,2:T(8,128)S(1)} collective-permute-done((f32[2,2,2,64,768]{4,3,1,0,2:T(8,128)S(1)}, f32[2,2,2,64,768]{4,3,1,0,2:T(8,128)S(1)}, u32[]{:S(2)}, u32[]{:S(2)}) %collective-permute-start.58) | collective-permute-done | bytes 1572896 | tf_op jit(solution)/shard_map/ppermute | solution.py:38
  830.1 13.9 %collective-permute-done.63 = f32[2,2,64,768]{3,2,1,0:T(8,128)S(1)} collective-permute-done((f32[2,2,64,768]{3,2,1,0:T(8,128)S(1)}, f32[2,2,64,768]{3,2,1,0:T(8,128)S(1)}, u32[]{:S(2)}, u32[]{:S(2)}) %collective-permute-start.63) | collective-permute-done | bytes 786464 | tf_op jit(solution)/shard_map/ppermute | solution.py:38
  867.4 9.7 collective-permute-done.65
  877.2 8.5 collective-permute-done.61
  885.7 11.6 %collective-permute-start.84 = (f32[2,2,2,24,2048]{4,3,2,1,0:T(8,128)}, f32[2,2,2,24,2048]{4,3,2,1,0:T(8,128)}, u32[]{:S(2)}, u32[]{:S(2)}) collective-permute-start(f32[2,2,2,24,2048]{4,3,2,1,0:T(8,128)} %dynamic-slice_bitcast_fusion.4), channel_id=1, source_target_pairs={{0,2},{1,3},{2,0},{3,1},{4,6},{5,7},{6,4},{7,5},{8,10},{9,11},{10,... | collective-permute-start | bytes 4718600 | tf_op jit(solution)/shard_map/ppermute | solution.py:38
  900.6 32.3 %collective-permute-done.84 = f32[2,2,2,24,2048]{4,3,2,1,0:T(8,128)} collective-permute-done((f32[2,2,2,24,2048]{4,3,2,1,0:T(8,128)}, f32[2,2,2,24,2048]{4,3,2,1,0:T(8,128)}, u32[]{:S(2)}, u32[]{:S(2)}) %collective-permute-start.84) | collective-permute-done | bytes 1572896 | tf_op jit(solution)/shard_map/ppermute | solution.py:38
  940.5 9.0 collective-permute-start.102
  974.6 48.8 %collective-permute-done.77 = f32[24,1280]{1,0:T(8,128)S(1)} collective-permute-done((f32[24,1280]{1,0:T(8,128)S(1)}, f32[24,1280]{1,0:T(8,128)S(1)}, u32[]{:S(2)}, u32[]{:S(2)}) %collective-permute-start.77) | collective-permute-done | bytes 122912 | tf_op jit(solution)/shard_map/ppermute | solution.py:38
  1044.9 19.4 %collective-permute-start.80 = (f32[2,2,24,2304]{3,2,1,0:T(8,128)S(1)}, f32[2,2,24,2304]{3,2,1,0:T(8,128)S(1)}, u32[]{:S(2)}, u32[]{:S(2)}) collective-permute-start(f32[2,2,24,2304]{3,2,1,0:T(8,128)S(1)} %dynamic-slice_bitcast_fusion.8), channel_id=1, source_target_pairs={{0,1},{1,0},{2,3},{3,2},{4,5},{5,4},{6,7},{7,6},{8,9},{9,8},{10,11... | collective-permute-start | bytes 2654216 | tf_op jit(solution)/shard_map/ppermute | solution.py:38
  1076.2 29.9 %collective-permute-done.81 = f32[2,24,2304]{2,1,0:T(8,128)S(1)} collective-permute-done((f32[2,24,2304]{2,1,0:T(8,128)S(1)}, f32[2,24,2304]{2,1,0:T(8,128)S(1)}, u32[]{:S(2)}, u32[]{:S(2)}) %collective-permute-start.81) | collective-permute-done | bytes 442400 | tf_op jit(solution)/shard_map/ppermute | solution.py:38
  (905 shorter events, 679.9 us)
Async XLA Ops:
  72.3 103.3 %collective-permute-start.1 = (f32[2,128,768]{2,1,0:T(8,128)S(1)}, f32[2,128,768]{2,1,0:T(8,128)S(1)}, u32[]{:S(2)}, u32[]{:S(2)}) collective-permute-start(f32[2,128,768]{2,1,0:T(8,128)S(1)} %get-tuple-element.156), channel_id=1, source_target_pairs={{1,0},{2,1},{3,2},{4,3},{5,4},{6,5},{7,6},{8,7},{9,8},{10,9},{11,1... | collective-permute-start | bytes 2359304 | tf_op jit(solution)/shard_map/ppermute | solution.py:85
  73.8 99.6 %collective-permute-start = (f32[2,128,768]{2,1,0:T(8,128)S(1)}, f32[2,128,768]{2,1,0:T(8,128)S(1)}, u32[]{:S(2)}, u32[]{:S(2)}) collective-permute-start(f32[2,128,768]{2,1,0:T(8,128)S(1)} %get-tuple-element.157), channel_id=1, source_target_pairs={{0,1},{1,2},{2,3},{3,4},{4,5},{5,6},{6,7},{7,8},{8,9},{9,10},{10,1... | collective-permute-start | bytes 2359304 | tf_op jit(solution)/shard_map/ppermute | solution.py:85
  170.7 68.0 %collective-permute-start.33 = (bf16[2,2,2,24,2048]{4,3,0,1,2:T(8,128)(2,1)S(1)}, bf16[2,2,2,24,2048]{4,3,0,1,2:T(8,128)(2,1)S(1)}, u32[]{:S(2)}, u32[]{:S(2)}) collective-permute-start(bf16[2,2,2,24,2048]{4,3,0,1,2:T(8,128)(2,1)S(1)} %pad_maximum_fusion.44), channel_id=1, source_target_pairs={{0,2},{1,3},{2,0},{3,1},{4,6},{5,7},{6,4},{7,5},{8,10},{9,11},{10,... | collective-permute-start | bytes 2359304 | tf_op jit(solution)/shard_map/ppermute | solution.py:38
  173.4 67.4 %collective-permute-start.39 = (bf16[2,2,2,2,24,1024]{5,4,0,1,2,3:T(8,128)(2,1)S(1)}, bf16[2,2,2,2,24,1024]{5,4,0,1,2,3:T(8,128)(2,1)S(1)}, u32[]{:S(2)}, u32[]{:S(2)}) collective-permute-start(bf16[2,2,2,2,24,1024]{5,4,0,1,2,3:T(8,128)(2,1)S(1)} %pad_maximum_fusion.45), channel_id=1, source_target_pairs={{0,16},{16,0},{1,17},{17,1},{2,18},{18,2},{3,19},{19,3},{4,20},{20... | collective-permute-start | bytes 2359304 | tf_op jit(solution)/shard_map/ppermute | solution.py:38
  192.7 69.6 %collective-permute-start.48 = (bf16[2,4,24,3072]{3,2,1,0:T(8,128)(2,1)S(1)}, bf16[2,4,24,3072]{3,2,1,0:T(8,128)(2,1)S(1)}, u32[]{:S(2)}, u32[]{:S(2)}) collective-permute-start(bf16[2,4,24,3072]{3,2,1,0:T(8,128)(2,1)S(1)} %pad_maximum_fusion.38), channel_id=1, source_target_pairs={{0,4},{1,5},{2,6},{3,7},{4,0},{5,1},{6,2},{7,3},{8,12},{9,13},{10,... | collective-permute-start | bytes 3538952 | tf_op jit(solution)/shard_map/ppermute | solution.py:38
  261.8 84.3 %collective-permute-start.34 = (bf16[2,2,2,2,24,2048]{5,4,0,1,3,2:T(8,128)(2,1)}, bf16[2,2,2,2,24,2048]{5,4,0,1,3,2:T(8,128)(2,1)}, u32[]{:S(2)}, u32[]{:S(2)}) collective-permute-start(bf16[2,2,2,2,24,2048]{5,4,0,1,3,2:T(8,128)(2,1)} %pad_maximum_fusion.31), channel_id=1, source_target_pairs={{0,16},{16,0},{1,17},{17,1},{2,18},{18,2},{3,19},{19,3},{4,20},{20... | collective-permute-start | bytes 4718600 | tf_op jit(solution)/shard_map/ppermute | solution.py:38
  262.4 88.2 %collective-permute-start.29 = (bf16[2,2,2,2,24,2304]{5,4,0,1,3,2:T(8,128)(2,1)}, bf16[2,2,2,2,24,2304]{5,4,0,1,3,2:T(8,128)(2,1)}, u32[]{:S(2)}, u32[]{:S(2)}) collective-permute-start(bf16[2,2,2,2,24,2304]{5,4,0,1,3,2:T(8,128)(2,1)} %pad_maximum_fusion.28), channel_id=1, source_target_pairs={{0,16},{16,0},{1,17},{17,1},{2,18},{18,2},{3,19},{19,3},{4,20},{20... | collective-permute-start | bytes 5308424 | tf_op jit(solution)/shard_map/ppermute | solution.py:38
  265.4 168.1 %collective-permute-start.49 = (bf16[2,2,4,24,3072]{4,3,2,1,0:T(8,128)(2,1)}, bf16[2,2,4,24,3072]{4,3,2,1,0:T(8,128)(2,1)}, u32[]{:S(2)}, u32[]{:S(2)}) collective-permute-start(bf16[2,2,4,24,3072]{4,3,2,1,0:T(8,128)(2,1)} %pad_maximum_fusion.24), channel_id=1, source_target_pairs={{0,16},{16,0},{1,17},{17,1},{2,18},{18,2},{3,19},{19,3},{4,20},{20... | collective-permute-start | bytes 7077896 | tf_op jit(solution)/shard_map/ppermute | solution.py:38
  278.4 77.2 %collective-permute-start.24 = (f32[2,2,2,64,768]{4,3,0,1,2:T(8,128)}, f32[2,2,2,64,768]{4,3,0,1,2:T(8,128)}, u32[]{:S(2)}, u32[]{:S(2)}) collective-permute-start(f32[2,2,2,64,768]{4,3,0,1,2:T(8,128)} %pad_maximum_fusion.30), channel_id=1, source_target_pairs={{0,2},{1,3},{2,0},{3,1},{4,6},{5,7},{6,4},{7,5},{8,10},{9,11},{10,... | collective-permute-start | bytes 4718600 | tf_op jit(solution)/shard_map/ppermute | solution.py:38
  281.3 76.5 %collective-permute-start.20 = (f32[2,2,2,64,768]{4,3,0,1,2:T(8,128)}, f32[2,2,2,64,768]{4,3,0,1,2:T(8,128)}, u32[]{:S(2)}, u32[]{:S(2)}) collective-permute-start(f32[2,2,2,64,768]{4,3,0,1,2:T(8,128)} %pad_maximum_fusion.29), channel_id=1, source_target_pairs={{0,1},{1,0},{2,3},{3,2},{4,5},{5,4},{6,7},{7,6},{8,9},{9,8},{10,11... | collective-permute-start | bytes 4718600 | tf_op jit(solution)/shard_map/ppermute | solution.py:38
  414.9 93.1 %collective-permute-start.88 = (f32[2,2,2,2,24,1024]{5,4,2,1,0,3:T(8,128)}, f32[2,2,2,2,24,1024]{5,4,2,1,0,3:T(8,128)}, u32[]{:S(2)}, u32[]{:S(2)}) collective-permute-start(f32[2,2,2,2,24,1024]{5,4,2,1,0,3:T(8,128)} %bitcast.642), channel_id=1, source_target_pairs={{0,16},{16,0},{1,17},{17,1},{2,18},{18,2},{3,19},{19,3},{4,20},{20... | collective-permute-start | bytes 4718600 | tf_op jit(solution)/shard_map/ppermute | solution.py:38
  432.4 342.4 %collective-permute-start.83 = (f32[2,2,2,2,24,2048]{5,4,3,1,0,2:T(8,128)}, f32[2,2,2,2,24,2048]{5,4,3,1,0,2:T(8,128)}, u32[]{:S(2)}, u32[]{:S(2)}) collective-permute-start(f32[2,2,2,2,24,2048]{5,4,3,1,0,2:T(8,128)} %bitcast.640), channel_id=1, source_target_pairs={{0,16},{16,0},{1,17},{17,1},{2,18},{18,2},{3,19},{19,3},{4,20},{20... | collective-permute-start | bytes 9437192 | tf_op jit(solution)/shard_map/ppermute | solution.py:38
  499.4 466.8 %collective-permute-start.93 = (f32[2,2,4,24,3072]{4,3,2,1,0:T(8,128)}, f32[2,2,4,24,3072]{4,3,2,1,0:T(8,128)}, u32[]{:S(2)}, u32[]{:S(2)}) collective-permute-start(f32[2,2,4,24,3072]{4,3,2,1,0:T(8,128)} %dynamic-slice_bitcast_fusion), channel_id=1, source_target_pairs={{0,16},{16,0},{1,17},{17,1},{2,18},{18,2},{3,19},{19,3},{4,20},{20... | collective-permute-start | bytes 14155784 | tf_op jit(solution)/shard_map/ppermute | solution.py:38
  501.4 253.7 %collective-permute-start.51 = (f32[2,64,768]{2,1,0:T(8,128)}, f32[2,64,768]{2,1,0:T(8,128)}, u32[]{:S(2)}, u32[]{:S(2)}) collective-permute-start(f32[2,64,768]{2,1,0:T(8,128)} %dynamic-slice_bitcast_fusion.23), channel_id=1, source_target_pairs={{0,1},{1,0},{2,3},{3,2},{4,5},{5,4},{6,7},{7,6},{8,9},{9,8},{10,11... | collective-permute-start | bytes 1179656 | tf_op jit(solution)/shard_map/ppermute | solution.py:38
  512.0 235.4 %collective-permute-start.89 = (f32[2,2,2,24,1024]{4,3,2,1,0:T(8,128)}, f32[2,2,2,24,1024]{4,3,2,1,0:T(8,128)}, u32[]{:S(2)}, u32[]{:S(2)}) collective-permute-start(f32[2,2,2,24,1024]{4,3,2,1,0:T(8,128)} %dynamic-slice_bitcast_fusion.9), channel_id=1, source_target_pairs={{0,1},{1,0},{2,3},{3,2},{4,5},{5,4},{6,7},{7,6},{8,9},{9,8},{10,11... | collective-permute-start | bytes 2359304 | tf_op jit(solution)/shard_map/ppermute | solution.py:38
  723.1 102.8 %collective-permute-start.73 = (f32[2,2,2,2,24,1280]{5,4,3,2,1,0:T(8,128)}, f32[2,2,2,2,24,1280]{5,4,3,2,1,0:T(8,128)}, u32[]{:S(2)}, u32[]{:S(2)}) collective-permute-start(f32[2,2,2,2,24,1280]{5,4,3,2,1,0:T(8,128)} %dynamic-slice_bitcast_fusion.2), channel_id=1, source_target_pairs={{0,16},{16,0},{1,17},{17,1},{2,18},{18,2},{3,19},{19,3},{4,20},{20... | collective-permute-start | bytes 5898248 | tf_op jit(solution)/shard_map/ppermute | solution.py:38
  794.2 104.2 %collective-permute-start.67 = (f32[2,128,768]{2,1,0:T(8,128)S(1)}, f32[2,128,768]{2,1,0:T(8,128)S(1)}, u32[]{:S(2)}, u32[]{:S(2)}) collective-permute-start(f32[2,128,768]{2,1,0:T(8,128)S(1)} %get-tuple-element.128), channel_id=1, source_target_pairs={{1,0},{2,1},{3,2},{4,3},{5,4},{6,5},{7,6},{8,7},{9,8},{10,9},{11,1... | collective-permute-start | bytes 2359304 | tf_op jit(solution)/shard_map/ppermute | solution.py:85
  857.9 105.2 %collective-permute-start.78 = (f32[2,2,2,2,24,2304]{5,4,3,1,0,2:T(8,128)}, f32[2,2,2,2,24,2304]{5,4,3,1,0,2:T(8,128)}, u32[]{:S(2)}, u32[]{:S(2)}) collective-permute-start(f32[2,2,2,2,24,2304]{5,4,3,1,0,2:T(8,128)} %bitcast.639), channel_id=1, source_target_pairs={{0,16},{16,0},{1,17},{17,1},{2,18},{18,2},{3,19},{19,3},{4,20},{20... | collective-permute-start | bytes 10616840 | tf_op jit(solution)/shard_map/ppermute | solution.py:38
  898.1 61.5 %collective-permute-start.69 = (f32[2,2,2,24,1536]{4,3,2,1,0:T(8,128)}, f32[2,2,2,24,1536]{4,3,2,1,0:T(8,128)}, u32[]{:S(2)}, u32[]{:S(2)}) collective-permute-start(f32[2,2,2,24,1536]{4,3,2,1,0:T(8,128)} %dynamic-slice_bitcast_fusion.6), channel_id=1, source_target_pairs={{0,1},{1,0},{2,3},{3,2},{4,5},{5,4},{6,7},{7,6},{8,9},{9,8},{10,11... | collective-permute-start | bytes 3538952 | tf_op jit(solution)/shard_map/ppermute | solution.py:38
  900.5 56.8 %collective-permute-start.75 = (f32[2,2,24,1280]{3,2,1,0:T(8,128)S(1)}, f32[2,2,24,1280]{3,2,1,0:T(8,128)S(1)}, u32[]{:S(2)}, u32[]{:S(2)}) collective-permute-start(f32[2,2,24,1280]{3,2,1,0:T(8,128)S(1)} %dynamic-slice_bitcast_fusion.16), channel_id=1, source_target_pairs={{0,2},{1,3},{2,0},{3,1},{4,6},{5,7},{6,4},{7,5},{8,10},{9,11},{10,... | collective-permute-start | bytes 1474568 | tf_op jit(solution)/shard_map/ppermute | solution.py:38
  961.3 72.7 %collective-permute-start.70 = (f32[2,2,24,1536]{3,2,1,0:T(8,128)S(1)}, f32[2,2,24,1536]{3,2,1,0:T(8,128)S(1)}, u32[]{:S(2)}, u32[]{:S(2)}) collective-permute-start(f32[2,2,24,1536]{3,2,1,0:T(8,128)S(1)} %dynamic-slice_bitcast_fusion.15), channel_id=1, source_target_pairs={{0,2},{1,3},{2,0},{3,1},{4,6},{5,7},{6,4},{7,5},{8,10},{9,11},{10,... | collective-permute-start | bytes 1769480 | tf_op jit(solution)/shard_map/ppermute | solution.py:38
  965.8 78.8 %collective-permute-start.79 = (f32[2,2,2,24,2304]{4,3,2,1,0:T(8,128)S(1)}, f32[2,2,2,24,2304]{4,3,2,1,0:T(8,128)S(1)}, u32[]{:S(2)}, u32[]{:S(2)}) collective-permute-start(f32[2,2,2,24,2304]{4,3,2,1,0:T(8,128)S(1)} %dynamic-slice_bitcast_fusion.3), channel_id=1, source_target_pairs={{0,2},{1,3},{2,0},{3,1},{4,6},{5,7},{6,4},{7,5},{8,10},{9,11},{10,... | collective-permute-start | bytes 5308424 | tf_op jit(solution)/shard_map/ppermute | solution.py:38
  969.5 94.7 %collective-permute-start.94 = (f32[2,4,24,3072]{3,2,1,0:T(8,128)S(1)}, f32[2,4,24,3072]{3,2,1,0:T(8,128)S(1)}, u32[]{:S(2)}, u32[]{:S(2)}) collective-permute-start(f32[2,4,24,3072]{3,2,1,0:T(8,128)S(1)} %dynamic-slice_bitcast_fusion.1), channel_id=1, source_target_pairs={{0,4},{1,5},{2,6},{3,7},{4,0},{5,1},{6,2},{7,3},{8,12},{9,13},{10,... | collective-permute-start | bytes 7077896 | tf_op jit(solution)/shard_map/ppermute | solution.py:38
  972.8 57.5 %collective-permute-start.86 = (f32[2,24,2048]{2,1,0:T(8,128)S(1)}, f32[2,24,2048]{2,1,0:T(8,128)S(1)}, u32[]{:S(2)}, u32[]{:S(2)}) collective-permute-start(f32[2,24,2048]{2,1,0:T(8,128)S(1)} %dynamic-slice_bitcast_fusion.19), channel_id=1, source_target_pairs={{0,4},{1,5},{2,6},{3,7},{4,0},{5,1},{6,2},{7,3},{8,12},{9,13},{10,... | collective-permute-start | bytes 1179656 | tf_op jit(solution)/shard_map/ppermute | solution.py:38
  (246 other events, 3406.0 us)

commit v2 on v1

v2 whole, which is shorter than its diff:
```python
import itertools

import jax
import jax.numpy as jnp
from jax import lax
from jax.experimental import pallas as pl
from jax.experimental.pallas import tpu as pltpu
from jax.sharding import PartitionSpec as P

HL = 8
HH = 12
DH = 64
FL = 1024
FH = 4096
W = 128
IL = 512
IH = 768
GROUP = 4

f32 = jnp.float32
bf16 = jnp.bfloat16
fine = lax.Precision.HIGH
eps = 1e-06
GELU_A = 0.7978845608
GELU_B = 0.044715


def bit_stages(axis):
    size, found, step = lax.axis_size(axis), [], 1
    while step < size:
        found.append((axis, step))
        step *= 2
    return found


def own_bit(stage):
    axis, step = stage
    return (lax.axis_index(axis) // step) % 2


def after(values, others):
    values, others = list(values), list(others)
    return list(lax.optimization_barrier(tuple(values) + tuple(others)))[: len(values)]


class Links:
    def __init__(self):
        self.recent = {}

    def queue(self, kind, values):
        recent = self.recent.setdefault(kind, [])
        return after(values, recent[-1]) if recent else values

    def near(self, value):
        groups = [
            list(range(i, i + GROUP)) for i in range(0, lax.axis_size("seq"), GROUP)
        ]
        (value,) = self.queue("near", [value])
        got = lax.all_to_all(value, "seq", 0, 0, axis_index_groups=groups, tiled=True)
        self.recent["near"].append([got])
        return got

    def near_share(self, value):
        return self.near(jnp.broadcast_to(value[None], (GROUP,) + value.shape))

    def far(self, values):
        devices = lax.axis_size("seq")
        sent = self.queue("far", values[1:])
        got = [
            lax.ppermute(v, "seq", [(i, i ^ (GROUP * j)) for i in range(devices)])
            for j, v in enumerate(sent, 1)
        ]
        self.recent["far"].append(got)
        return [values[0]] + got

    def far_share(self, value):
        return self.far([value] * (lax.axis_size("seq") // GROUP))

    def flip(self, values, stage):
        axis, step = stage
        pairs = [(i, i ^ step) for i in range(lax.axis_size(axis))]
        return [lax.ppermute(v, axis, pairs) for v in values]


def far_place():
    return lax.axis_index("seq") // GROUP


def stack_kernel(place, *refs):
    sources, out = refs[:-1], refs[-1]
    for j, source in enumerate(sources):

        @pl.when(pl.program_id(0) == j)
        def _(source=source):
            out[...] = source[...]


def stacked(values, place):
    shape = values[0].shape
    zeros = (0,) * len(shape)
    return pl.pallas_call(
        stack_kernel,
        name="stack",
        grid_spec=pltpu.PrefetchScalarGridSpec(
            num_scalar_prefetch=1,
            grid=(len(values),),
            in_specs=[pl.BlockSpec(shape, lambda j, _: zeros)] * len(values),
            out_specs=pl.BlockSpec((None,) + shape, lambda j, me: (me[0] ^ j,) + zeros),
        ),
        out_shape=jax.ShapeDtypeStruct((len(values),) + shape, values[0].dtype),
        compiler_params=pltpu.CompilerParams(vmem_limit_bytes=40 * 2**20),
        cost_estimate=pl.CostEstimate(
            flops=0, bytes_accessed=4 * values[0].size * len(values), transcendentals=0
        ),
    )(jnp.stack([place]).astype(jnp.int32), *values)


def join_kernel(bit, value, other, out):
    mine = pl.program_id(1) == bit[0]

    @pl.when(mine)
    def _():
        out[...] = value[...]

    @pl.when(jnp.logical_not(mine))
    def _():
        out[...] = other[...]


def joined_halves(value, other, bit, turned):
    steps, inner, rows, width = value.shape
    source = pl.BlockSpec((None, inner, rows, width), lambda i, j, _: (i, 0, 0, 0))
    if turned:
        shape = (2, inner, steps, rows, width)
        target = pl.BlockSpec(
            (None, inner, None, rows, width), lambda i, j, _: (j, 0, i, 0, 0)
        )
    else:
        shape = (2, steps, inner, rows, width)
        target = pl.BlockSpec(
            (None, None, inner, rows, width), lambda i, j, _: (j, i, 0, 0, 0)
        )
    return pl.pallas_call(
        join_kernel,
        name="join",
        grid_spec=pltpu.PrefetchScalarGridSpec(
            num_scalar_prefetch=1,
            grid=(steps, 2),
            in_specs=[source, source],
            out_specs=target,
        ),
        out_shape=jax.ShapeDtypeStruct(shape, value.dtype),
        compiler_params=pltpu.CompilerParams(vmem_limit_bytes=40 * 2**20),
        cost_estimate=pl.CostEstimate(
            flops=0, bytes_accessed=8 * value.size, transcendentals=0
        ),
    )(jnp.stack([bit]).astype(jnp.int32), value, other)


def power_of(block):
    top = jnp.max(jnp.abs(block), axis=-2, keepdims=True)
    return jnp.ceil(jnp.log2(jnp.maximum(top, 1e-30)) + 0.01)


def steps_of(block, power):
    return jnp.floor(block * jnp.exp2(15.0 - power) + 0.5)


def pack_rows(value):
    power = power_of(value)
    extra = jnp.broadcast_to(power, power.shape[:-2] + (8, power.shape[-1]))
    return jnp.concatenate([steps_of(value, power), extra], axis=-2).astype(jnp.int16)


def unpack_rows(packed):
    packed = packed.astype(f32)
    rows = packed.shape[-2] - 8
    return packed[..., :rows, :] * jnp.exp2(packed[..., rows : rows + 1, :] - 15.0)


def power_rows(blocks):
    return -(-blocks // 16) * 16


def packed_blocks(blocks):
    powers = [power_of(block) for block in blocks]
    steps = [steps_of(block, power) for block, power in zip(blocks, powers)]
    powers += [jnp.zeros_like(powers[0])] * (power_rows(len(powers)) - len(powers))
    return jnp.concatenate(steps + powers, axis=0).astype(jnp.int32).astype(jnp.int16)


def block_sum(sources, count, depth):
    totals = [None] * count
    for source in sources:
        steps = source.astype(jnp.int32).astype(f32)
        powers = jnp.exp2(steps[count * depth : count * depth + count] - 15.0)
        for n in range(count):
            block = steps[n * depth : (n + 1) * depth] * powers[n : n + 1]
            totals[n] = block if totals[n] is None else totals[n] + block
    return totals


def give(blocks, layout, place, outs, total):
    if total is None:
        for p, wanted in enumerate(layout):
            outs[0][p] = packed_blocks([blocks[n][low:high] for n, low, high in wanted])
        return
    for p, wanted in enumerate(layout):
        row = 0
        for n, low, high in wanted:
            total[p, row : row + high - low] = blocks[n][low:high]
            row += high - low
    sizes = [high - low for _, low, high in layout[0]]
    for j, out in enumerate(outs):
        rows = total[place ^ j]
        cuts = [sum(sizes[:n]) for n in range(len(sizes) + 1)]
        out[...] = packed_blocks([rows[p:q] for p, q in zip(cuts, cuts[1:])])


def given_form(layout, far, width, tile):
    inner = sum(high - low for _, low, high in layout[0])
    rows = inner + power_rows(len(layout[0]))
    if far:
        return (
            [jax.ShapeDtypeStruct((rows, width), jnp.int16)] * len(layout),
            [pl.BlockSpec((rows, tile), lambda c, _: (0, c))] * len(layout),
            [pltpu.VMEM((len(layout), inner, tile), f32)],
        )
    return (
        [jax.ShapeDtypeStruct((len(layout), rows, width), jnp.int16)],
        [pl.BlockSpec((len(layout), rows, tile), lambda c, _: (0, 0, c))],
        [],
    )


def send_kernel(spans, layout, received, far, place, *refs):
    count = len(spans)
    values, refs = refs[:count], refs[count:]
    others = [None] * count
    if received:
        others, refs = refs[:count], refs[count:]
    outs, total = (refs[:-1], refs[-1]) if far else (refs, None)

    def one(value, other):
        blocks = [value[n] for n in range(value.shape[0])]
        if other is not None:
            got = block_sum([other[...]], len(blocks), blocks[0].shape[0])
            blocks = [p + q for p, q in zip(blocks, got)]
        give(blocks, layout, place[0], outs, total)

    for i, (low, high) in enumerate(spans):
        one_piece = lambda i=i: one(values[i], others[i])
        if count == 1:
            one_piece()
        else:
            pl.when((pl.program_id(0) >= low) & (pl.program_id(0) < high))(one_piece)


def send_form(values, others, layout, far):
    widths = [v.shape[2] for v in values]
    tile = max(t for t in (128, 256, 384, 512) if all(w % t == 0 for w in widths))
    spans, begin = [], 0
    for w in widths:
        spans.append((begin, begin + w // tile))
        begin += w // tile
    received = others[0] is not None

    def spec(shape, span):
        lead = (0,) * (len(shape) - 1)
        return pl.BlockSpec(
            shape[:-1] + (tile,),
            lambda c, _: lead + (jnp.clip(c - span[0], 0, span[1] - span[0] - 1),),
        )

    args = list(values) + (list(others) if received else [])
    shapes, out_specs, scratch = given_form(layout, far, sum(widths), tile)
    got = pl.pallas_call(
        lambda *refs: send_kernel(spans, layout, received, far, *refs),
        name="send",
        grid_spec=pltpu.PrefetchScalarGridSpec(
            num_scalar_prefetch=1,
            grid=(begin,),
            in_specs=[spec(v.shape, s) for v, s in zip(args, spans * 2)],
            out_specs=out_specs,
            scratch_shapes=scratch,
        ),
        out_shape=shapes,
        compiler_params=pltpu.CompilerParams(vmem_limit_bytes=48 * 2**20),
        cost_estimate=pl.CostEstimate(
            flops=20 * sum(v.size for v in values),
            bytes_accessed=8 * sum(v.size for v in values),
            transcendentals=0,
        ),
    )(jnp.stack([far_place()]).astype(jnp.int32), *args)
    return got if far else got[0]


def arrived_kernel(sources, count, depth, layout, far, place, *refs):
    if sources is None:
        packed, refs = [refs[0][n] for n in range(refs[0].shape[0])], refs[1:]
    else:
        packed, refs = [r[...] for r in refs[:sources]], refs[sources:]
    blocks = block_sum(packed, count, depth)
    if layout is None:
        for n, block in enumerate(blocks):
            refs[0][n * depth : (n + 1) * depth] = block
        return
    outs, total = (refs[:-1], refs[-1]) if far else (refs, None)
    give(blocks, layout, place[0], outs, total)


def arrived(packed, count, depth, layout=None, far=False):
    args = list(packed) if isinstance(packed, (list, tuple)) else [packed]
    sources = len(args) if isinstance(packed, (list, tuple)) else None
    width = args[0].shape[-1]
    tile = max(t for t in (128, 256, 384, 512) if width % t == 0)
    if layout is None:
        shapes = [jax.ShapeDtypeStruct((count * depth, width), f32)]
        out_specs, scratch = [pl.BlockSpec((count * depth, tile), lambda c, _: (0, c))], []
    else:
        shapes, out_specs, scratch = given_form(layout, far, width, tile)
    lead = (0,) * (args[0].ndim - 1)
    got = pl.pallas_call(
        lambda *refs: arrived_kernel(sources, count, depth, layout, far, *refs),
        name="arrived",
        grid_spec=pltpu.PrefetchScalarGridSpec(
            num_scalar_prefetch=1,
            grid=(width // tile,),
            in_specs=[
                pl.BlockSpec(a.shape[:-1] + (tile,), lambda c, _: lead + (c,)) for a in args
            ],
            out_specs=out_specs,
            scratch_shapes=scratch,
        ),
        out_shape=shapes,
        compiler_params=pltpu.CompilerParams(vmem_limit_bytes=48 * 2**20),
        cost_estimate=pl.CostEstimate(
            flops=10 * sum(a.size for a in args),
            bytes_accessed=4 * sum(a.size for a in args),
            transcendentals=0,
        ),
    )(jnp.stack([far_place()]).astype(jnp.int32), *args)
    return got if far else got[0]


def grad_kernel(depth, bits, x, y, kept, sent, x_high, x_low):
    @pl.when(pl.program_id(0) == 0)
    def _():
        x_high[...], x_low[...] = split(x[...].T)

    y_high, y_low = split(y[...])
    half = x_high.shape[0] // 2

    def part(which):
        rows = pl.ds(pl.multiple_of(which * half, half), half)
        high = x_high[rows, :]
        return dot_nn(high, y_high) + dot_nn(x_low[rows, :], y_high) + dot_nn(high, y_low)

    kept[...] = part(bits[0])
    other = part(1 - bits[0])
    sent[...] = packed_blocks([other[n : n + depth] for n in range(0, half, depth)])


def grad_split(x, y, bit, depth):
    rows, width = x.shape
    half, columns = width // 2, y.shape[1]
    tile = max(t for t in (128, 256, 512) if columns % t == 0)
    packed = half + power_rows(half // depth)
    return pl.pallas_call(
        lambda *refs: grad_kernel(depth, *refs),
        name="grad",
        grid_spec=pltpu.PrefetchScalarGridSpec(
            num_scalar_prefetch=1,
            grid=(columns // tile,),
            in_specs=[
                pl.BlockSpec((rows, width), lambda c, _: (0, 0)),
                pl.BlockSpec((rows, tile), lambda c, _: (0, c)),
            ],
            out_specs=[
                pl.BlockSpec((half, tile), lambda c, _: (0, c)),
                pl.BlockSpec((packed, tile), lambda c, _: (0, c)),
            ],
            scratch_shapes=[pltpu.VMEM((width, rows), bf16)] * 2,
        ),
        out_shape=[
            jax.ShapeDtypeStruct((half, columns), f32),
            jax.ShapeDtypeStruct((packed, columns), jnp.int16),
        ],
        compiler_params=pltpu.CompilerParams(vmem_limit_bytes=48 * 2**20),
        cost_estimate=pl.CostEstimate(
            flops=6 * rows * width * columns,
            bytes_accessed=4 * (rows * width + rows * columns) + 3 * width * columns,
            transcendentals=0,
        ),
    )(jnp.stack([bit]).astype(jnp.int32), x, y)


def shifted(value, by):
    length = lax.axis_size("seq")
    pairs = [(i, i + by) for i in range(length) if 0 <= i + by < length]
    return unpack_rows(lax.ppermute(pack_rows(value), "seq", pairs))


def product(formula, left_side, right_side):
    return jnp.einsum(
        formula,
        left_side.astype(f32),
        right_side.astype(f32),
        precision=fine,
        preferred_element_type=f32,
    )


def unit_rms(values):
    scale = lax.rsqrt(jnp.mean(values * values, axis=-1, keepdims=True) + eps)
    return values * scale, scale


def norm_back(unit, scale, scaled_grad):
    return scale * (scaled_grad - unit * jnp.mean(scaled_grad * unit, axis=-1, keepdims=True))


def gelu_both(values):
    squared = values * values
    bend = jnp.tanh(GELU_A * (values + GELU_B * squared * values))
    half = 0.5 * (1.0 + bend)
    slope = half + 0.5 * values * (1.0 - bend * bend) * GELU_A * (1.0 + 3.0 * GELU_B * squared)
    return values * half, slope


def local_slots(route_row, row_begin, span_rows, capacity):
    below = jnp.sum((route_row < row_begin).astype(jnp.int32))
    upper = jnp.sum((route_row < row_begin + span_rows).astype(jnp.int32))
    slot = below + jnp.arange(capacity, dtype=jnp.int32)
    index = jnp.arange(route_row.shape[0], dtype=jnp.int32)
    positions = jnp.sum(
        jnp.where(slot[:, None] == index[None, :], route_row[None, :], 0), axis=1
    )
    offsets = positions - row_begin
    matched = (offsets[:, None] == jnp.arange(span_rows, dtype=jnp.int32)[None, :]) & (
        slot < upper
    )[:, None]
    return positions, matched.astype(bf16)


def slot_table(route_row, span_rows, devices, capacity):
    home = route_row // span_rows
    before = jnp.sum((route_row[None, :] < (home * span_rows)[:, None]).astype(jnp.int32), axis=1)
    rank = jnp.arange(route_row.shape[0], dtype=jnp.int32) - before
    place = home * capacity + rank
    return (
        place[:, None] == jnp.arange(devices * capacity, dtype=jnp.int32)[None, :]
    ).astype(bf16)


def split(value):
    high = value.astype(bf16)
    return high, (value - high.astype(f32)).astype(bf16)


def dot_nt(a, b):
    return lax.dot_general(a, b, (((1,), (1,)), ((), ())), preferred_element_type=f32)


def dot_nn(a, b):
    return lax.dot_general(a, b, (((1,), (0,)), ((), ())), preferred_element_type=f32)


def dot_tn(a, b):
    return lax.dot_general(a, b, (((0,), (0,)), ((), ())), preferred_element_type=f32)


def two_heads(value):
    first = lax.broadcasted_iota(jnp.int32, value.shape, 1) < DH
    zero = jnp.zeros_like(value)
    return jnp.concatenate([jnp.where(first, value, zero), jnp.where(first, zero, value)], axis=0)


def one_row_each(value):
    half = value.shape[0] // 2
    first = lax.broadcasted_iota(jnp.int32, (half, value.shape[1]), 1) < DH
    return jnp.where(first, value[:half], value[half:])


def wide_nt(rows_high, rows_low, cols_high, cols_low):
    return dot_nt(
        jnp.concatenate([rows_high, rows_low], axis=1),
        jnp.concatenate([cols_high, cols_high], axis=1),
    ) + dot_nt(rows_high, cols_low)


def wide_nn(a_high, a_low, b_high, b_low):
    columns = b_high.shape[1]
    both = dot_nn(a_high, jnp.concatenate([b_high, b_low], axis=1))
    return both[:, :columns] + both[:, columns:] + dot_nn(a_low, b_high)


def wide_tn(a_high, a_low, b_high, b_low):
    return dot_tn(a_high, b_high) + dot_tn(a_low, b_high) + dot_tn(a_high, b_low)


def pair_probs(query, key_high, key_low, allowed):
    high, low = split(two_heads(query * DH**-0.5))
    scores = wide_nt(key_high, key_low, high, low)
    scores = jnp.where(allowed, scores, -1e30)
    weights = jnp.exp(scores - jnp.max(scores, axis=0, keepdims=True))
    return weights / jnp.sum(weights, axis=0, keepdims=True), high, low


def pair_forward(query, key, value, allowed):
    probs, _, _ = pair_probs(query, *split(key), allowed)
    mixed = wide_tn(*split(value), *split(probs))
    return one_row_each(mixed.T)


def pair_backward(query, key, value, d_out, allowed):
    key_high, key_low = split(key)
    probs, query_high, query_low = pair_probs(query, key_high, key_low, allowed)
    out_high, out_low = split(two_heads(d_out))
    d_value = wide_nn(*split(probs), out_high, out_low)
    d_probs = wide_nt(*split(value), out_high, out_low)
    dots = jnp.sum(probs * d_probs, axis=0, keepdims=True)
    score_high, score_low = split(probs * (d_probs - dots))
    d_key = wide_nn(score_high, score_low, query_high, query_low)
    d_query = wide_tn(key_high, key_low, score_high, score_low)
    return one_row_each(d_query.T) * DH**-0.5, d_key, d_value


def light_allowed(places, seq, block):
    begin, full_len, prefix = places[0], places[1], places[2 + seq]
    shape = (3 * W, 2 * W)
    key_pos = begin + (block - 1) * W + lax.broadcasted_iota(jnp.int32, shape, 0)
    lane = lax.broadcasted_iota(jnp.int32, shape, 1)
    query_pos = begin + block * W + jnp.where(lane < W, lane, lane - W)
    near = jnp.abs(query_pos - key_pos) < W
    inside = (key_pos >= 0) & (key_pos < full_len)
    return near & inside & ((key_pos <= query_pos) | (key_pos < prefix))


def light_forward_kernel(places, q, kv, out):
    seq, block = pl.program_id(0), pl.program_id(1)
    allowed = light_allowed(places, seq, block)
    span = pl.ds(pl.multiple_of(block * W, W), 3 * W)
    for pair in range(HL // 2):
        lanes = slice(2 * DH * pair, 2 * DH * (pair + 1))
        values = slice(IL + 2 * DH * pair, IL + 2 * DH * (pair + 1))
        out[0, :, lanes] = pair_forward(
            q[0, :, lanes], kv[0, span, lanes], kv[0, span, values], allowed
        )


def light_backward_kernel(places, q, kv, d_out, d_q, d_kv):
    seq, block = pl.program_id(0), pl.program_id(1)
    allowed = light_allowed(places, seq, block)
    span = pl.ds(pl.multiple_of(block * W, W), 3 * W)

    @pl.when(block == 0)
    def _():
        d_kv[...] = jnp.zeros_like(d_kv)

    for pair in range(HL // 2):
        lanes = slice(2 * DH * pair, 2 * DH * (pair + 1))
        values = slice(IL + 2 * DH * pair, IL + 2 * DH * (pair + 1))
        d_query, d_key, d_value = pair_backward(
            q[0, :, lanes], kv[0, span, lanes], kv[0, span, values], d_out[0, :, lanes], allowed
        )
        d_q[0, :, lanes] = d_query
        d_kv[0, span, lanes] += d_key
        d_kv[0, span, values] += d_value


def light_call(kernel, places, args, out_shapes, flops):
    seqs, rows, _ = args[0].shape

    def spec(shape):
        if shape[1] == rows:
            return pl.BlockSpec((1, W, shape[2]), lambda s, b, _: (s, b, 0))
        return pl.BlockSpec((1,) + shape[1:], lambda s, b, _: (s, 0, 0))

    return pl.pallas_call(
        kernel,
        name=kernel.__name__,
        grid_spec=pltpu.PrefetchScalarGridSpec(
            num_scalar_prefetch=1,
            grid=(seqs, rows // W),
            in_specs=[spec(a.shape) for a in args],
            out_specs=[spec(o) for o in out_shapes],
        ),
        out_shape=[jax.ShapeDtypeStruct(o, f32) for o in out_shapes],
        compiler_params=pltpu.CompilerParams(vmem_limit_bytes=48 * 2**20),
        cost_estimate=pl.CostEstimate(flops=flops, bytes_accessed=2**23, transcendentals=2**21),
    )(places, *args)


def heavy_allowed(prefix, key_pos, query_pos):
    return (key_pos <= query_pos) | (key_pos < prefix)


def heavy_forward_kernel(places, key_pos, query_pos, q, kv, out):
    allowed = heavy_allowed(places[2 + pl.program_id(0)], key_pos[0], query_pos[0])
    for pair in range(HH // 2):
        lanes = slice(2 * DH * pair, 2 * DH * (pair + 1))
        values = slice(IH + 2 * DH * pair, IH + 2 * DH * (pair + 1))
        out[0, :, lanes] = pair_forward(
            q[0, :, lanes], kv[0, :, lanes], kv[0, :, values], allowed
        )


def heavy_backward_kernel(places, key_pos, query_pos, q, kv, d_out, d_q, d_kv):
    allowed = heavy_allowed(places[2 + pl.program_id(0)], key_pos[0], query_pos[0])
    for pair in range(HH // 2):
        lanes = slice(2 * DH * pair, 2 * DH * (pair + 1))
        values = slice(IH + 2 * DH * pair, IH + 2 * DH * (pair + 1))
        d_query, d_key, d_value = pair_backward(
            q[0, :, lanes], kv[0, :, lanes], kv[0, :, values], d_out[0, :, lanes], allowed
        )
        d_q[0, :, lanes] = d_query
        d_kv[0, :, lanes] = d_key
        d_kv[0, :, values] = d_value


def heavy_call(kernel, places, args, out_shapes, flops):
    def spec(shape):
        return pl.BlockSpec((1,) + shape[1:], lambda s, _: (s, 0, 0))

    return pl.pallas_call(
        kernel,
        name=kernel.__name__,
        grid_spec=pltpu.PrefetchScalarGridSpec(
            num_scalar_prefetch=1,
            grid=(args[0].shape[0],),
            in_specs=[spec(a.shape) for a in args],
            out_specs=[spec(o) for o in out_shapes],
        ),
        out_shape=[jax.ShapeDtypeStruct(o, f32) for o in out_shapes],
        compiler_params=pltpu.CompilerParams(vmem_limit_bytes=48 * 2**20),
        cost_estimate=pl.CostEstimate(flops=flops, bytes_accessed=2**23, transcendentals=2**20),
    )(places, *args)


def on_device(
    tokens,
    cotangent,
    prefix_len,
    query_routes,
    key_routes,
    ffn_routes,
    light_qkv,
    light_out,
    heavy_qkv,
    heavy_out,
    light_ff_in,
    light_ff_out,
    heavy_ff_in,
    heavy_ff_out,
    gains,
    routers,
):
    seqs, rows, width = tokens.shape
    devices = lax.axis_size("seq")
    row_begin = lax.axis_index("seq") * rows
    full_len = rows * devices
    capacity = rows // 4
    units = FH // GROUP

    batch_bits = bit_stages("batch")
    far = devices // GROUP
    device_rows = width // (devices * lax.axis_size("batch"))
    core = lax.axis_index("batch") % 2
    tiled = len(batch_bits) == 1 and device_rows % 8 == 0
    links = Links()

    def joined(*pieces):
        return jnp.concatenate(pieces, axis=1)

    def flat(value):
        return value.reshape(-1, value.shape[-1])

    def chip_gather(value, turned):
        for stage in batch_bits:
            (other,) = links.flip([value], stage)
            value = joined_halves(value, other, own_bit(stage), turned)
            value = value.reshape((value.shape[0] * value.shape[1],) + value.shape[2:])
            turned = False
        return flat(value)

    class Sum:
        def __init__(self, pieces, depth, first):
            self.depth, self.first, self.value = depth, first, None
            if not tiled:
                value = joined(
                    *[p if not isinstance(p, tuple) else product("rd,re->de", *p) for p in pieces]
                )
                value = value.reshape((2,) * len(batch_bits) + (-1, value.shape[1]))
                for stage in batch_bits[::-1]:
                    mine = own_bit(stage)
                    sent = lax.dynamic_index_in_dim(value, 1 - mine, 0, keepdims=False)
                    kept = lax.dynamic_index_in_dim(value, mine, 0, keepdims=False)
                    value = kept + links.flip([sent], stage)[0]
                self.value = value.reshape(far, GROUP, device_rows, -1)
                return
            kept, sent = [], []
            for p in pieces:
                if isinstance(p, tuple):
                    mine, other = grad_split(*p, core, depth)
                else:
                    p = p.reshape(2, -1, depth, p.shape[1])
                    mine = lax.dynamic_index_in_dim(p, core, 0, keepdims=False)
                    other = lax.dynamic_index_in_dim(p, 1 - core, 0, keepdims=False)
                    power = power_of(other)
                    spare = jnp.zeros((power_rows(len(other)) - len(other), p.shape[3]), f32)
                    other = jnp.concatenate(
                        [flat(steps_of(other, power)), flat(power), spare], axis=0
                    ).astype(jnp.int16)
                kept.append(mine.reshape(-1, depth, mine.shape[-1]))
                sent.append(other)
            got = links.flip(sent, batch_bits[0])
            if first == "near":
                layout = [[(f * GROUP + p, 0, depth) for f in range(far)] for p in range(GROUP)]
            else:
                layout = [[(f, 0, depth)] for f in range(far)]
            self.sent = send_form(kept, got, layout, first == "far")

        def near(self):
            if not tiled:
                if self.first == "near":
                    self.value = jnp.sum(links.near(jnp.swapaxes(self.value, 0, 1)), axis=0)
                else:
                    self.value = links.near(self.value)
                return
            self.value = links.near(self.sent)
            if self.first == "near":
                layout = [[(f, 0, self.depth)] for f in range(far)]
                self.sent = arrived(self.value, far, self.depth, layout, True)

        def far(self):
            if not tiled:
                parts = [
                    lax.dynamic_index_in_dim(self.value, far_place() ^ j, 0, keepdims=False)
                    for j in range(far)
                ]
                self.value = sum(links.far(parts))
                return
            self.value = links.far(self.sent)
            if self.first == "far":
                layout = [
                    [(0, p * device_rows, (p + 1) * device_rows)] for p in range(GROUP)
                ]
                self.sent = arrived(self.value, 1, self.depth, layout)

        def result(self):
            if not tiled:
                return self.value
            if self.first == "near":
                return arrived(self.value, 1, self.depth)
            value = self.value.astype(f32)
            power = value[:, device_rows : device_rows + 1]
            return value[:, :device_rows] * jnp.exp2(power - 15.0)

    n_one, r_one = unit_rms(tokens)
    def picker(route_row):
        return local_slots(route_row, row_begin, rows, capacity)

    query_at, query_pick = jax.vmap(picker)(query_routes)
    _, key_pick = jax.vmap(picker)(key_routes)
    _, ffn_pick = jax.vmap(picker)(ffn_routes)
    table = jax.vmap(lambda r: slot_table(r, rows, devices, capacity))(key_routes)

    picked = product("sct,std->scd", jnp.concatenate([query_pick, key_pick], axis=1), n_one)
    query_unit, key_unit_own = picked[:, :capacity], picked[:, capacity:]

    spare = jnp.zeros((gains.shape[0], 128 - 5), bf16)
    before = shifted(tokens[:, rows - W :], 1)
    after_rows = shifted(tokens[:, :W], -1)
    first = links.far_share(joined(light_qkv, heavy_qkv, gains, routers, spare))
    key_far = links.far_share(pack_rows(key_unit_own))
    first = links.near_share(stacked(first, far_place()))
    key_far = stacked(key_far, far_place())
    first, key_far = after([first, key_far], [])

    def unit_parts(value):
        return jnp.swapaxes(value.reshape(value.shape[0], -1, units), 0, 1)

    big = jnp.concatenate(
        [
            unit_parts(heavy_ff_in).reshape(2, GROUP, device_rows, units),
            unit_parts(heavy_ff_out).reshape(1, GROUP, device_rows, units),
        ]
    )
    big = jnp.swapaxes(big, 0, 1).transpose(0, 2, 1, 3).reshape(GROUP, device_rows, 3 * units)
    big = links.near(big)
    first = chip_gather(first, True)
    (first,) = after([first], [big])
    keys = links.near_share(key_far)
    later_far = links.far_share(joined(light_out, heavy_out, light_ff_out, light_ff_in))
    big = links.far_share(big)
    qkv_light, qkv_heavy = first[:, : 3 * IL], first[:, 3 * IL : 3 * IL + 3 * IH]
    small = first[:, 3 * (IL + IH) :].astype(f32)
    gain_one, gain_two = small[:, 0], small[:, 1]
    router_q, router_k, router_f = small[:, 2], small[:, 3], small[:, 4]

    key_slots = unpack_rows(keys.transpose(2, 1, 0, 3, 4)).reshape(seqs, -1, width)
    cot_own = product("sct,std->scd", ffn_pick, cotangent)

    n_ext = unit_rms(jnp.concatenate([before, tokens, after_rows], axis=1))[0]
    normed_ext = n_ext * gain_one
    normed = n_one * gain_one
    light_q = product("std,de->ste", normed, qkv_light[:, :IL])
    light_kv = product("std,de->ste", normed_ext, qkv_light[:, IL:])
    places = jnp.concatenate(
        [jnp.stack([row_begin, jnp.int32(full_len)]), prefix_len]
    ).astype(jnp.int32)
    later = links.near_share(stacked(after(later_far, [light_kv]), far_place()))
    (attended,) = light_call(
        light_forward_kernel, places, (light_q, light_kv), (light_q.shape,), 2**33
    )
    query_rows = query_unit * gain_one
    key_unit = product("skp,spd->skd", table, key_slots)
    key_rows = key_unit * gain_one
    query_score = jax.nn.sigmoid(jnp.sum(query_rows * router_q, axis=-1))
    key_score = jax.nn.sigmoid(jnp.sum(key_rows * router_k, axis=-1))
    heavy_q = product("scd,di->sci", query_rows, qkv_heavy[:, :IH])
    heavy_kv = product("skd,de->ske", key_rows, qkv_heavy[:, IH:])
    heavy_v_raw = heavy_kv[..., IH:]
    heavy_kv = jnp.concatenate(
        [heavy_kv[..., :IH], heavy_v_raw * key_score[..., None]], axis=-1
    )
    key_column = key_routes[:, :, None]
    query_row = jnp.concatenate([query_at, query_at], axis=1)[:, None, :]
    (heavy_mixed,) = heavy_call(
        heavy_forward_kernel,
        places,
        (key_column, query_row, heavy_q, heavy_kv),
        (heavy_q.shape,),
        2**33,
    )
    big = stacked(after(big, [attended]), far_place())
    later = chip_gather(later, True)
    out_light, out_heavy = later[:, :IL], later[:, IL : IL + IH]
    ff_out, ff_in = later[:, IL + IH : IL + IH + FL], later[:, IL + IH + FL :]
    light_branch = product("sti,di->std", attended, out_light)
    big = chip_gather(big, False)
    big_in, big_out = big[:, : 2 * units], big[:, 2 * units :]

    heavy_plain = product("sci,di->scd", heavy_mixed, out_heavy)
    heavy_rows = heavy_plain * query_score[..., None]
    hidden = tokens + light_branch + product("sct,scd->std", query_pick, heavy_rows)

    n_two, r_two = unit_rms(hidden)
    second = n_two * gain_two
    ffn_own = product("sct,std->scd", ffn_pick, second)
    routed = unpack_rows(links.near_share(pack_rows(jnp.stack([ffn_own, cot_own]))))
    ffn_rows, cot_rows = (flat(routed[:, i]) for i in range(2))
    gate_up = product("std,de->ste", second, ff_in)
    gate, up = gate_up[..., :FL], gate_up[..., FL:]
    gate_act, gate_slope = gelu_both(gate)
    light_act = gate_act * up
    light_ff = product("stf,df->std", light_act, ff_out)
    d_act = product("std,df->stf", cotangent, ff_out)
    d_gate_up = jnp.concatenate([d_act * up * gate_slope, d_act * gate_act], axis=-1)
    d_second = product("ste,de->std", d_gate_up, ff_in)
    d_ff = Sum(
        [(flat(cotangent), flat(light_act)), (flat(second), flat(d_gate_up))], device_rows, "near"
    )

    ffn_score = jax.nn.sigmoid(jnp.sum(ffn_rows * router_f, axis=-1, keepdims=True))
    big_gate_up = product("rd,de->re", ffn_rows, big_in)
    big_gate, big_up = big_gate_up[:, :units], big_gate_up[:, units:]
    big_act, big_slope = gelu_both(big_gate)
    big_mix = big_act * big_up
    cot_mix = product("rd,df->rf", cot_rows, big_out)
    d_score = jnp.sum(cot_mix * big_mix, axis=-1, keepdims=True)
    d_score_in = d_score * ffn_score * (1.0 - ffn_score)
    d_mix = cot_mix * ffn_score
    d_big = jnp.concatenate([d_mix * big_up * big_slope, d_mix * big_act], axis=-1)
    d_ffn_rows = product("re,de->rd", d_big, big_in) + d_score_in * router_f
    d_router_f = jnp.sum(d_score_in * ffn_rows, axis=0)

    big_rows = product("rf,df->rd", big_mix, big_out) * ffn_score
    both = jnp.stack([d_ffn_rows, big_rows]).reshape(-1, capacity, width)
    layout = [
        [((m * GROUP + p) * seqs + i, 0, capacity) for m in range(2) for i in range(seqs)]
        for p in range(GROUP)
    ]
    back = arrived(
        links.near(send_form([both], [None], layout, False)), 2 * seqs, capacity
    ).reshape(2, seqs, capacity, width)
    ffn_own, out_own = back[0], back[1]
    d_big_all = Sum(
        [(ffn_rows, d_big), (cot_rows, big_mix * ffn_score)], GROUP * device_rows, "far"
    )
    d_big_all.far()
    d_ff.near()

    output = hidden + light_ff + product("sct,scd->std", ffn_pick, out_own)
    d_second = d_second + product("sct,scd->std", ffn_pick, ffn_own)
    d_gain_two = jnp.sum(d_second * n_two, axis=(0, 1))
    d_hidden = cotangent + norm_back(n_two, r_two, d_second * gain_two)

    d_heavy_rows = product("sct,std->scd", query_pick, d_hidden)
    d_query_score = jnp.sum(d_heavy_rows * heavy_plain, axis=-1)
    d_plain = d_heavy_rows * query_score[..., None]
    d_mixed = product("scd,di->sci", d_plain, out_heavy)
    d_attended = product("std,di->sti", d_hidden, out_light)
    (d_mixed,) = after([d_mixed], list(d_big_all.sent) if tiled else [d_big_all.value])
    d_hq, d_hkv = heavy_call(
        heavy_backward_kernel,
        places,
        (key_column, query_row, heavy_q, heavy_kv, d_mixed),
        (heavy_q.shape, heavy_kv.shape),
        2**34,
    )
    d_hq, d_hkv = after([d_hq, d_hkv], [d_ff.value])
    d_hv = d_hkv[..., IH:]
    d_key_score = jnp.sum(d_hv * heavy_v_raw, axis=-1)
    d_key_in = d_key_score * key_score * (1.0 - key_score)
    d_query_in = d_query_score * query_score * (1.0 - query_score)
    d_kv = jnp.concatenate([d_hkv[..., :IH], d_hv * key_score[..., None]], axis=-1)
    d_key_rows = product("ske,de->skd", d_kv, qkv_heavy[:, IH:]) + d_key_in[..., None] * router_k
    d_query_rows = (
        product("sci,di->scd", d_hq, qkv_heavy[:, :IH]) + d_query_in[..., None] * router_q
    )
    d_router_k = jnp.sum(d_key_in[..., None] * key_rows, axis=(0, 1))
    d_router_q = jnp.sum(d_query_in[..., None] * query_rows, axis=(0, 1))
    d_key_slots = product("skp,skd->spd", table, d_key_rows)
    layout = [
        [((i * far + f) * GROUP + p, 0, capacity) for f in range(far) for i in range(seqs)]
        for p in range(GROUP)
    ]
    key_sent = send_form([d_key_slots.reshape(-1, capacity, width)], [None], layout, False)
    key_near = links.near(key_sent)
    d_ff.far()
    layout = [[(f * seqs + i, 0, capacity) for i in range(seqs)] for f in range(far)]
    d_key_own = links.far(arrived(key_near, far * seqs, capacity, layout, True))
    d_key_own = arrived(d_key_own, seqs, capacity).reshape(seqs, capacity, width)
    d_mid = Sum(
        [
            (flat(d_hidden), flat(attended)),
            (flat(d_plain), flat(heavy_mixed)),
            (flat(query_rows), flat(d_hq)),
            (flat(key_rows), flat(d_kv)),
        ],
        device_rows,
        "near",
    )
    (d_attended,) = after([d_attended], [d_mid.sent if tiled else d_mid.value])

    d_lq, d_lkv = light_call(
        light_backward_kernel,
        places,
        (light_q, light_kv, d_attended),
        (light_q.shape, light_kv.shape),
        2**34,
    )
    d_lq, d_lkv = after([d_lq, d_lkv], [key_near])
    d_ext = product("ste,de->std", d_lkv, qkv_light[:, IL:])
    from_next = shifted(d_ext[:, :W], -1)
    from_prev = shifted(d_ext[:, W + rows :], 1)
    d_own = product("ste,de->std", d_lq, qkv_light[:, :IL]) + product(
        "sct,scd->std", query_pick, d_query_rows
    )
    d_gain_one = (
        jnp.sum(d_ext * n_ext, axis=(0, 1))
        + jnp.sum(d_own * n_one, axis=(0, 1))
        + jnp.sum(d_key_rows * key_unit, axis=(0, 1))
    )
    edges = jnp.pad(from_prev, ((0, 0), (0, rows - W), (0, 0))) + jnp.pad(
        from_next, ((0, 0), (rows - W, 0), (0, 0))
    )
    vectors = jnp.stack([d_gain_one, d_gain_two, d_router_q, d_router_k, d_router_f])
    vectors = jnp.pad(vectors, ((0, 128 - 5), (0, 0))).T
    last = Sum(
        [(flat(normed), flat(d_lq)), (flat(normed_ext), flat(d_lkv)), vectors],
        device_rows,
        "near",
    )
    d_mid.near()
    last.near()
    d_mid.far()
    last.far()
    d_big_all.near()
    d_ff, d_mid, last = d_ff.result(), d_mid.result(), last.result()
    d_big_all = d_big_all.result()
    vectors = last[:, 3 * IL :]

    def spread(value):
        return jnp.swapaxes(value, 0, 1).reshape(value.shape[1], -1)

    d_heavy_ff_in = joined(
        spread(d_big_all[..., :units]), spread(d_big_all[..., units : 2 * units])
    )
    d_heavy_ff_out = spread(d_big_all[..., 2 * units :])

    d_normed = (
        d_own
        + d_ext[:, W : W + rows]
        + edges
        + product("sct,scd->std", key_pick, d_key_own)
    )
    grad_tokens = d_hidden + norm_back(n_one, r_one, d_normed * gain_one)

    return (
        output,
        grad_tokens,
        last[:, : 3 * IL],
        d_mid[:, :IL],
        d_mid[:, IL + IH :],
        d_mid[:, IL : IL + IH],
        d_ff[:, FL:],
        d_ff[:, :FL],
        d_heavy_ff_in,
        d_heavy_ff_out,
        vectors[:, :2],
        vectors[:, 2:5],
    )


def solution(mesh):
    rows = P("batch", "seq", None)
    routes = P("batch", None)
    weight = P(("batch", "seq"), None)
    return jax.shard_map(
        on_device,
        mesh=mesh,
        in_specs=(rows, rows, P("batch"), routes, routes, routes) + (weight,) * 10,
        out_specs=(rows, rows) + (weight,) * 10,
        check_vma=False,
    )
```

time: 1130 us -> 653 us (0.58)
  waiting for transfers between devices: 421 us -> 93.9 us
  Pallas kernels: 0 us -> 195 us
  local copies, waits for them, and re-layouts: 227 us -> 64.5 us
  matrix products: 208 us -> 107 us
  other arithmetic: 116 us -> 57.8 us
  starting transfers between devices: 146 us -> 120 us
    ppermute x104 -> x45, waiting for transfers between devices: 421 us -> 65.2 us  [the longest x27 46.7 us: far(): lax.ppermute(v, 'seq', [(i, i ^ GROUP * j) for i in range(devices)])]
    pallas_call x0 -> x37, Pallas kernels: none -> 195 us  [the longest x10 57.7 us: grad_split(): pl.pallas_call(lambda *refs: grad_kernel(depth, *refs), name='grad', grid...]
    dot_general x53 -> x31, matrix products: 208 us -> 107 us  [product(): jnp.einsum(formula, left_side.astype(f32), right_side.astype(f32), precis...]
    ppermute x104 -> x45, starting transfers between devices: 146 us -> 69.4 us  [the longest x27 54.6 us: far(): lax.ppermute(v, 'seq', [(i, i ^ GROUP * j) for i in range(devices)])]
    scatter-add x6 -> x0, local copies, waits for them, and re-layouts: 66.1 us -> none  [overlapped(): total = total.at[:, b:b + 3].add(value[:, b])]
    all_to_all x0 -> x11, starting transfers between devices: none -> 50.7 us  [near(): lax.all_to_all(value, 'seq', 0, 0, axis_index_groups=groups, tiled=True)]
    another operation x101 -> x6, other arithmetic: 34.5 us -> 2.71 us  [the longest x94 33.3 us: gather_blocks(): value = jnp.stack([low, high], axis=at)]
    reshape x9 -> x5, local copies, waits for them, and re-layouts: 35.5 us -> 3.84 us  [the longest x1 1.95 us: on_device(): jnp.swapaxes(big, 0, 1).transpose(0, 2, 1, 3)]
  transfers between devices with their start and end apart: 104 -> 56, of which waited for: 51 -> 17; matrix products, arithmetic and copies ran while one was open for 46% -> 29% of each run, Pallas kernels for 0% -> 25%
where the time goes in v2:
time: 653 us; the launch traced here: 641 us
  Pallas kernels  195 us (30%)
  starting transfers between devices  120 us (18%)
  matrix products  107 us (16%)
  waiting for transfers between devices  93.9 us (14%)
  local copies, waits for them, and re-layouts  64.5 us (10%)
  other arithmetic  57.8 us (9%)
    dot_general x31, matrix products, product(): jnp.einsum(formula, left_side.astype(f32), right_side.astype(f32), precis...  107 us
    pallas_call x10, Pallas kernels, grad_split(): pl.pallas_call(lambda *refs: grad_kernel(depth, *refs), name='grad', grid...  57.7 us
    ppermute x27, starting transfers between devices, far(): lax.ppermute(v, 'seq', [(i, i ^ GROUP * j) for i in range(devices)])  54.6 us
    all_to_all x11, starting transfers between devices, near(): lax.all_to_all(value, 'seq', 0, 0, axis_index_groups=groups, tiled=True)  50.7 us
    ppermute x27, waiting for transfers between devices, far(): lax.ppermute(v, 'seq', [(i, i ^ GROUP * j) for i in range(devices)])  46.7 us
    pallas_call x6, Pallas kernels, send_form(): pl.pallas_call(lambda *refs: send_kernel(spans, layout, received, far, *r...  36.1 us
    unnamed x235, local copies, waits for them, and re-layouts  34.2 us
    pallas_call x2, Pallas kernels, light_call(): pl.pallas_call(kernel, name=kernel.__name__, grid_spec=pltpu.PrefetchScal...  32.3 us
  transfers between devices with their start and end apart: 56, of which 17 were waited for; matrix products, arithmetic and copies ran while one was open for 29% of the time, Pallas kernels for 25%

profile of v2, /device:TPU:0, one launch (start us, length us, event | category | flops | bytes accessed | tf_op | source)
XLA Modules:
  0.0 641.4 jit_solution(741107281470901362)
XLA Ops:
  46.2 8.1 %collective-permute-done.4.refs_2_ = s16[2,72,768]{2,1,0:T(8,128)(2,1)S(1)} collective-permute-done((s16[2,72,768]{2,1,0:T(8,128)(2,1)S(1)}, s16[2,72,768]{2,1,0:T(8,128)(2,1)S(1)}, u32[]{:S(2)}, u32[]{:S(2)}) %collective-permute-start.4) | collective-permute-done | bytes 221216 | tf_op jit(solution)/shard_map/ppermute | solution.py:70
  55.4 11.9 %all-to-all-done.value = bf16[4,4,24,3968]{3,2,1,0:T(8,128)(2,1)S(1)} async-done(((bf16[4,4,24,3968]{3,2,1,0:T(8,128)(2,1)}), bf16[4,4,24,3968]{3,2,1,0:T(8,128)(2,1)S(1)}, u32[]{:S(2)}, u32[]{:S(2)}) %all-to-all-start) | async-done | bytes 3047456 | tf_op jit(solution)/shard_map/all_to_all | solution.py:59
  76.8 7.2 %all-to-all-done.1.refs_0_ = bf16[4,24,3072]{2,1,0:T(8,128)(2,1)} async-done(((bf16[4,24,3072]{2,1,0:T(8,128)(2,1)}), bf16[4,24,3072]{2,1,0:T(8,128)(2,1)}, u32[]{:S(2)}, u32[]{:S(2)}) %all-to-all-start.1) | async-done | bytes 589856 | tf_op jit(solution)/shard_map/all_to_all | solution.py:59
  106.9 10.1 %collective-permute-done.10.refs_2_ = bf16[24,4352]{1,0:T(8,128)(2,1)S(1)} collective-permute-done((bf16[24,4352]{1,0:T(8,128)(2,1)S(1)}, bf16[24,4352]{1,0:T(8,128)(2,1)S(1)}, u32[]{:S(2)}, u32[]{:S(2)}) %collective-permute-start.10) | collective-permute-done | bytes 208928 | tf_op jit(solution)/shard_map/ppermute | solution.py:70
  145.9 9.0 %light_forward_kernel.1 = f32[2,256,512]{2,1,0:T(8,128)S(1)} custom-call(s32[4]{0:T(128)S(1)} %pad_add_fusion.8.places, f32[2,256,512]{2,1,0:T(8,128)S(1)} %fusion.56.q, f32[2,512,1024]{2,1,0:T(8,128)} %fusion.3.kv), custom_call_target="tpu_custom_call" | custom-call | flops 8589934592 | bytes 8388608 | tf_op jit(solution)/shard_map/light_forward_kernel/pallas_call | solution.py:580
  154.9 8.0 %collective-permute-done.14.refs_2_ = bf16[4,24,3072]{2,1,0:T(8,128)(2,1)} collective-permute-done((bf16[4,24,3072]{2,1,0:T(8,128)(2,1)}, bf16[4,24,3072]{2,1,0:T(8,128)(2,1)}, u32[]{:S(2)}, u32[]{:S(2)}) %collective-permute-start.14) | collective-permute-done | bytes 589856 | tf_op jit(solution)/shard_map/ppermute | solution.py:70
  184.0 6.4 %multiply_reduce_fusion.4 = (f32[2,512]{1,0:T(2,128)S(1)}, f32[2,512,768]{2,1,0:T(8,128)S(1)}, f32[2,512,768]{2,1,0:T(8,128)}) fusion(f32[768]{0:T(1024)S(1)} %get-tuple-element.283, f32[768]{0:T(1024)S(1)} %get-tuple-element.284, f32[2,1024,768]{2,1,0:T(8,128)S(1)} %bitcast.248, s32[2,512]{1,0:T(2,128)S(1)} %subtract_add_fusion), kind=kOutput, calls=%fused_computation.22 | convolution fusion | flops 4835245056 | bytes 12597248 | tf_op jit(solution)/shard_map/skp,spd->skd/dot_general | solution.py:405
  192.2 6.9 %fusion.14 = f32[2,512,1536]{2,1,0:T(8,128)S(1)} fusion(f32[2,512,768]{2,1,0:T(8,128)S(1)} %get-tuple-element.300, bf16[768,3968]{1,0:T(8,128)(2,1)} %bitcast.201), kind=kOutput, calls=%fused_computation.37 | convolution fusion | flops 7247757312 | bytes 11796480 | tf_op jit(solution)/shard_map/skd,de->ske/dot_general | solution.py:405
  205.3 8.8 %heavy_forward_kernel.1 = f32[2,64,768]{2,1,0:T(8,128)S(1)} custom-call(s32[4]{0:T(128)S(1)} %pad_add_fusion.8.places, s32[2,512,1]{2,1,0:T(8,128)S(1)} %copy-done.31, s32[2,1,128]{2,1,0:T(1,128)S(1)} %bitcast.246, f32[2,64,768]{2,1,0:T(8,128)S(1)} %copy-done.38, f32[2,512,1536]{2,1,0:T(8,128)} %pad_maximum_fusion.kv), custom_call_target="tpu_custom_call" | custom-call | flops 8589934592 | bytes 8388608 | tf_op jit(solution)/shard_map/heavy_forward_kernel/pallas_call | solution.py:626
  240.2 6.2 fusion.20
  249.7 8.9 %grad.13 = (f32[384,2048]{1,0:T(8,128)}, s16[400,2048]{1,0:T(8,128)(2,1)}) custom-call(s32[1]{0:T(128)} %bitcast.1.bit.refs_0_, f32[512,768]{1,0:T(8,128)S(1)} %bitcast.217, f32[512,2048]{1,0:T(8,128)} %bitcast.251), custom_call_target="tpu_custom_call" | custom-call | flops 4831838208 | bytes 10485760 | tf_op jit(solution)/shard_map/grad/pallas_call | solution.py:369
  309.7 8.6 %grad.16 = (f32[384,2048]{1,0:T(8,128)}, s16[400,2048]{1,0:T(8,128)(2,1)}) custom-call(s32[1]{0:T(128)} %bitcast.1.bit.refs_0_, f32[512,768]{1,0:T(8,128)S(1)} %bitcast.234, f32[512,2048]{1,0:T(8,128)} %pad_maximum_fusion.2.refs_2_), custom_call_target="tpu_custom_call" | custom-call | flops 4831838208 | bytes 10485760 | tf_op jit(solution)/shard_map/grad/pallas_call | solution.py:369
  318.5 7.0 %send.7 = s16[4,112,3072]{2,1,0:T(8,128)(2,1)} custom-call(s32[1]{0:T(128)} %bitcast.2.place.refs_0_, f32[16,24,1024]{2,1,0:T(8,128)S(1)} %bitcast.231, f32[16,24,2048]{2,1,0:T(8,128)} %bitcast.253, s16[400,1024]{1,0:T(8,128)(2,1)S(1)} %collective-permute-done.17.refs_3_, s16[400,2048]{1,0:T(8,128)(2,1)} %collective-permute-done.18.refs_4_), custom_call_target="tpu_custom_call" | custom-call | flops 23592960 | bytes 9437184 | tf_op jit(solution)/shard_map/send/pallas_call | solution.py:277
  342.4 15.4 %heavy_backward_kernel.1 = (f32[2,64,768]{2,1,0:T(8,128)S(1)}, f32[2,512,1536]{2,1,0:T(8,128)}) custom-call(s32[4]{0:T(128)S(1)} %pad_add_fusion.8.places, s32[2,512,1]{2,1,0:T(8,128)S(1)} %copy-done.32, s32[2,1,128]{2,1,0:T(1,128)S(1)} %bitcast.247, f32[2,64,768]{2,1,0:T(8,128)S(1)} %copy-done.39, f32[2,512,1536]{2,1,0:T(8,128)} %pad_maximum_fusion.kv, ...), custom_call_target="tpu_custom_call" | custom-call | flops 17179869184 | bytes 8388608 | tf_op jit(solution)/shard_map/heavy_backward_kernel/pallas_call | solution.py:626
  361.3 6.7 %send.10 = (s16[112,3072]{1,0:T(8,128)(2,1)S(1)}, s16[112,3072]{1,0:T(8,128)(2,1)}, s16[112,3072]{1,0:T(8,128)(2,1)}, s16[112,3072]{1,0:T(8,128)(2,1)}) custom-call(s32[1]{0:T(128)} %bitcast.2.place.refs_0_, f32[4,96,2048]{2,1,0:T(8,128)} %bitcast.254, f32[4,96,1024]{2,1,0:T(8,128)S(1)} %bitcast.230, s16[400,2048]{1,0:T(8,128)(2,1)} %collective-permute-done.25.refs_3_, ...), custom_call_target="tpu_custom_call" | custom-call | flops 23592960 | bytes 9437184 | tf_op jit(solution)/shard_map/send/pallas_call | solution.py:277
  368.9 6.7 %collective-permute-start.27 = (s16[112,3072]{1,0:T(8,128)(2,1)}, s16[112,3072]{1,0:T(8,128)(2,1)}, u32[]{:S(2)}, u32[]{:S(2)}) collective-permute-start(s16[112,3072]{1,0:T(8,128)(2,1)} %get-tuple-element.168), channel_id=1, source_target_pairs={{0,4},{1,5},{2,6},{3,7},{4,0},{5,1},{6,2},{7,3},{8,12},{9,13},{10,... | collective-permute-start | bytes 2064392 | tf_op jit(solution)/shard_map/ppermute | solution.py:70
  386.0 13.7 %grad.15 = (f32[384,1536]{1,0:T(8,128)S(1)}, s16[400,1536]{1,0:T(8,128)(2,1)}) custom-call(s32[1]{0:T(128)} %bitcast.1.bit.refs_0_, f32[1024,768]{1,0:T(8,128)} %bitcast.255, f32[1024,1536]{1,0:T(8,128)} %bitcast.250), custom_call_target="tpu_custom_call" | custom-call | flops 7247757312 | bytes 12976128 | tf_op jit(solution)/shard_map/grad/pallas_call | solution.py:369
  399.8 9.4 %multiply_reduce_fusion = (f32[768]{0:T(1024)S(1)}, f32[768]{0:T(1024)}, f32[2,512,768]{2,1,0:T(8,128)S(1)}) fusion(f32[2,512,768]{2,1,0:T(8,128)S(1)} %copy-done.70, f32[2,512]{1,0:T(2,128)S(1)} %subtract_multiply_fusion.1, f32[2,512,768]{2,1,0:T(8,128)} %get-tuple-element.349, f32[768]{0:T(1024)S(1)} %get-tuple-element.283, ...), kind=kOutput, calls=%fused_computation.15 | convolution fusion | flops 7254047232 | bytes 18101248 | tf_op jit(solution)/shard_map/ske,de->skd/dot_general | solution.py:405
  451.4 10.0 %send.8 = s16[4,112,3584]{2,1,0:T(8,128)(2,1)} custom-call(s32[1]{0:T(128)} %bitcast.2.place.refs_0_, f32[16,24,512]{2,1,0:T(8,128)S(1)} %bitcast.243, f32[16,24,768]{2,1,0:T(8,128)S(1)} %bitcast.238, f32[16,24,768]{2,1,0:T(8,128)S(1)} %bitcast.239, f32[16,24,1536]{2,1,0:T(8,128)} %bitcast.227, s16[400,512]{1,0:T(8,128)(2,1)S(1)} %collective-permute-done.19.refs_5_, ...), custom_call_target="tpu_custom_call" | custom-call | flops 27525120 | bytes 11010048 | tf_op jit(solution)/shard_map/send/pallas_call | solution.py:277
  461.4 23.3 %light_backward_kernel.1 = (f32[2,256,512]{2,1,0:T(8,128)S(1)}, f32[2,512,1024]{2,1,0:T(8,128)}) custom-call(s32[4]{0:T(128)S(1)} %pad_add_fusion.8.places, f32[2,256,512]{2,1,0:T(8,128)S(1)} %copy-done.23, f32[2,512,1024]{2,1,0:T(8,128)} %fusion.3.kv, f32[2,256,512]{2,1,0:T(8,128)S(1)} %fusion.61.d_out), custom_call_target="tpu_custom_call" | custom-call | flops 17179869184 | bytes 8388608 | tf_op jit(solution)/shard_map/light_backward_kernel/pallas_call | solution.py:580
  485.8 10.1 %multiply_reduce_fusion.2 = (f32[768]{0:T(1024)}, f32[2,512,768]{2,1,0:T(8,128)}, f32[2,512,768]{2,1,0:T(8,128)}) fusion(f32[2,512]{1,0:T(2,128)S(1)} %copy-done.87, f32[2,128,768]{2,1,0:T(8,128)S(1)} %copy-done.58, f32[2,256,768]{2,1,0:T(8,128)} %param.16, f32[2,128,768]{2,1,0:T(8,128)} %copy-done.59, f32[2,512,1024]{2,1,0:T(8,128)} %get-tuple-element.153, ...), kind=kOutput, calls=%fused_computation.17 | convolution fusion | flops 4835769344 | bytes 15211520 | tf_op jit(solution)/shard_map/ste,de->std/dot_general | solution.py:405
  518.9 9.2 %grad.19 = (f32[384,1024]{1,0:T(8,128)S(1)}, s16[400,1024]{1,0:T(8,128)(2,1)}) custom-call(s32[1]{0:T(128)} %bitcast.1.bit.refs_0_, f32[1024,768]{1,0:T(8,128)S(1)} %fusion.2.refs_1_, f32[1024,1024]{1,0:T(8,128)} %bitcast.252), custom_call_target="tpu_custom_call" | custom-call | flops 4831838208 | bytes 9699328 | tf_op jit(solution)/shard_map/grad/pallas_call | solution.py:369
  536.0 11.6 %collective-permute-done.24 = s16[2,136,768]{2,1,0:T(8,128)(2,1)S(1)} collective-permute-done((s16[2,136,768]{2,1,0:T(8,128)(2,1)S(1)}, s16[2,136,768]{2,1,0:T(8,128)(2,1)S(1)}, u32[]{:S(2)}, u32[]{:S(2)}) %collective-permute-start.24) | collective-permute-done | bytes 417824 | tf_op jit(solution)/shard_map/ppermute | solution.py:401
  565.9 6.4 send.11
  (533 shorter events, 408.3 us)
Async XLA Ops:
  11.8 87.7 %collective-permute-start.8 = (s16[2,136,768]{2,1,0:T(8,128)(2,1)}, s16[2,136,768]{2,1,0:T(8,128)(2,1)}, u32[]{:S(2)}, u32[]{:S(2)}) collective-permute-start(s16[2,136,768]{2,1,0:T(8,128)(2,1)} %pad_add_fusion.2), channel_id=1, source_target_pairs={{1,0},{2,1},{3,2},{4,3},{5,4},{6,5},{7,6},{8,7},{9,8},{10,9},{11,1... | collective-permute-start | bytes 1253384 | tf_op jit(solution)/shard_map/ppermute | solution.py:401
  13.9 88.7 %collective-permute-start.7 = (s16[2,136,768]{2,1,0:T(8,128)(2,1)}, s16[2,136,768]{2,1,0:T(8,128)(2,1)}, u32[]{:S(2)}, u32[]{:S(2)}) collective-permute-start(s16[2,136,768]{2,1,0:T(8,128)(2,1)} %pad_add_fusion.1), channel_id=1, source_target_pairs={{0,1},{1,2},{2,3},{3,4},{4,5},{5,6},{6,7},{7,8},{8,9},{9,10},{10,1... | collective-permute-start | bytes 1253384 | tf_op jit(solution)/shard_map/ppermute | solution.py:401
  67.3 55.2 %collective-permute-start.6 = (bf16[4,4,24,3968]{3,2,1,0:T(8,128)(2,1)S(1)}, bf16[4,4,24,3968]{3,2,1,0:T(8,128)(2,1)}, u32[]{:S(2)}, u32[]{:S(2)}) collective-permute-start(bf16[4,4,24,3968]{3,2,1,0:T(8,128)(2,1)S(1)} %all-to-all-done.value), channel_id=1, source_target_pairs={{0,16},{16,0},{1,17},{17,1},{2,18},{18,2},{3,19},{19,3},{4,20},{20... | collective-permute-start | bytes 9142280 | tf_op jit(solution)/shard_map/ppermute | solution.py:82
  87.2 49.8 %all-to-all-start.2 = ((s16[4,4,2,72,768]{4,3,1,2,0:T(8,128)(2,1)}), s16[4,4,2,72,768]{4,3,1,2,0:T(8,128)(2,1)}, u32[]{:S(2)}, u32[]{:S(2)}) async-start(s16[4,4,2,72,768]{4,3,1,2,0:T(8,128)(2,1)} %broadcast_in_dim.59), calls=%async_computation.2 | async-start | bytes 7077888 | tf_op jit(solution)/shard_map/all_to_all | solution.py:59
  120.2 42.8 %collective-permute-start.14 = (bf16[4,24,3072]{2,1,0:T(8,128)(2,1)}, bf16[4,24,3072]{2,1,0:T(8,128)(2,1)}, u32[]{:S(2)}, u32[]{:S(2)}) collective-permute-start(bf16[4,24,3072]{2,1,0:T(8,128)(2,1)} %all-to-all-done.1.refs_0_), channel_id=1, source_target_pairs={{0,8},{1,9},{2,10},{3,11},{4,12},{5,13},{6,14},{7,15},{8,0},{9,1},... | collective-permute-start | bytes 1769480 | tf_op jit(solution)/shard_map/ppermute | solution.py:70
  120.7 42.2 %collective-permute-start.15 = (bf16[4,24,3072]{2,1,0:T(8,128)(2,1)}, bf16[4,24,3072]{2,1,0:T(8,128)(2,1)}, u32[]{:S(2)}, u32[]{:S(2)}) collective-permute-start(bf16[4,24,3072]{2,1,0:T(8,128)(2,1)} %all-to-all-done.1.refs_0_), channel_id=1, source_target_pairs={{0,12},{1,13},{2,14},{3,15},{4,8},{5,9},{6,10},{7,11},{8,4},{9,5},... | collective-permute-start | bytes 1769480 | tf_op jit(solution)/shard_map/ppermute | solution.py:70
  139.0 41.7 %all-to-all-start.3 = ((bf16[4,4,24,4352]{3,2,1,0:T(8,128)(2,1)}), bf16[4,4,24,4352]{3,2,1,0:T(8,128)(2,1)S(1)}, u32[]{:S(2)}, u32[]{:S(2)}) async-start(bf16[4,4,24,4352]{3,2,1,0:T(8,128)(2,1)} %broadcast_in_dim.58), calls=%async_computation.3 | async-start | bytes 6684672 | tf_op jit(solution)/shard_map/all_to_all | solution.py:59
  166.5 47.6 %collective-permute-start.16 = (bf16[4,4,24,3072]{3,2,1,0:T(8,128)(2,1)}, bf16[4,4,24,3072]{3,2,1,0:T(8,128)(2,1)}, u32[]{:S(2)}, u32[]{:S(2)}) collective-permute-start(bf16[4,4,24,3072]{3,2,1,0:T(8,128)(2,1)} %stack.95.value), channel_id=1, source_target_pairs={{0,16},{16,0},{1,17},{17,1},{2,18},{18,2},{3,19},{19,3},{4,20},{20... | collective-permute-start | bytes 7077896 | tf_op jit(solution)/shard_map/ppermute | solution.py:82
  180.7 41.1 %collective-permute-start.12 = (bf16[4,4,24,4352]{3,2,1,0:T(8,128)(2,1)S(1)}, bf16[4,4,24,4352]{3,2,1,0:T(8,128)(2,1)S(1)}, u32[]{:S(2)}, u32[]{:S(2)}) collective-permute-start(bf16[4,4,24,4352]{3,2,1,0:T(8,128)(2,1)S(1)} %all-to-all-done.3.value), channel_id=1, source_target_pairs={{0,16},{16,0},{1,17},{17,1},{2,18},{18,2},{3,19},{19,3},{4,20},{20... | collective-permute-start | bytes 10027016 | tf_op jit(solution)/shard_map/ppermute | solution.py:82
  258.6 59.8 %collective-permute-start.18 = (s16[400,2048]{1,0:T(8,128)(2,1)}, s16[400,2048]{1,0:T(8,128)(2,1)}, u32[]{:S(2)}, u32[]{:S(2)}) collective-permute-start(s16[400,2048]{1,0:T(8,128)(2,1)} %get-tuple-element.138), channel_id=1, source_target_pairs={{0,16},{16,0},{1,17},{17,1},{2,18},{18,2},{3,19},{19,3},{4,20},{20... | collective-permute-start | bytes 4915208 | tf_op jit(solution)/shard_map/ppermute | solution.py:82
  304.5 56.8 %collective-permute-start.26 = (s16[400,1024]{1,0:T(8,128)(2,1)}, s16[400,1024]{1,0:T(8,128)(2,1)}, u32[]{:S(2)}, u32[]{:S(2)}) collective-permute-start(s16[400,1024]{1,0:T(8,128)(2,1)} %get-tuple-element.164), channel_id=1, source_target_pairs={{0,16},{16,0},{1,17},{17,1},{2,18},{18,2},{3,19},{19,3},{4,20},{20... | collective-permute-start | bytes 2457608 | tf_op jit(solution)/shard_map/ppermute | solution.py:82
  318.3 43.0 %collective-permute-start.25 = (s16[400,2048]{1,0:T(8,128)(2,1)}, s16[400,2048]{1,0:T(8,128)(2,1)}, u32[]{:S(2)}, u32[]{:S(2)}) collective-permute-start(s16[400,2048]{1,0:T(8,128)(2,1)} %get-tuple-element.163), channel_id=1, source_target_pairs={{0,16},{16,0},{1,17},{17,1},{2,18},{18,2},{3,19},{19,3},{4,20},{20... | collective-permute-start | bytes 4915208 | tf_op jit(solution)/shard_map/ppermute | solution.py:82
  337.4 40.6 %all-to-all-start.6 = ((s16[4,112,3072]{2,1,0:T(8,128)(2,1)}), s16[4,112,3072]{2,1,0:T(8,128)(2,1)}, u32[]{:S(2)}, u32[]{:S(2)}) async-start(s16[4,112,3072]{2,1,0:T(8,128)(2,1)} %send.7), calls=%async_computation.6 | async-start | bytes 5505024 | tf_op jit(solution)/shard_map/all_to_all | solution.py:59
  368.9 63.2 %collective-permute-start.27 = (s16[112,3072]{1,0:T(8,128)(2,1)}, s16[112,3072]{1,0:T(8,128)(2,1)}, u32[]{:S(2)}, u32[]{:S(2)}) collective-permute-start(s16[112,3072]{1,0:T(8,128)(2,1)} %get-tuple-element.168), channel_id=1, source_target_pairs={{0,4},{1,5},{2,6},{3,7},{4,0},{5,1},{6,2},{7,3},{8,12},{9,13},{10,... | collective-permute-start | bytes 2064392 | tf_op jit(solution)/shard_map/ppermute | solution.py:70
  375.6 59.1 %collective-permute-start.28 = (s16[112,3072]{1,0:T(8,128)(2,1)}, s16[112,3072]{1,0:T(8,128)(2,1)}, u32[]{:S(2)}, u32[]{:S(2)}) collective-permute-start(s16[112,3072]{1,0:T(8,128)(2,1)} %get-tuple-element.169), channel_id=1, source_target_pairs={{0,8},{1,9},{2,10},{3,11},{4,12},{5,13},{6,14},{7,15},{8,0},{9,1},... | collective-permute-start | bytes 2064392 | tf_op jit(solution)/shard_map/ppermute | solution.py:70
  376.1 66.7 %collective-permute-start.29 = (s16[112,3072]{1,0:T(8,128)(2,1)}, s16[112,3072]{1,0:T(8,128)(2,1)}, u32[]{:S(2)}, u32[]{:S(2)}) collective-permute-start(s16[112,3072]{1,0:T(8,128)(2,1)} %get-tuple-element.170), channel_id=1, source_target_pairs={{0,12},{1,13},{2,14},{3,15},{4,8},{5,9},{6,10},{7,11},{8,4},{9,5},... | collective-permute-start | bytes 2064392 | tf_op jit(solution)/shard_map/ppermute | solution.py:70
  399.7 51.6 %collective-permute-start.22 = (s16[400,1536]{1,0:T(8,128)(2,1)}, s16[400,1536]{1,0:T(8,128)(2,1)}, u32[]{:S(2)}, u32[]{:S(2)}) collective-permute-start(s16[400,1536]{1,0:T(8,128)(2,1)} %get-tuple-element.147), channel_id=1, source_target_pairs={{0,16},{16,0},{1,17},{17,1},{2,18},{18,2},{3,19},{19,3},{4,20},{20... | collective-permute-start | bytes 3686408 | tf_op jit(solution)/shard_map/ppermute | solution.py:82
  420.6 65.2 %all-to-all-start.7 = ((s16[4,528,768]{2,1,0:T(8,128)(2,1)}), s16[4,528,768]{2,1,0:T(8,128)(2,1)}, u32[]{:S(2)}, u32[]{:S(2)}) async-start(s16[4,528,768]{2,1,0:T(8,128)(2,1)} %copy-done.2), calls=%async_computation.7 | async-start | bytes 6488064 | tf_op jit(solution)/shard_map/all_to_all | solution.py:59
  442.9 70.8 %collective-permute-start.30 = (s16[40,3072]{1,0:T(8,128)(2,1)}, s16[40,3072]{1,0:T(8,128)(2,1)}, u32[]{:S(2)}, u32[]{:S(2)}) collective-permute-start(s16[40,3072]{1,0:T(8,128)(2,1)} %get-tuple-element.171), channel_id=1, source_target_pairs={{0,4},{1,5},{2,6},{3,7},{4,0},{5,1},{6,2},{7,3},{8,12},{9,13},{10,... | collective-permute-start | bytes 737288 | tf_op jit(solution)/shard_map/ppermute | solution.py:70
  449.0 64.7 %collective-permute-start.31 = (s16[40,3072]{1,0:T(8,128)(2,1)}, s16[40,3072]{1,0:T(8,128)(2,1)}, u32[]{:S(2)}, u32[]{:S(2)}) collective-permute-start(s16[40,3072]{1,0:T(8,128)(2,1)} %get-tuple-element.172), channel_id=1, source_target_pairs={{0,8},{1,9},{2,10},{3,11},{4,12},{5,13},{6,14},{7,15},{8,0},{9,1},... | collective-permute-start | bytes 737288 | tf_op jit(solution)/shard_map/ppermute | solution.py:70
  449.5 64.2 %collective-permute-start.32 = (s16[40,3072]{1,0:T(8,128)(2,1)}, s16[40,3072]{1,0:T(8,128)(2,1)}, u32[]{:S(2)}, u32[]{:S(2)}) collective-permute-start(s16[40,3072]{1,0:T(8,128)(2,1)} %get-tuple-element.173), channel_id=1, source_target_pairs={{0,12},{1,13},{2,14},{3,15},{4,8},{5,9},{6,10},{7,11},{8,4},{9,5},... | collective-permute-start | bytes 737288 | tf_op jit(solution)/shard_map/ppermute | solution.py:70
  495.9 77.5 %all-to-all-start.8 = ((s16[4,112,3584]{2,1,0:T(8,128)(2,1)}), s16[4,112,3584]{2,1,0:T(8,128)(2,1)}, u32[]{:S(2)}, u32[]{:S(2)}) async-start(s16[4,112,3584]{2,1,0:T(8,128)(2,1)} %send.8), calls=%async_computation.8 | async-start | bytes 6422528 | tf_op jit(solution)/shard_map/all_to_all | solution.py:59
  504.0 43.7 %collective-permute-start.24 = (s16[2,136,768]{2,1,0:T(8,128)(2,1)S(1)}, s16[2,136,768]{2,1,0:T(8,128)(2,1)S(1)}, u32[]{:S(2)}, u32[]{:S(2)}) collective-permute-start(s16[2,136,768]{2,1,0:T(8,128)(2,1)S(1)} %pad_add_fusion.4), channel_id=1, source_target_pairs={{1,0},{2,1},{3,2},{4,3},{5,4},{6,5},{7,6},{8,7},{9,8},{10,9},{11,1... | collective-permute-start | bytes 1253384 | tf_op jit(solution)/shard_map/ppermute | solution.py:401
  505.6 47.8 %collective-permute-start.23 = (s16[2,136,768]{2,1,0:T(8,128)(2,1)S(1)}, s16[2,136,768]{2,1,0:T(8,128)(2,1)S(1)}, u32[]{:S(2)}, u32[]{:S(2)}) collective-permute-start(s16[2,136,768]{2,1,0:T(8,128)(2,1)S(1)} %pad_add_fusion.3), channel_id=1, source_target_pairs={{0,1},{1,2},{2,3},{3,4},{4,5},{5,6},{6,7},{7,8},{8,9},{9,10},{10,1... | collective-permute-start | bytes 1253384 | tf_op jit(solution)/shard_map/ppermute | solution.py:401
  (141 other events, 2121.4 us)

commit v3 on v2

--- a/solution.py
+++ b/solution.py
@@ -244,7 +244,9 @@
     def one(value, other):
         blocks = [value[n] for n in range(value.shape[0])]
         if other is not None:
-            got = block_sum([other[...]], len(blocks), blocks[0].shape[0])
+            parts = [other[...]] if len(other.shape) == 2 else [other[g] for g in range(other.shape[0])]
+            each = len(blocks) // len(parts)
+            got = [q for part in parts for q in block_sum([part], each, blocks[0].shape[0])]
             blocks = [p + q for p, q in zip(blocks, got)]
         give(blocks, layout, place[0], outs, total)
 
@@ -393,6 +395,129 @@
             transcendentals=0,
         ),
     )(jnp.stack([bit]).astype(jnp.int32), x, y)
+
+
+def ffn_kernel(depth, scored, bits, *refs):
+    x, c, w_gate, w_up, w_out = refs[:5]
+    if scored:
+        score, router = refs[5:7]
+        rows, d_score, kept, sent = refs[7:11]
+    else:
+        rows, kept, sent = refs[5:8]
+    x_high, x_low, c_high, c_low, xt_high, xt_low, ct_high, ct_low = refs[-8:]
+    step = pl.program_id(0)
+
+    @pl.when(step == 0)
+    def _():
+        for value, high, low, turned_high, turned_low in (
+            (x, x_high, x_low, xt_high, xt_low),
+            (c, c_high, c_low, ct_high, ct_low),
+        ):
+            high[...], low[...] = split(value[...])
+            turned_high[...], turned_low[...] = split(value[...].T)
+        rows[...] = jnp.zeros_like(rows)
+        if scored:
+            d_score[...] = jnp.zeros_like(d_score)
+
+    gate = dot_nn(x_high[...], w_gate[...]) + dot_nn(x_low[...], w_gate[...])
+    up = dot_nn(x_high[...], w_up[...]) + dot_nn(x_low[...], w_up[...])
+    cot = dot_nn(c_high[...], w_out[...]) + dot_nn(c_low[...], w_out[...])
+    act, slope = gelu_both(gate)
+    mix = act * up
+    if scored:
+        d_score[...] += jnp.sum(cot * mix, axis=1, keepdims=True)
+        cot = cot * score[...]
+        mix = mix * score[...]
+    gate_high, gate_low = split(cot * up * slope)
+    up_high, up_low = split(cot * act)
+    mix_high, mix_low = split(mix)
+    rows[0] += (
+        dot_nt(gate_high, w_gate[...])
+        + dot_nt(gate_low, w_gate[...])
+        + dot_nt(up_high, w_up[...])
+        + dot_nt(up_low, w_up[...])
+    )
+    rows[1] += dot_nt(mix_high, w_out[...]) + dot_nt(mix_low, w_out[...])
+    if scored:
+
+        @pl.when(step == pl.num_programs(0) - 1)
+        def _():
+            into = d_score[...] * score[...] * (1.0 - score[...])
+            rows[0] += into * router[...]
+
+    half = xt_high.shape[0] // 2
+    for g, (left_high, left_low, high, low) in enumerate(
+        (
+            (xt_high, xt_low, gate_high, gate_low),
+            (xt_high, xt_low, up_high, up_low),
+            (ct_high, ct_low, mix_high, mix_low),
+        )
+    ):
+        for mine in (True, False):
+            which = bits[0] if mine else 1 - bits[0]
+            part = pl.ds(pl.multiple_of(which * half, half), half)
+            left = left_high[part, :]
+            value = dot_nn(left, high) + dot_nn(left_low[part, :], high) + dot_nn(left, low)
+            if mine:
+                kept[g] = value
+            else:
+                sent[g] = packed_blocks([value[n : n + depth] for n in range(0, half, depth)])
+
+
+def ffn_call(x, c, w_in, w_out, depth, bit, score=None, router=None):
+    count, width = x.shape
+    units = w_out.shape[1]
+    tile, half = 512, width // 2
+    tiles = units // tile
+    packed = half + power_rows(half // depth)
+    scored = score is not None
+    whole = pl.BlockSpec((count, width), lambda t, _: (0, 0))
+    column = pl.BlockSpec((count, 1), lambda t, _: (0, 0))
+    outs = [
+        jax.ShapeDtypeStruct((2, count, width), f32),
+        jax.ShapeDtypeStruct((count, 1), f32),
+        jax.ShapeDtypeStruct((3, half, units), f32),
+        jax.ShapeDtypeStruct((3, packed, units), jnp.int16),
+    ]
+    out_specs = [
+        pl.BlockSpec((2, count, width), lambda t, _: (0, 0, 0)),
+        column,
+        pl.BlockSpec((3, half, tile), lambda t, _: (0, 0, t)),
+        pl.BlockSpec((3, packed, tile), lambda t, _: (0, 0, t)),
+    ]
+    args = [x, c, w_in, w_in, w_out]
+    in_specs = [
+        whole,
+        whole,
+        pl.BlockSpec((width, tile), lambda t, _: (0, t)),
+        pl.BlockSpec((width, tile), lambda t, _: (0, t + tiles)),
+        pl.BlockSpec((width, tile), lambda t, _: (0, t)),
+    ]
+    if scored:
+        args += [score, router]
+        in_specs += [column, pl.BlockSpec((1, width), lambda t, _: (0, 0))]
+    else:
+        outs.pop(1)
+        out_specs.pop(1)
+    return pl.pallas_call(
+        lambda *refs: ffn_kernel(depth, scored, *refs),
+        name="ffn",
+        grid_spec=pltpu.PrefetchScalarGridSpec(
+            num_scalar_prefetch=1,
+            grid=(tiles,),
+            in_specs=in_specs,
+            out_specs=out_specs,
+            scratch_shapes=[pltpu.VMEM((count, width), bf16)] * 4
+            + [pltpu.VMEM((width, count), bf16)] * 4,
+        ),
+        out_shape=outs,
+        compiler_params=pltpu.CompilerParams(vmem_limit_bytes=56 * 2**20),
+        cost_estimate=pl.CostEstimate(
+            flops=42 * count * width * units,
+            bytes_accessed=24 * count * width + 24 * width * units,
+            transcendentals=count * units,
+        ),
+    )(jnp.stack([bit]).astype(jnp.int32), *args)
 
 
 def shifted(value, by):
@@ -685,8 +810,8 @@
         return flat(value)
 
     class Sum:
-        def __init__(self, pieces, depth, first):
-            self.depth, self.first, self.value = depth, first, None
+        def __init__(self, pieces, depth, first, split_already=None):
+            self.depth, self.first, self.value, self.groups = depth, first, None, 1
             if not tiled:
                 value = joined(
                     *[p if not isinstance(p, tuple) else product("rd,re->de", *p) for p in pieces]
@@ -700,6 +825,11 @@
                 self.value = value.reshape(far, GROUP, device_rows, -1)
                 return
             kept, sent = [], []
+            if split_already is not None:
+                mine, other = split_already
+                self.groups = mine.shape[0]
+                kept.append(mine.reshape(-1, depth, mine.shape[-1]))
+                sent.append(other)
             for p in pieces:
                 if isinstance(p, tuple):
                     mine, other = grad_split(*p, core, depth)
@@ -715,10 +845,14 @@
                 kept.append(mine.reshape(-1, depth, mine.shape[-1]))
                 sent.append(other)
             got = links.flip(sent, batch_bits[0])
+            groups = range(self.groups)
             if first == "near":
-                layout = [[(f * GROUP + p, 0, depth) for f in range(far)] for p in range(GROUP)]
+                layout = [
+                    [((g * far + f) * GROUP + p, 0, depth) for f in range(far) for g in groups]
+                    for p in range(GROUP)
+                ]
             else:
-                layout = [[(f, 0, depth)] for f in range(far)]
+                layout = [[(g * far + f, 0, depth) for g in groups] for f in range(far)]
             self.sent = send_form(kept, got, layout, first == "far")
 
         def near(self):
@@ -730,8 +864,11 @@
                 return
             self.value = links.near(self.sent)
             if self.first == "near":
-                layout = [[(f, 0, self.depth)] for f in range(far)]
-                self.sent = arrived(self.value, far, self.depth, layout, True)
+                groups = self.groups
+                layout = [
+                    [(f * groups + g, 0, self.depth) for g in range(groups)] for f in range(far)
+                ]
+                self.sent = arrived(self.value, far * groups, self.depth, layout, True)
 
         def far(self):
             if not tiled:
@@ -744,20 +881,28 @@
             self.value = links.far(self.sent)
             if self.first == "far":
                 layout = [
-                    [(0, p * device_rows, (p + 1) * device_rows)] for p in range(GROUP)
+                    [
+                        (g, p * device_rows, (p + 1) * device_rows)
+                        for g in range(self.groups)
+                    ]
+                    for p in range(GROUP)
                 ]
-                self.sent = arrived(self.value, 1, self.depth, layout)
+                self.sent = arrived(self.value, self.groups, self.depth, layout)
 
         def result(self):
             if not tiled:
                 return self.value
+            groups = self.groups
             if self.first == "near":
-                return arrived(self.value, 1, self.depth)
+                value = arrived(self.value, groups, self.depth)
+                return value.reshape(groups, self.depth, -1) if groups > 1 else value
             value = self.value.astype(f32)
-            power = value[:, device_rows : device_rows + 1]
-            return value[:, :device_rows] * jnp.exp2(power - 15.0)
+            power = value[:, groups * device_rows : groups * (device_rows + 1), None]
+            value = value[:, : groups * device_rows]
+            return value.reshape(GROUP, groups, device_rows, -1) * jnp.exp2(power - 15.0)
 
     n_one, r_one = unit_rms(tokens)
+
     def picker(route_row):
         return local_slots(route_row, row_begin, rows, capacity)
 
@@ -851,33 +996,45 @@
     ffn_own = product("sct,std->scd", ffn_pick, second)
     routed = unpack_rows(links.near_share(pack_rows(jnp.stack([ffn_own, cot_own]))))
     ffn_rows, cot_rows = (flat(routed[:, i]) for i in range(2))
-    gate_up = product("std,de->ste", second, ff_in)
-    gate, up = gate_up[..., :FL], gate_up[..., FL:]
-    gate_act, gate_slope = gelu_both(gate)
-    light_act = gate_act * up
-    light_ff = product("stf,df->std", light_act, ff_out)
-    d_act = product("std,df->stf", cotangent, ff_out)
-    d_gate_up = jnp.concatenate([d_act * up * gate_slope, d_act * gate_act], axis=-1)
-    d_second = product("ste,de->std", d_gate_up, ff_in)
-    d_ff = Sum(
-        [(flat(cotangent), flat(light_act)), (flat(second), flat(d_gate_up))], device_rows, "near"
-    )
-
     ffn_score = jax.nn.sigmoid(jnp.sum(ffn_rows * router_f, axis=-1, keepdims=True))
-    big_gate_up = product("rd,de->re", ffn_rows, big_in)
-    big_gate, big_up = big_gate_up[:, :units], big_gate_up[:, units:]
-    big_act, big_slope = gelu_both(big_gate)
-    big_mix = big_act * big_up
-    cot_mix = product("rd,df->rf", cot_rows, big_out)
-    d_score = jnp.sum(cot_mix * big_mix, axis=-1, keepdims=True)
-    d_score_in = d_score * ffn_score * (1.0 - ffn_score)
-    d_mix = cot_mix * ffn_score
-    d_big = jnp.concatenate([d_mix * big_up * big_slope, d_mix * big_act], axis=-1)
-    d_ffn_rows = product("re,de->rd", d_big, big_in) + d_score_in * router_f
-    d_router_f = jnp.sum(d_score_in * ffn_rows, axis=0)
-
-    big_rows = product("rf,df->rd", big_mix, big_out) * ffn_score
-    both = jnp.stack([d_ffn_rows, big_rows]).reshape(-1, capacity, width)
+
+    def plain_ffn(x, c, w_in, w_out, score):
+        count = w_out.shape[1]
+        gate_up = product("rd,de->re", x, w_in)
+        act, slope = gelu_both(gate_up[:, :count])
+        up = gate_up[:, count:]
+        cot = product("rd,df->rf", c, w_out)
+        d_score = jnp.sum(cot * act * up, axis=1, keepdims=True)
+        mix = act * up * score
+        d_in = jnp.concatenate([cot * score * up * slope, cot * score * act], axis=1)
+        d_x = product("re,de->rd", d_in, w_in) + d_score * score * (1.0 - score) * router_f
+        y = product("rf,df->rd", mix, w_out)
+        return jnp.stack([d_x, y]), d_score, [(x, d_in), (c, mix)]
+
+    if tiled:
+        light_rows, *grads = ffn_call(
+            flat(second), flat(cotangent), ff_in, ff_out, device_rows, core
+        )
+        d_ff = Sum([], device_rows, "near", grads)
+        both, d_score, *grads = ffn_call(
+            ffn_rows,
+            cot_rows,
+            big_in,
+            big_out,
+            GROUP * device_rows,
+            core,
+            ffn_score,
+            router_f[None],
+        )
+        d_big_all = Sum([], GROUP * device_rows, "far", grads)
+    else:
+        light_rows, _, pairs = plain_ffn(flat(second), flat(cotangent), ff_in, ff_out, 1.0)
+        d_ff = Sum(pairs, device_rows, "near")
+        both, d_score, pairs = plain_ffn(ffn_rows, cot_rows, big_in, big_out, ffn_score)
+        d_big_all = Sum(pairs, GROUP * device_rows, "far")
+    d_second, light_ff = light_rows.reshape(2, seqs, rows, width)
+    d_router_f = jnp.sum(d_score * ffn_score * (1.0 - ffn_score) * ffn_rows, axis=0)
+    both = both.reshape(-1, capacity, width)
     layout = [
         [((m * GROUP + p) * seqs + i, 0, capacity) for m in range(2) for i in range(seqs)]
         for p in range(GROUP)
@@ -886,9 +1043,6 @@
         links.near(send_form([both], [None], layout, False)), 2 * seqs, capacity
     ).reshape(2, seqs, capacity, width)
     ffn_own, out_own = back[0], back[1]
-    d_big_all = Sum(
-        [(ffn_rows, d_big), (cot_rows, big_mix * ffn_score)], GROUP * device_rows, "far"
-    )
     d_big_all.far()
     d_ff.near()
 
@@ -968,7 +1122,7 @@
         from_next, ((0, 0), (rows - W, 0), (0, 0))
     )
     vectors = jnp.stack([d_gain_one, d_gain_two, d_router_q, d_router_k, d_router_f])
-    vectors = jnp.pad(vectors, ((0, 128 - 5), (0, 0))).T
+    vectors = jnp.pad(vectors, ((0, 256 - 5), (0, 0))).T
     last = Sum(
         [(flat(normed), flat(d_lq)), (flat(normed_ext), flat(d_lkv)), vectors],
         device_rows,
@@ -983,13 +1137,19 @@
     d_big_all = d_big_all.result()
     vectors = last[:, 3 * IL :]
 
-    def spread(value):
-        return jnp.swapaxes(value, 0, 1).reshape(value.shape[1], -1)
-
-    d_heavy_ff_in = joined(
-        spread(d_big_all[..., :units]), spread(d_big_all[..., units : 2 * units])
-    )
-    d_heavy_ff_out = spread(d_big_all[..., 2 * units :])
+    if tiled:
+        big_gate, big_up, d_heavy_ff_out = (
+            jnp.swapaxes(d_big_all[:, g], 0, 1).reshape(device_rows, -1) for g in range(3)
+        )
+        d_heavy_ff_in = joined(big_gate, big_up)
+        d_ff_in, d_ff_out = joined(d_ff[0], d_ff[1]), d_ff[2]
+    else:
+        turned = jnp.swapaxes(d_big_all, 0, 1).reshape(device_rows, GROUP, 3, units)
+        big_gate, big_up, d_heavy_ff_out = (
+            turned[:, :, g].reshape(device_rows, -1) for g in range(3)
+        )
+        d_heavy_ff_in = joined(big_gate, big_up)
+        d_ff_in, d_ff_out = d_ff[:, : 2 * FL], d_ff[:, 2 * FL :]
 
     d_normed = (
         d_own
@@ -1006,8 +1166,8 @@
         d_mid[:, :IL],
         d_mid[:, IL + IH :],
         d_mid[:, IL : IL + IH],
-        d_ff[:, FL:],
-        d_ff[:, :FL],
+        d_ff_in,
+        d_ff_out,
         d_heavy_ff_in,
         d_heavy_ff_out,
         vectors[:, :2],

time: 653 us -> 634 us (0.971)
  matrix products: 107 us -> 75.8 us
  Pallas kernels: 195 us -> 209 us
    pallas_call x0 -> x2, Pallas kernels: none -> 51.1 us  [ffn_call(): pl.pallas_call(lambda *refs: ffn_kernel(depth, scored, *refs), name='ffn'...]
    dot_general x31 -> x23, matrix products: 107 us -> 75.8 us  [product(): jnp.einsum(formula, left_side.astype(f32), right_side.astype(f32), precis...]
    pallas_call x10 -> x6, Pallas kernels: 57.7 us -> 31.8 us  [grad_split(): pl.pallas_call(lambda *refs: grad_kernel(depth, *refs), name='grad', grid...]
    ppermute x4, waiting for transfers between devices: 17.2 us -> 9.6 us  [shifted(): return unpack_rows(lax.ppermute(pack_rows(value), 'seq', pairs))]
    concatenate x2 -> x0, other arithmetic: 7.53 us -> none  [the longest x1 4.72 us: on_device(): jnp.concatenate([d_mix * big_up * big_slope, d_mix * big_act], axis=-1)]
    pallas_call x10, Pallas kernels: 28.6 us -> 21.4 us  [arrived(): pl.pallas_call(lambda *refs: arrived_kernel(sources, count, depth, layout...]
    unnamed x235 -> x202, local copies, waits for them, and re-layouts: 34.2 us -> 27.4 us
  transfers between devices with their start and end apart: 56 -> 54, of which waited for: 17 -> 17; matrix products, arithmetic and copies ran while one was open for 29% -> 26% of each run, Pallas kernels for 25% -> 28%
where the time goes in v3:
time: 634 us; the launch traced here: 623 us
  Pallas kernels  209 us (33%)
  starting transfers between devices  118 us (19%)
  waiting for transfers between devices  95.1 us (15%)
  matrix products  75.8 us (12%)
  local copies, waits for them, and re-layouts  70.5 us (11%)
  other arithmetic  51.8 us (8%)
    dot_general x23, matrix products, product(): jnp.einsum(formula, left_side.astype(f32), right_side.astype(f32), precis...  75.8 us
    ppermute x27, starting transfers between devices, far(): lax.ppermute(v, 'seq', [(i, i ^ GROUP * j) for i in range(devices)])  56.3 us
    ppermute x27, waiting for transfers between devices, far(): lax.ppermute(v, 'seq', [(i, i ^ GROUP * j) for i in range(devices)])  51.2 us
    pallas_call x2, Pallas kernels, ffn_call(): pl.pallas_call(lambda *refs: ffn_kernel(depth, scored, *refs), name='ffn'...  51.1 us
    all_to_all x11, starting transfers between devices, near(): lax.all_to_all(value, 'seq', 0, 0, axis_index_groups=groups, tiled=True)  48.5 us
    all_to_all x11, waiting for transfers between devices, near(): lax.all_to_all(value, 'seq', 0, 0, axis_index_groups=groups, tiled=True)  32.9 us
    pallas_call x2, Pallas kernels, light_call(): pl.pallas_call(kernel, name=kernel.__name__, grid_spec=pltpu.PrefetchScal...  32.4 us
    pallas_call x6, Pallas kernels, send_form(): pl.pallas_call(lambda *refs: send_kernel(spans, layout, received, far, *r...  32.1 us
  transfers between devices with their start and end apart: 54, of which 17 were waited for; matrix products, arithmetic and copies ran while one was open for 26% of the time, Pallas kernels for 28%

profile of v3, /device:TPU:0, one launch (start us, length us, event | category | flops | bytes accessed | tf_op | source)
XLA Modules:
  0.0 622.9 jit_solution(7919313445188976785)
XLA Ops:
  46.3 11.3 %collective-permute-done.4.refs_2_ = s16[2,72,768]{2,1,0:T(8,128)(2,1)S(1)} collective-permute-done((s16[2,72,768]{2,1,0:T(8,128)(2,1)S(1)}, s16[2,72,768]{2,1,0:T(8,128)(2,1)S(1)}, u32[]{:S(2)}, u32[]{:S(2)}) %collective-permute-start.4) | collective-permute-done | bytes 221216 | tf_op jit(solution)/shard_map/ppermute | solution.py:70
  58.7 11.0 %all-to-all-done.value = bf16[4,4,24,3968]{3,2,1,0:T(8,128)(2,1)S(1)} async-done(((bf16[4,4,24,3968]{3,2,1,0:T(8,128)(2,1)}), bf16[4,4,24,3968]{3,2,1,0:T(8,128)(2,1)S(1)}, u32[]{:S(2)}, u32[]{:S(2)}) %all-to-all-start) | async-done | bytes 3047456 | tf_op jit(solution)/shard_map/all_to_all | solution.py:59
  79.1 7.2 %all-to-all-done.1.refs_0_ = bf16[4,24,3072]{2,1,0:T(8,128)(2,1)} async-done(((bf16[4,24,3072]{2,1,0:T(8,128)(2,1)}), bf16[4,24,3072]{2,1,0:T(8,128)(2,1)}, u32[]{:S(2)}, u32[]{:S(2)}) %all-to-all-start.1) | async-done | bytes 589856 | tf_op jit(solution)/shard_map/all_to_all | solution.py:59
  105.5 10.6 %collective-permute-done.10.refs_2_ = bf16[24,4352]{1,0:T(8,128)(2,1)S(1)} collective-permute-done((bf16[24,4352]{1,0:T(8,128)(2,1)S(1)}, bf16[24,4352]{1,0:T(8,128)(2,1)S(1)}, u32[]{:S(2)}, u32[]{:S(2)}) %collective-permute-start.10) | collective-permute-done | bytes 208928 | tf_op jit(solution)/shard_map/ppermute | solution.py:70
  145.1 9.0 %light_forward_kernel.1 = f32[2,256,512]{2,1,0:T(8,128)S(1)} custom-call(s32[4]{0:T(128)S(1)} %pad_add_fusion.8.places, f32[2,256,512]{2,1,0:T(8,128)S(1)} %fusion.36.q, f32[2,512,1024]{2,1,0:T(8,128)} %fusion.3.kv), custom_call_target="tpu_custom_call" | custom-call | flops 8589934592 | bytes 8388608 | tf_op jit(solution)/shard_map/light_forward_kernel/pallas_call | solution.py:705
  154.1 8.1 %collective-permute-done.14.refs_2_ = bf16[4,24,3072]{2,1,0:T(8,128)(2,1)} collective-permute-done((bf16[4,24,3072]{2,1,0:T(8,128)(2,1)}, bf16[4,24,3072]{2,1,0:T(8,128)(2,1)}, u32[]{:S(2)}, u32[]{:S(2)}) %collective-permute-start.14) | collective-permute-done | bytes 589856 | tf_op jit(solution)/shard_map/ppermute | solution.py:70
  183.9 6.4 %multiply_reduce_fusion.4 = (f32[2,512]{1,0:T(2,128)S(1)}, f32[2,512,768]{2,1,0:T(8,128)S(1)}, f32[2,512,768]{2,1,0:T(8,128)}) fusion(f32[768]{0:T(1024)S(1)} %get-tuple-element.281, f32[768]{0:T(1024)S(1)} %get-tuple-element.282, f32[2,1024,768]{2,1,0:T(8,128)S(1)} %bitcast.204, s32[2,512]{1,0:T(2,128)S(1)} %subtract_add_fusion), kind=kOutput, calls=%fused_computation.16 | convolution fusion | flops 4835245056 | bytes 12597248 | tf_op jit(solution)/shard_map/skp,spd->skd/dot_general | solution.py:530
  192.0 6.9 %fusion.8 = f32[2,512,1536]{2,1,0:T(8,128)S(1)} fusion(f32[2,512,768]{2,1,0:T(8,128)S(1)} %get-tuple-element.296, bf16[768,3968]{1,0:T(8,128)(2,1)} %bitcast.180), kind=kOutput, calls=%fused_computation.25 | convolution fusion | flops 7247757312 | bytes 11796480 | tf_op jit(solution)/shard_map/skd,de->ske/dot_general | solution.py:530
  205.1 9.0 %heavy_forward_kernel.1 = f32[2,64,768]{2,1,0:T(8,128)S(1)} custom-call(s32[4]{0:T(128)S(1)} %pad_add_fusion.8.places, s32[2,512,1]{2,1,0:T(8,128)S(1)} %copy-done.25, s32[2,1,128]{2,1,0:T(1,128)S(1)} %bitcast.202, f32[2,64,768]{2,1,0:T(8,128)S(1)} %copy-done.30, f32[2,512,1536]{2,1,0:T(8,128)} %pad_maximum_fusion.kv), custom_call_target="tpu_custom_call" | custom-call | flops 8589934592 | bytes 8388608 | tf_op jit(solution)/shard_map/heavy_forward_kernel/pallas_call | solution.py:751
  238.0 24.8 %ffn.2 = (f32[2,512,768]{2,1,0:T(8,128)}, f32[3,384,1024]{2,1,0:T(8,128)}, s16[3,400,1024]{2,1,0:T(8,128)(2,1)}) custom-call(s32[1]{0:T(128)} %bitcast.1.bit.refs_0_, f32[512,768]{1,0:T(8,128)} %bitcast.210, f32[512,768]{1,0:T(8,128)} %bitcast.207, bf16[768,2048]{1,0:T(8,128)(2,1)} %slice.264.refs_3_.refs_4_, bf16[768,2048]{1,0:T(8,128)(2,1)} %slice.264.refs_3_.refs_4_, ...), custom_call_target="tpu_custom_call" | custom-call | flops 16911433728 | bytes 28311552 | tf_op jit(solution)/shard_map/ffn/pallas_call | solution.py:502
  269.4 26.4 %ffn.3 = (f32[2,512,768]{2,1,0:T(8,128)}, f32[512,1]{1,0:T(8,128)}, f32[3,384,1024]{2,1,0:T(8,128)}, s16[3,400,1024]{2,1,0:T(8,128)(2,1)}) custom-call(s32[1]{0:T(128)} %bitcast.1.bit.refs_0_, f32[512,768]{1,0:T(8,128)} %bitcast.225, f32[512,768]{1,0:T(8,128)} %bitcast.224, bf16[768,2048]{1,0:T(8,128)(2,1)} %slice.270.refs_3_.refs_4_, ...), custom_call_target="tpu_custom_call" | custom-call | flops 16911433728 | bytes 28311552 | tf_op jit(solution)/shard_map/ffn/pallas_call | solution.py:502
  315.4 9.0 %all-to-all-done.5.refs_1_ = s16[4,272,768]{2,1,0:T(8,128)(2,1)S(1)} async-done(((s16[4,272,768]{2,1,0:T(8,128)(2,1)}), s16[4,272,768]{2,1,0:T(8,128)(2,1)S(1)}, u32[]{:S(2)}, u32[]{:S(2)}) %all-to-all-start.5) | async-done | bytes 1671200 | tf_op jit(solution)/shard_map/all_to_all | solution.py:59
  342.3 15.4 %heavy_backward_kernel.1 = (f32[2,64,768]{2,1,0:T(8,128)S(1)}, f32[2,512,1536]{2,1,0:T(8,128)}) custom-call(s32[4]{0:T(128)S(1)} %pad_add_fusion.8.places, s32[2,512,1]{2,1,0:T(8,128)S(1)} %copy-done.26, s32[2,1,128]{2,1,0:T(1,128)S(1)} %bitcast.203, f32[2,64,768]{2,1,0:T(8,128)S(1)} %copy-done.31, f32[2,512,1536]{2,1,0:T(8,128)} %pad_maximum_fusion.kv, ...), custom_call_target="tpu_custom_call" | custom-call | flops 17179869184 | bytes 8388608 | tf_op jit(solution)/shard_map/heavy_backward_kernel/pallas_call | solution.py:751
  365.0 7.0 %collective-permute-start.25 = (s16[304,1024]{1,0:T(8,128)(2,1)}, s16[304,1024]{1,0:T(8,128)(2,1)}, u32[]{:S(2)}, u32[]{:S(2)}) collective-permute-start(s16[304,1024]{1,0:T(8,128)(2,1)} %get-tuple-element.165), channel_id=1, source_target_pairs={{0,4},{1,5},{2,6},{3,7},{4,0},{5,1},{6,2},{7,3},{8,12},{9,13},{10,... | collective-permute-start | bytes 1867784 | tf_op jit(solution)/shard_map/ppermute | solution.py:70
  383.2 13.3 %grad.9 = (f32[384,1536]{1,0:T(8,128)S(1)}, s16[400,1536]{1,0:T(8,128)(2,1)}) custom-call(s32[1]{0:T(128)} %bitcast.1.bit.refs_0_, f32[1024,768]{1,0:T(8,128)} %bitcast.216, f32[1024,1536]{1,0:T(8,128)} %bitcast.206), custom_call_target="tpu_custom_call" | custom-call | flops 7247757312 | bytes 12976128 | tf_op jit(solution)/shard_map/grad/pallas_call | solution.py:371
  396.5 9.5 %multiply_reduce_fusion = (f32[768]{0:T(1024)S(1)}, f32[768]{0:T(1024)}, f32[2,512,768]{2,1,0:T(8,128)S(1)}) fusion(f32[2,512,768]{2,1,0:T(8,128)S(1)} %copy-done.62, f32[2,512]{1,0:T(2,128)S(1)} %subtract_multiply_fusion, f32[2,512,768]{2,1,0:T(8,128)} %get-tuple-element.344, f32[768]{0:T(1024)S(1)} %get-tuple-element.281, ...), kind=kOutput, calls=%fused_computation.11 | convolution fusion | flops 7254047232 | bytes 18101248 | tf_op jit(solution)/shard_map/ske,de->skd/dot_general | solution.py:530
  443.2 10.2 %send.8 = s16[4,112,3584]{2,1,0:T(8,128)(2,1)} custom-call(s32[1]{0:T(128)} %bitcast.2.place.refs_0_, f32[16,24,512]{2,1,0:T(8,128)S(1)} %bitcast.198, f32[16,24,768]{2,1,0:T(8,128)S(1)} %bitcast.194, f32[16,24,768]{2,1,0:T(8,128)S(1)} %bitcast.195, f32[16,24,1536]{2,1,0:T(8,128)} %bitcast.190, s16[400,512]{1,0:T(8,128)(2,1)S(1)} %collective-permute-done.18.refs_5_, ...), custom_call_target="tpu_custom_call" | custom-call | flops 27525120 | bytes 11010048 | tf_op jit(solution)/shard_map/send/pallas_call | solution.py:279
  453.5 23.4 %light_backward_kernel.1 = (f32[2,256,512]{2,1,0:T(8,128)S(1)}, f32[2,512,1024]{2,1,0:T(8,128)}) custom-call(s32[4]{0:T(128)S(1)} %pad_add_fusion.8.places, f32[2,256,512]{2,1,0:T(8,128)S(1)} %copy-done.16, f32[2,512,1024]{2,1,0:T(8,128)} %fusion.3.kv, f32[2,256,512]{2,1,0:T(8,128)S(1)} %copy-done.17), custom_call_target="tpu_custom_call" | custom-call | flops 17179869184 | bytes 8388608 | tf_op jit(solution)/shard_map/light_backward_kernel/pallas_call | solution.py:705
  482.8 8.6 %multiply_reduce_fusion.2 = (f32[768]{0:T(1024)S(1)}, f32[2,512,768]{2,1,0:T(8,128)}, f32[2,512,768]{2,1,0:T(8,128)S(1)}) fusion(f32[2,512]{1,0:T(2,128)S(1)} %copy-done.77, f32[2,128,768]{2,1,0:T(8,128)S(1)} %copy-done.51, f32[2,256,768]{2,1,0:T(8,128)} %param.16, f32[2,128,768]{2,1,0:T(8,128)} %copy-done.52, f32[2,512,1024]{2,1,0:T(8,128)} %get-tuple-element.152, ...), kind=kOutput, calls=%fused_computation.13 | convolution fusion | flops 4835769344 | bytes 15211520 | tf_op jit(solution)/shard_map/ste,de->std/dot_general | solution.py:530
  510.0 9.2 %grad.11 = (f32[384,1024]{1,0:T(8,128)S(1)}, s16[400,1024]{1,0:T(8,128)(2,1)}) custom-call(s32[1]{0:T(128)} %bitcast.1.bit.refs_0_, f32[1024,768]{1,0:T(8,128)S(1)} %fusion.2.refs_1_, f32[1024,1024]{1,0:T(8,128)} %bitcast.214), custom_call_target="tpu_custom_call" | custom-call | flops 4831838208 | bytes 9699328 | tf_op jit(solution)/shard_map/grad/pallas_call | solution.py:371
  527.8 7.3 %collective-permute-done.22 = s16[2,136,768]{2,1,0:T(8,128)(2,1)S(1)} collective-permute-done((s16[2,136,768]{2,1,0:T(8,128)(2,1)}, s16[2,136,768]{2,1,0:T(8,128)(2,1)S(1)}, u32[]{:S(2)}, u32[]{:S(2)}) %collective-permute-start.22) | collective-permute-done | bytes 417824 | tf_op jit(solution)/shard_map/ppermute | solution.py:526
  568.5 5.9 arrived.15
  589.2 8.5 %collective-permute-done.38.refs_3_ = s16[40,3584]{1,0:T(8,128)(2,1)} collective-permute-done((s16[40,3584]{1,0:T(8,128)(2,1)}, s16[40,3584]{1,0:T(8,128)(2,1)}, u32[]{:S(2)}, u32[]{:S(2)}) %collective-permute-start.38) | collective-permute-done | bytes 286752 | tf_op jit(solution)/shard_map/ppermute | solution.py:70
  597.7 5.9 collective-permute-start.40
  (487 shorter events, 356.4 us)
Async XLA Ops:
  13.1 89.6 %collective-permute-start.8 = (s16[2,136,768]{2,1,0:T(8,128)(2,1)}, s16[2,136,768]{2,1,0:T(8,128)(2,1)}, u32[]{:S(2)}, u32[]{:S(2)}) collective-permute-start(s16[2,136,768]{2,1,0:T(8,128)(2,1)} %pad_add_fusion.2), channel_id=1, source_target_pairs={{1,0},{2,1},{3,2},{4,3},{5,4},{6,5},{7,6},{8,7},{9,8},{10,9},{11,1... | collective-permute-start | bytes 1253384 | tf_op jit(solution)/shard_map/ppermute | solution.py:526
  15.2 88.6 %collective-permute-start.7 = (s16[2,136,768]{2,1,0:T(8,128)(2,1)}, s16[2,136,768]{2,1,0:T(8,128)(2,1)}, u32[]{:S(2)}, u32[]{:S(2)}) collective-permute-start(s16[2,136,768]{2,1,0:T(8,128)(2,1)} %pad_add_fusion.1), channel_id=1, source_target_pairs={{0,1},{1,2},{2,3},{3,4},{4,5},{5,6},{6,7},{7,8},{8,9},{9,10},{10,1... | collective-permute-start | bytes 1253384 | tf_op jit(solution)/shard_map/ppermute | solution.py:526
  25.2 44.5 %all-to-all-start = ((bf16[4,4,24,3968]{3,2,1,0:T(8,128)(2,1)}), bf16[4,4,24,3968]{3,2,1,0:T(8,128)(2,1)S(1)}, u32[]{:S(2)}, u32[]{:S(2)}) async-start(bf16[4,4,24,3968]{3,2,1,0:T(8,128)(2,1)} %broadcast_in_dim.51), calls=%async_computation | async-start | bytes 6094848 | tf_op jit(solution)/shard_map/all_to_all | solution.py:59
  69.6 52.4 %collective-permute-start.6 = (bf16[4,4,24,3968]{3,2,1,0:T(8,128)(2,1)S(1)}, bf16[4,4,24,3968]{3,2,1,0:T(8,128)(2,1)}, u32[]{:S(2)}, u32[]{:S(2)}) collective-permute-start(bf16[4,4,24,3968]{3,2,1,0:T(8,128)(2,1)S(1)} %all-to-all-done.value), channel_id=1, source_target_pairs={{0,16},{16,0},{1,17},{17,1},{2,18},{18,2},{3,19},{19,3},{4,20},{20... | collective-permute-start | bytes 9142280 | tf_op jit(solution)/shard_map/ppermute | solution.py:82
  89.4 47.1 %all-to-all-start.2 = ((s16[4,4,2,72,768]{4,3,1,2,0:T(8,128)(2,1)}), s16[4,4,2,72,768]{4,3,1,2,0:T(8,128)(2,1)}, u32[]{:S(2)}, u32[]{:S(2)}) async-start(s16[4,4,2,72,768]{4,3,1,2,0:T(8,128)(2,1)} %broadcast_in_dim.59), calls=%async_computation.2 | async-start | bytes 7077888 | tf_op jit(solution)/shard_map/all_to_all | solution.py:59
  119.5 42.8 %collective-permute-start.14 = (bf16[4,24,3072]{2,1,0:T(8,128)(2,1)}, bf16[4,24,3072]{2,1,0:T(8,128)(2,1)}, u32[]{:S(2)}, u32[]{:S(2)}) collective-permute-start(bf16[4,24,3072]{2,1,0:T(8,128)(2,1)} %all-to-all-done.1.refs_0_), channel_id=1, source_target_pairs={{0,8},{1,9},{2,10},{3,11},{4,12},{5,13},{6,14},{7,15},{8,0},{9,1},... | collective-permute-start | bytes 1769480 | tf_op jit(solution)/shard_map/ppermute | solution.py:70
  120.6 41.7 %collective-permute-start.15 = (bf16[4,24,3072]{2,1,0:T(8,128)(2,1)}, bf16[4,24,3072]{2,1,0:T(8,128)(2,1)}, u32[]{:S(2)}, u32[]{:S(2)}) collective-permute-start(bf16[4,24,3072]{2,1,0:T(8,128)(2,1)} %all-to-all-done.1.refs_0_), channel_id=1, source_target_pairs={{0,12},{1,13},{2,14},{3,15},{4,8},{5,9},{6,10},{7,11},{8,4},{9,5},... | collective-permute-start | bytes 1769480 | tf_op jit(solution)/shard_map/ppermute | solution.py:70
  138.5 42.1 %all-to-all-start.3 = ((bf16[4,4,24,4352]{3,2,1,0:T(8,128)(2,1)}), bf16[4,4,24,4352]{3,2,1,0:T(8,128)(2,1)S(1)}, u32[]{:S(2)}, u32[]{:S(2)}) async-start(bf16[4,4,24,4352]{3,2,1,0:T(8,128)(2,1)} %broadcast_in_dim.58), calls=%async_computation.3 | async-start | bytes 6684672 | tf_op jit(solution)/shard_map/all_to_all | solution.py:59
  165.8 48.3 %collective-permute-start.16 = (bf16[4,4,24,3072]{3,2,1,0:T(8,128)(2,1)}, bf16[4,4,24,3072]{3,2,1,0:T(8,128)(2,1)}, u32[]{:S(2)}, u32[]{:S(2)}) collective-permute-start(bf16[4,4,24,3072]{3,2,1,0:T(8,128)(2,1)} %stack.40.value), channel_id=1, source_target_pairs={{0,16},{16,0},{1,17},{17,1},{2,18},{18,2},{3,19},{19,3},{4,20},{20... | collective-permute-start | bytes 7077896 | tf_op jit(solution)/shard_map/ppermute | solution.py:82
  180.5 42.2 %collective-permute-start.12 = (bf16[4,4,24,4352]{3,2,1,0:T(8,128)(2,1)S(1)}, bf16[4,4,24,4352]{3,2,1,0:T(8,128)(2,1)S(1)}, u32[]{:S(2)}, u32[]{:S(2)}) collective-permute-start(bf16[4,4,24,4352]{3,2,1,0:T(8,128)(2,1)S(1)} %all-to-all-done.3.value), channel_id=1, source_target_pairs={{0,16},{16,0},{1,17},{17,1},{2,18},{18,2},{3,19},{19,3},{4,20},{20... | collective-permute-start | bytes 10027016 | tf_op jit(solution)/shard_map/ppermute | solution.py:82
  262.8 47.1 %collective-permute-start.17 = (s16[3,400,1024]{2,1,0:T(8,128)(2,1)}, s16[3,400,1024]{2,1,0:T(8,128)(2,1)}, u32[]{:S(2)}, u32[]{:S(2)}) collective-permute-start(s16[3,400,1024]{2,1,0:T(8,128)(2,1)} %get-tuple-element.137), channel_id=1, source_target_pairs={{0,16},{16,0},{1,17},{17,1},{2,18},{18,2},{3,19},{19,3},{4,20},{20... | collective-permute-start | bytes 7372808 | tf_op jit(solution)/shard_map/ppermute | solution.py:82
  307.5 51.0 %collective-permute-start.24 = (s16[3,400,1024]{2,1,0:T(8,128)(2,1)}, s16[3,400,1024]{2,1,0:T(8,128)(2,1)}, u32[]{:S(2)}, u32[]{:S(2)}) collective-permute-start(s16[3,400,1024]{2,1,0:T(8,128)(2,1)} %get-tuple-element.161), channel_id=1, source_target_pairs={{0,16},{16,0},{1,17},{17,1},{2,18},{18,2},{3,19},{19,3},{4,20},{20... | collective-permute-start | bytes 7372808 | tf_op jit(solution)/shard_map/ppermute | solution.py:82
  324.4 50.9 %all-to-all-start.6 = ((s16[4,304,1024]{2,1,0:T(8,128)(2,1)}), s16[4,304,1024]{2,1,0:T(8,128)(2,1)}, u32[]{:S(2)}, u32[]{:S(2)}) async-start(s16[4,304,1024]{2,1,0:T(8,128)(2,1)} %send.7), calls=%async_computation.6 | async-start | bytes 4980736 | tf_op jit(solution)/shard_map/all_to_all | solution.py:59
  342.3 99.4 %collective-permute-start.19 = (s16[400,768]{1,0:T(8,128)(2,1)}, s16[400,768]{1,0:T(8,128)(2,1)}, u32[]{:S(2)}, u32[]{:S(2)}) collective-permute-start(s16[400,768]{1,0:T(8,128)(2,1)} %get-tuple-element.144), channel_id=1, source_target_pairs={{0,16},{16,0},{1,17},{17,1},{2,18},{18,2},{3,19},{19,3},{4,20},{20... | collective-permute-start | bytes 1843208 | tf_op jit(solution)/shard_map/ppermute | solution.py:82
  365.0 61.7 %collective-permute-start.25 = (s16[304,1024]{1,0:T(8,128)(2,1)}, s16[304,1024]{1,0:T(8,128)(2,1)}, u32[]{:S(2)}, u32[]{:S(2)}) collective-permute-start(s16[304,1024]{1,0:T(8,128)(2,1)} %get-tuple-element.165), channel_id=1, source_target_pairs={{0,4},{1,5},{2,6},{3,7},{4,0},{5,1},{6,2},{7,3},{8,12},{9,13},{10,... | collective-permute-start | bytes 1867784 | tf_op jit(solution)/shard_map/ppermute | solution.py:70
  372.0 58.0 %collective-permute-start.26 = (s16[304,1024]{1,0:T(8,128)(2,1)}, s16[304,1024]{1,0:T(8,128)(2,1)}, u32[]{:S(2)}, u32[]{:S(2)}) collective-permute-start(s16[304,1024]{1,0:T(8,128)(2,1)} %get-tuple-element.166), channel_id=1, source_target_pairs={{0,8},{1,9},{2,10},{3,11},{4,12},{5,13},{6,14},{7,15},{8,0},{9,1},... | collective-permute-start | bytes 1867784 | tf_op jit(solution)/shard_map/ppermute | solution.py:70
  373.9 62.4 %collective-permute-start.27 = (s16[304,1024]{1,0:T(8,128)(2,1)}, s16[304,1024]{1,0:T(8,128)(2,1)}, u32[]{:S(2)}, u32[]{:S(2)}) collective-permute-start(s16[304,1024]{1,0:T(8,128)(2,1)} %get-tuple-element.167), channel_id=1, source_target_pairs={{0,12},{1,13},{2,14},{3,15},{4,8},{5,9},{6,10},{7,11},{8,4},{9,5},... | collective-permute-start | bytes 1867784 | tf_op jit(solution)/shard_map/ppermute | solution.py:70
  396.5 46.7 %collective-permute-start.21 = (s16[400,1536]{1,0:T(8,128)(2,1)}, s16[400,1536]{1,0:T(8,128)(2,1)S(1)}, u32[]{:S(2)}, u32[]{:S(2)}) collective-permute-start(s16[400,1536]{1,0:T(8,128)(2,1)} %get-tuple-element.146), channel_id=1, source_target_pairs={{0,16},{16,0},{1,17},{17,1},{2,18},{18,2},{3,19},{19,3},{4,20},{20... | collective-permute-start | bytes 3686408 | tf_op jit(solution)/shard_map/ppermute | solution.py:82
  417.7 60.2 %all-to-all-start.7 = ((s16[4,528,768]{2,1,0:T(8,128)(2,1)}), s16[4,528,768]{2,1,0:T(8,128)(2,1)}, u32[]{:S(2)}, u32[]{:S(2)}) async-start(s16[4,528,768]{2,1,0:T(8,128)(2,1)} %copy-done.2), calls=%async_computation.7 | async-start | bytes 6488064 | tf_op jit(solution)/shard_map/all_to_all | solution.py:59
  436.2 66.0 %collective-permute-start.28 = (s16[88,1024]{1,0:T(8,128)(2,1)}, s16[88,1024]{1,0:T(8,128)(2,1)S(1)}, u32[]{:S(2)}, u32[]{:S(2)}) collective-permute-start(s16[88,1024]{1,0:T(8,128)(2,1)} %get-tuple-element.168), channel_id=1, source_target_pairs={{0,4},{1,5},{2,6},{3,7},{4,0},{5,1},{6,2},{7,3},{8,12},{9,13},{10,... | collective-permute-start | bytes 540680 | tf_op jit(solution)/shard_map/ppermute | solution.py:70
  439.4 62.8 %collective-permute-start.29 = (s16[88,1024]{1,0:T(8,128)(2,1)}, s16[88,1024]{1,0:T(8,128)(2,1)S(1)}, u32[]{:S(2)}, u32[]{:S(2)}) collective-permute-start(s16[88,1024]{1,0:T(8,128)(2,1)} %get-tuple-element.169), channel_id=1, source_target_pairs={{0,8},{1,9},{2,10},{3,11},{4,12},{5,13},{6,14},{7,15},{8,0},{9,1},... | collective-permute-start | bytes 540680 | tf_op jit(solution)/shard_map/ppermute | solution.py:70
  441.7 60.5 %collective-permute-start.30 = (s16[88,1024]{1,0:T(8,128)(2,1)}, s16[88,1024]{1,0:T(8,128)(2,1)S(1)}, u32[]{:S(2)}, u32[]{:S(2)}) collective-permute-start(s16[88,1024]{1,0:T(8,128)(2,1)} %get-tuple-element.170), channel_id=1, source_target_pairs={{0,12},{1,13},{2,14},{3,15},{4,8},{5,9},{6,10},{7,11},{8,4},{9,5},... | collective-permute-start | bytes 540680 | tf_op jit(solution)/shard_map/ppermute | solution.py:70
  477.8 78.5 %all-to-all-start.8 = ((s16[4,112,3584]{2,1,0:T(8,128)(2,1)}), s16[4,112,3584]{2,1,0:T(8,128)(2,1)}, u32[]{:S(2)}, u32[]{:S(2)}) async-start(s16[4,112,3584]{2,1,0:T(8,128)(2,1)} %send.8), calls=%async_computation.8 | async-start | bytes 6422528 | tf_op jit(solution)/shard_map/all_to_all | solution.py:59
  492.8 42.2 %collective-permute-start.22 = (s16[2,136,768]{2,1,0:T(8,128)(2,1)}, s16[2,136,768]{2,1,0:T(8,128)(2,1)S(1)}, u32[]{:S(2)}, u32[]{:S(2)}) collective-permute-start(s16[2,136,768]{2,1,0:T(8,128)(2,1)} %pad_add_fusion.3), channel_id=1, source_target_pairs={{0,1},{1,2},{2,3},{3,4},{4,5},{5,6},{6,7},{7,8},{8,9},{9,10},{10,1... | collective-permute-start | bytes 1253384 | tf_op jit(solution)/shard_map/ppermute | solution.py:526
  (123 other events, 2154.5 us)

commit v4 on v3

--- a/solution.py
+++ b/solution.py
@@ -621,7 +621,9 @@
 
 
 def wide_tn(a_high, a_low, b_high, b_low):
-    return dot_tn(a_high, b_high) + dot_tn(a_low, b_high) + dot_tn(a_high, b_low)
+    columns = a_high.shape[1]
+    both = dot_tn(jnp.concatenate([a_high, a_low], axis=1), b_high)
+    return both[:columns] + both[columns:] + dot_tn(a_high, b_low)
 
 
 def pair_probs(query, key_high, key_low, allowed):
@@ -629,7 +631,7 @@
     scores = wide_nt(key_high, key_low, high, low)
     scores = jnp.where(allowed, scores, -1e30)
     weights = jnp.exp(scores - jnp.max(scores, axis=0, keepdims=True))
-    return weights / jnp.sum(weights, axis=0, keepdims=True), high, low
+    return weights * (1.0 / jnp.sum(weights, axis=0, keepdims=True)), high, low
 
 
 def pair_forward(query, key, value, allowed):
@@ -653,13 +655,14 @@
 
 def light_allowed(places, seq, block):
     begin, full_len, prefix = places[0], places[1], places[2 + seq]
-    shape = (3 * W, 2 * W)
+    shape = (3 * W, W)
     key_pos = begin + (block - 1) * W + lax.broadcasted_iota(jnp.int32, shape, 0)
-    lane = lax.broadcasted_iota(jnp.int32, shape, 1)
-    query_pos = begin + block * W + jnp.where(lane < W, lane, lane - W)
+    query_pos = begin + block * W + lax.broadcasted_iota(jnp.int32, shape, 1)
     near = jnp.abs(query_pos - key_pos) < W
     inside = (key_pos >= 0) & (key_pos < full_len)
-    return near & inside & ((key_pos <= query_pos) | (key_pos < prefix))
+    one_head = near & inside & ((key_pos <= query_pos) | (key_pos < prefix))
+    one_head = jnp.where(one_head, 1, 0)
+    return jnp.concatenate([one_head, one_head], axis=1) > 0
 
 
 def light_forward_kernel(places, q, kv, out):

time: 634 us -> 634 us (level)
  no operation moved by 1% of the time
where the time goes in v4:
time: 634 us; the launch traced here: 623 us
  Pallas kernels  209 us (33%)
  starting transfers between devices  118 us (19%)
  waiting for transfers between devices  95 us (15%)
  matrix products  75.8 us (12%)
  local copies, waits for them, and re-layouts  70.5 us (11%)
  other arithmetic  51.8 us (8%)
    dot_general x23, matrix products, product(): jnp.einsum(formula, left_side.astype(f32), right_side.astype(f32), precis...  75.8 us
    ppermute x27, starting transfers between devices, far(): lax.ppermute(v, 'seq', [(i, i ^ GROUP * j) for i in range(devices)])  56.4 us
    pallas_call x2, Pallas kernels, ffn_call(): pl.pallas_call(lambda *refs: ffn_kernel(depth, scored, *refs), name='ffn'...  51.1 us
    ppermute x27, waiting for transfers between devices, far(): lax.ppermute(v, 'seq', [(i, i ^ GROUP * j) for i in range(devices)])  51.1 us
    all_to_all x11, starting transfers between devices, near(): lax.all_to_all(value, 'seq', 0, 0, axis_index_groups=groups, tiled=True)  48.5 us
    all_to_all x11, waiting for transfers between devices, near(): lax.all_to_all(value, 'seq', 0, 0, axis_index_groups=groups, tiled=True)  32.9 us
    pallas_call x2, Pallas kernels, light_call(): pl.pallas_call(kernel, name=kernel.__name__, grid_spec=pltpu.PrefetchScal...  32.3 us
    pallas_call x6, Pallas kernels, send_form(): pl.pallas_call(lambda *refs: send_kernel(spans, layout, received, far, *r...  32.1 us
  transfers between devices with their start and end apart: 54, of which 17 were waited for; matrix products, arithmetic and copies ran while one was open for 26% of the time, Pallas kernels for 28%

profile of v4, /device:TPU:0, one launch (start us, length us, event | category | flops | bytes accessed | tf_op | source)
XLA Modules:
  0.0 622.9 jit_solution(6317863076395956070)
XLA Ops:
  46.3 11.3 %collective-permute-done.4.refs_2_ = s16[2,72,768]{2,1,0:T(8,128)(2,1)S(1)} collective-permute-done((s16[2,72,768]{2,1,0:T(8,128)(2,1)S(1)}, s16[2,72,768]{2,1,0:T(8,128)(2,1)S(1)}, u32[]{:S(2)}, u32[]{:S(2)}) %collective-permute-start.4) | collective-permute-done | bytes 221216 | tf_op jit(solution)/shard_map/ppermute | solution.py:70
  58.7 11.0 %all-to-all-done.value = bf16[4,4,24,3968]{3,2,1,0:T(8,128)(2,1)S(1)} async-done(((bf16[4,4,24,3968]{3,2,1,0:T(8,128)(2,1)}), bf16[4,4,24,3968]{3,2,1,0:T(8,128)(2,1)S(1)}, u32[]{:S(2)}, u32[]{:S(2)}) %all-to-all-start) | async-done | bytes 3047456 | tf_op jit(solution)/shard_map/all_to_all | solution.py:59
  79.1 7.2 %all-to-all-done.1.refs_0_ = bf16[4,24,3072]{2,1,0:T(8,128)(2,1)} async-done(((bf16[4,24,3072]{2,1,0:T(8,128)(2,1)}), bf16[4,24,3072]{2,1,0:T(8,128)(2,1)}, u32[]{:S(2)}, u32[]{:S(2)}) %all-to-all-start.1) | async-done | bytes 589856 | tf_op jit(solution)/shard_map/all_to_all | solution.py:59
  105.5 10.6 %collective-permute-done.10.refs_2_ = bf16[24,4352]{1,0:T(8,128)(2,1)S(1)} collective-permute-done((bf16[24,4352]{1,0:T(8,128)(2,1)S(1)}, bf16[24,4352]{1,0:T(8,128)(2,1)S(1)}, u32[]{:S(2)}, u32[]{:S(2)}) %collective-permute-start.10) | collective-permute-done | bytes 208928 | tf_op jit(solution)/shard_map/ppermute | solution.py:70
  145.1 9.1 %light_forward_kernel.1 = f32[2,256,512]{2,1,0:T(8,128)S(1)} custom-call(s32[4]{0:T(128)S(1)} %pad_add_fusion.8.places, f32[2,256,512]{2,1,0:T(8,128)S(1)} %fusion.36.q, f32[2,512,1024]{2,1,0:T(8,128)} %fusion.3.kv), custom_call_target="tpu_custom_call" | custom-call | flops 8589934592 | bytes 8388608 | tf_op jit(solution)/shard_map/light_forward_kernel/pallas_call | solution.py:708
  154.2 8.0 %collective-permute-done.14.refs_2_ = bf16[4,24,3072]{2,1,0:T(8,128)(2,1)} collective-permute-done((bf16[4,24,3072]{2,1,0:T(8,128)(2,1)}, bf16[4,24,3072]{2,1,0:T(8,128)(2,1)}, u32[]{:S(2)}, u32[]{:S(2)}) %collective-permute-start.14) | collective-permute-done | bytes 589856 | tf_op jit(solution)/shard_map/ppermute | solution.py:70
  183.9 6.4 %multiply_reduce_fusion.4 = (f32[2,512]{1,0:T(2,128)S(1)}, f32[2,512,768]{2,1,0:T(8,128)S(1)}, f32[2,512,768]{2,1,0:T(8,128)}) fusion(f32[768]{0:T(1024)S(1)} %get-tuple-element.281, f32[768]{0:T(1024)S(1)} %get-tuple-element.282, f32[2,1024,768]{2,1,0:T(8,128)S(1)} %bitcast.204, s32[2,512]{1,0:T(2,128)S(1)} %subtract_add_fusion), kind=kOutput, calls=%fused_computation.16 | convolution fusion | flops 4835245056 | bytes 12597248 | tf_op jit(solution)/shard_map/skp,spd->skd/dot_general | solution.py:530
  192.0 6.9 %fusion.8 = f32[2,512,1536]{2,1,0:T(8,128)S(1)} fusion(f32[2,512,768]{2,1,0:T(8,128)S(1)} %get-tuple-element.296, bf16[768,3968]{1,0:T(8,128)(2,1)} %bitcast.180), kind=kOutput, calls=%fused_computation.25 | convolution fusion | flops 7247757312 | bytes 11796480 | tf_op jit(solution)/shard_map/skd,de->ske/dot_general | solution.py:530
  205.1 9.0 %heavy_forward_kernel.1 = f32[2,64,768]{2,1,0:T(8,128)S(1)} custom-call(s32[4]{0:T(128)S(1)} %pad_add_fusion.8.places, s32[2,512,1]{2,1,0:T(8,128)S(1)} %copy-done.25, s32[2,1,128]{2,1,0:T(1,128)S(1)} %bitcast.202, f32[2,64,768]{2,1,0:T(8,128)S(1)} %copy-done.30, f32[2,512,1536]{2,1,0:T(8,128)} %pad_maximum_fusion.kv), custom_call_target="tpu_custom_call" | custom-call | flops 8589934592 | bytes 8388608 | tf_op jit(solution)/shard_map/heavy_forward_kernel/pallas_call | solution.py:754
  238.0 24.8 %ffn.2 = (f32[2,512,768]{2,1,0:T(8,128)}, f32[3,384,1024]{2,1,0:T(8,128)}, s16[3,400,1024]{2,1,0:T(8,128)(2,1)}) custom-call(s32[1]{0:T(128)} %bitcast.1.bit.refs_0_, f32[512,768]{1,0:T(8,128)} %bitcast.210, f32[512,768]{1,0:T(8,128)} %bitcast.207, bf16[768,2048]{1,0:T(8,128)(2,1)} %slice.264.refs_3_.refs_4_, bf16[768,2048]{1,0:T(8,128)(2,1)} %slice.264.refs_3_.refs_4_, ...), custom_call_target="tpu_custom_call" | custom-call | flops 16911433728 | bytes 28311552 | tf_op jit(solution)/shard_map/ffn/pallas_call | solution.py:502
  269.4 26.4 %ffn.3 = (f32[2,512,768]{2,1,0:T(8,128)}, f32[512,1]{1,0:T(8,128)}, f32[3,384,1024]{2,1,0:T(8,128)}, s16[3,400,1024]{2,1,0:T(8,128)(2,1)}) custom-call(s32[1]{0:T(128)} %bitcast.1.bit.refs_0_, f32[512,768]{1,0:T(8,128)} %bitcast.225, f32[512,768]{1,0:T(8,128)} %bitcast.224, bf16[768,2048]{1,0:T(8,128)(2,1)} %slice.270.refs_3_.refs_4_, ...), custom_call_target="tpu_custom_call" | custom-call | flops 16911433728 | bytes 28311552 | tf_op jit(solution)/shard_map/ffn/pallas_call | solution.py:502
  315.4 9.0 %all-to-all-done.5.refs_1_ = s16[4,272,768]{2,1,0:T(8,128)(2,1)S(1)} async-done(((s16[4,272,768]{2,1,0:T(8,128)(2,1)}), s16[4,272,768]{2,1,0:T(8,128)(2,1)S(1)}, u32[]{:S(2)}, u32[]{:S(2)}) %all-to-all-start.5) | async-done | bytes 1671200 | tf_op jit(solution)/shard_map/all_to_all | solution.py:59
  342.3 15.6 %heavy_backward_kernel.1 = (f32[2,64,768]{2,1,0:T(8,128)S(1)}, f32[2,512,1536]{2,1,0:T(8,128)}) custom-call(s32[4]{0:T(128)S(1)} %pad_add_fusion.8.places, s32[2,512,1]{2,1,0:T(8,128)S(1)} %copy-done.26, s32[2,1,128]{2,1,0:T(1,128)S(1)} %bitcast.203, f32[2,64,768]{2,1,0:T(8,128)S(1)} %copy-done.31, f32[2,512,1536]{2,1,0:T(8,128)} %pad_maximum_fusion.kv, ...), custom_call_target="tpu_custom_call" | custom-call | flops 17179869184 | bytes 8388608 | tf_op jit(solution)/shard_map/heavy_backward_kernel/pallas_call | solution.py:754
  365.1 7.0 %collective-permute-start.25 = (s16[304,1024]{1,0:T(8,128)(2,1)}, s16[304,1024]{1,0:T(8,128)(2,1)}, u32[]{:S(2)}, u32[]{:S(2)}) collective-permute-start(s16[304,1024]{1,0:T(8,128)(2,1)} %get-tuple-element.165), channel_id=1, source_target_pairs={{0,4},{1,5},{2,6},{3,7},{4,0},{5,1},{6,2},{7,3},{8,12},{9,13},{10,... | collective-permute-start | bytes 1867784 | tf_op jit(solution)/shard_map/ppermute | solution.py:70
  383.3 13.3 %grad.9 = (f32[384,1536]{1,0:T(8,128)S(1)}, s16[400,1536]{1,0:T(8,128)(2,1)}) custom-call(s32[1]{0:T(128)} %bitcast.1.bit.refs_0_, f32[1024,768]{1,0:T(8,128)} %bitcast.216, f32[1024,1536]{1,0:T(8,128)} %bitcast.206), custom_call_target="tpu_custom_call" | custom-call | flops 7247757312 | bytes 12976128 | tf_op jit(solution)/shard_map/grad/pallas_call | solution.py:371
  396.6 9.5 %multiply_reduce_fusion = (f32[768]{0:T(1024)S(1)}, f32[768]{0:T(1024)}, f32[2,512,768]{2,1,0:T(8,128)S(1)}) fusion(f32[2,512,768]{2,1,0:T(8,128)S(1)} %copy-done.62, f32[2,512]{1,0:T(2,128)S(1)} %subtract_multiply_fusion, f32[2,512,768]{2,1,0:T(8,128)} %get-tuple-element.344, f32[768]{0:T(1024)S(1)} %get-tuple-element.281, ...), kind=kOutput, calls=%fused_computation.11 | convolution fusion | flops 7254047232 | bytes 18101248 | tf_op jit(solution)/shard_map/ske,de->skd/dot_general | solution.py:530
  443.3 10.2 %send.8 = s16[4,112,3584]{2,1,0:T(8,128)(2,1)} custom-call(s32[1]{0:T(128)} %bitcast.2.place.refs_0_, f32[16,24,512]{2,1,0:T(8,128)S(1)} %bitcast.198, f32[16,24,768]{2,1,0:T(8,128)S(1)} %bitcast.194, f32[16,24,768]{2,1,0:T(8,128)S(1)} %bitcast.195, f32[16,24,1536]{2,1,0:T(8,128)} %bitcast.190, s16[400,512]{1,0:T(8,128)(2,1)S(1)} %collective-permute-done.18.refs_5_, ...), custom_call_target="tpu_custom_call" | custom-call | flops 27525120 | bytes 11010048 | tf_op jit(solution)/shard_map/send/pallas_call | solution.py:279
  453.6 23.2 %light_backward_kernel.1 = (f32[2,256,512]{2,1,0:T(8,128)S(1)}, f32[2,512,1024]{2,1,0:T(8,128)}) custom-call(s32[4]{0:T(128)S(1)} %pad_add_fusion.8.places, f32[2,256,512]{2,1,0:T(8,128)S(1)} %copy-done.16, f32[2,512,1024]{2,1,0:T(8,128)} %fusion.3.kv, f32[2,256,512]{2,1,0:T(8,128)S(1)} %copy-done.17), custom_call_target="tpu_custom_call" | custom-call | flops 17179869184 | bytes 8388608 | tf_op jit(solution)/shard_map/light_backward_kernel/pallas_call | solution.py:708
  482.8 8.6 %multiply_reduce_fusion.2 = (f32[768]{0:T(1024)S(1)}, f32[2,512,768]{2,1,0:T(8,128)}, f32[2,512,768]{2,1,0:T(8,128)S(1)}) fusion(f32[2,512]{1,0:T(2,128)S(1)} %copy-done.77, f32[2,128,768]{2,1,0:T(8,128)S(1)} %copy-done.51, f32[2,256,768]{2,1,0:T(8,128)} %param.16, f32[2,128,768]{2,1,0:T(8,128)} %copy-done.52, f32[2,512,1024]{2,1,0:T(8,128)} %get-tuple-element.152, ...), kind=kOutput, calls=%fused_computation.13 | convolution fusion | flops 4835769344 | bytes 15211520 | tf_op jit(solution)/shard_map/ste,de->std/dot_general | solution.py:530
  509.9 9.2 %grad.11 = (f32[384,1024]{1,0:T(8,128)S(1)}, s16[400,1024]{1,0:T(8,128)(2,1)}) custom-call(s32[1]{0:T(128)} %bitcast.1.bit.refs_0_, f32[1024,768]{1,0:T(8,128)S(1)} %fusion.2.refs_1_, f32[1024,1024]{1,0:T(8,128)} %bitcast.214), custom_call_target="tpu_custom_call" | custom-call | flops 4831838208 | bytes 9699328 | tf_op jit(solution)/shard_map/grad/pallas_call | solution.py:371
  527.8 7.2 %collective-permute-done.22 = s16[2,136,768]{2,1,0:T(8,128)(2,1)S(1)} collective-permute-done((s16[2,136,768]{2,1,0:T(8,128)(2,1)}, s16[2,136,768]{2,1,0:T(8,128)(2,1)S(1)}, u32[]{:S(2)}, u32[]{:S(2)}) %collective-permute-start.22) | collective-permute-done | bytes 417824 | tf_op jit(solution)/shard_map/ppermute | solution.py:526
  568.4 5.9 arrived.15
  589.2 8.5 %collective-permute-done.38.refs_3_ = s16[40,3584]{1,0:T(8,128)(2,1)} collective-permute-done((s16[40,3584]{1,0:T(8,128)(2,1)}, s16[40,3584]{1,0:T(8,128)(2,1)}, u32[]{:S(2)}, u32[]{:S(2)}) %collective-permute-start.38) | collective-permute-done | bytes 286752 | tf_op jit(solution)/shard_map/ppermute | solution.py:70
  597.6 5.9 collective-permute-start.40
  (487 shorter events, 356.4 us)
Async XLA Ops:
  13.1 89.6 %collective-permute-start.8 = (s16[2,136,768]{2,1,0:T(8,128)(2,1)}, s16[2,136,768]{2,1,0:T(8,128)(2,1)}, u32[]{:S(2)}, u32[]{:S(2)}) collective-permute-start(s16[2,136,768]{2,1,0:T(8,128)(2,1)} %pad_add_fusion.2), channel_id=1, source_target_pairs={{1,0},{2,1},{3,2},{4,3},{5,4},{6,5},{7,6},{8,7},{9,8},{10,9},{11,1... | collective-permute-start | bytes 1253384 | tf_op jit(solution)/shard_map/ppermute | solution.py:526
  15.2 88.6 %collective-permute-start.7 = (s16[2,136,768]{2,1,0:T(8,128)(2,1)}, s16[2,136,768]{2,1,0:T(8,128)(2,1)}, u32[]{:S(2)}, u32[]{:S(2)}) collective-permute-start(s16[2,136,768]{2,1,0:T(8,128)(2,1)} %pad_add_fusion.1), channel_id=1, source_target_pairs={{0,1},{1,2},{2,3},{3,4},{4,5},{5,6},{6,7},{7,8},{8,9},{9,10},{10,1... | collective-permute-start | bytes 1253384 | tf_op jit(solution)/shard_map/ppermute | solution.py:526
  25.2 44.5 %all-to-all-start = ((bf16[4,4,24,3968]{3,2,1,0:T(8,128)(2,1)}), bf16[4,4,24,3968]{3,2,1,0:T(8,128)(2,1)S(1)}, u32[]{:S(2)}, u32[]{:S(2)}) async-start(bf16[4,4,24,3968]{3,2,1,0:T(8,128)(2,1)} %broadcast_in_dim.51), calls=%async_computation | async-start | bytes 6094848 | tf_op jit(solution)/shard_map/all_to_all | solution.py:59
  69.6 52.4 %collective-permute-start.6 = (bf16[4,4,24,3968]{3,2,1,0:T(8,128)(2,1)S(1)}, bf16[4,4,24,3968]{3,2,1,0:T(8,128)(2,1)}, u32[]{:S(2)}, u32[]{:S(2)}) collective-permute-start(bf16[4,4,24,3968]{3,2,1,0:T(8,128)(2,1)S(1)} %all-to-all-done.value), channel_id=1, source_target_pairs={{0,16},{16,0},{1,17},{17,1},{2,18},{18,2},{3,19},{19,3},{4,20},{20... | collective-permute-start | bytes 9142280 | tf_op jit(solution)/shard_map/ppermute | solution.py:82
  89.4 47.1 %all-to-all-start.2 = ((s16[4,4,2,72,768]{4,3,1,2,0:T(8,128)(2,1)}), s16[4,4,2,72,768]{4,3,1,2,0:T(8,128)(2,1)}, u32[]{:S(2)}, u32[]{:S(2)}) async-start(s16[4,4,2,72,768]{4,3,1,2,0:T(8,128)(2,1)} %broadcast_in_dim.59), calls=%async_computation.2 | async-start | bytes 7077888 | tf_op jit(solution)/shard_map/all_to_all | solution.py:59
  119.5 42.8 %collective-permute-start.14 = (bf16[4,24,3072]{2,1,0:T(8,128)(2,1)}, bf16[4,24,3072]{2,1,0:T(8,128)(2,1)}, u32[]{:S(2)}, u32[]{:S(2)}) collective-permute-start(bf16[4,24,3072]{2,1,0:T(8,128)(2,1)} %all-to-all-done.1.refs_0_), channel_id=1, source_target_pairs={{0,8},{1,9},{2,10},{3,11},{4,12},{5,13},{6,14},{7,15},{8,0},{9,1},... | collective-permute-start | bytes 1769480 | tf_op jit(solution)/shard_map/ppermute | solution.py:70
  120.6 41.7 %collective-permute-start.15 = (bf16[4,24,3072]{2,1,0:T(8,128)(2,1)}, bf16[4,24,3072]{2,1,0:T(8,128)(2,1)}, u32[]{:S(2)}, u32[]{:S(2)}) collective-permute-start(bf16[4,24,3072]{2,1,0:T(8,128)(2,1)} %all-to-all-done.1.refs_0_), channel_id=1, source_target_pairs={{0,12},{1,13},{2,14},{3,15},{4,8},{5,9},{6,10},{7,11},{8,4},{9,5},... | collective-permute-start | bytes 1769480 | tf_op jit(solution)/shard_map/ppermute | solution.py:70
  138.5 42.1 %all-to-all-start.3 = ((bf16[4,4,24,4352]{3,2,1,0:T(8,128)(2,1)}), bf16[4,4,24,4352]{3,2,1,0:T(8,128)(2,1)S(1)}, u32[]{:S(2)}, u32[]{:S(2)}) async-start(bf16[4,4,24,4352]{3,2,1,0:T(8,128)(2,1)} %broadcast_in_dim.58), calls=%async_computation.3 | async-start | bytes 6684672 | tf_op jit(solution)/shard_map/all_to_all | solution.py:59
  165.8 48.3 %collective-permute-start.16 = (bf16[4,4,24,3072]{3,2,1,0:T(8,128)(2,1)}, bf16[4,4,24,3072]{3,2,1,0:T(8,128)(2,1)}, u32[]{:S(2)}, u32[]{:S(2)}) collective-permute-start(bf16[4,4,24,3072]{3,2,1,0:T(8,128)(2,1)} %stack.40.value), channel_id=1, source_target_pairs={{0,16},{16,0},{1,17},{17,1},{2,18},{18,2},{3,19},{19,3},{4,20},{20... | collective-permute-start | bytes 7077896 | tf_op jit(solution)/shard_map/ppermute | solution.py:82
  180.5 42.2 %collective-permute-start.12 = (bf16[4,4,24,4352]{3,2,1,0:T(8,128)(2,1)S(1)}, bf16[4,4,24,4352]{3,2,1,0:T(8,128)(2,1)S(1)}, u32[]{:S(2)}, u32[]{:S(2)}) collective-permute-start(bf16[4,4,24,4352]{3,2,1,0:T(8,128)(2,1)S(1)} %all-to-all-done.3.value), channel_id=1, source_target_pairs={{0,16},{16,0},{1,17},{17,1},{2,18},{18,2},{3,19},{19,3},{4,20},{20... | collective-permute-start | bytes 10027016 | tf_op jit(solution)/shard_map/ppermute | solution.py:82
  262.8 47.1 %collective-permute-start.17 = (s16[3,400,1024]{2,1,0:T(8,128)(2,1)}, s16[3,400,1024]{2,1,0:T(8,128)(2,1)}, u32[]{:S(2)}, u32[]{:S(2)}) collective-permute-start(s16[3,400,1024]{2,1,0:T(8,128)(2,1)} %get-tuple-element.137), channel_id=1, source_target_pairs={{0,16},{16,0},{1,17},{17,1},{2,18},{18,2},{3,19},{19,3},{4,20},{20... | collective-permute-start | bytes 7372808 | tf_op jit(solution)/shard_map/ppermute | solution.py:82
  307.5 51.1 %collective-permute-start.24 = (s16[3,400,1024]{2,1,0:T(8,128)(2,1)}, s16[3,400,1024]{2,1,0:T(8,128)(2,1)}, u32[]{:S(2)}, u32[]{:S(2)}) collective-permute-start(s16[3,400,1024]{2,1,0:T(8,128)(2,1)} %get-tuple-element.161), channel_id=1, source_target_pairs={{0,16},{16,0},{1,17},{17,1},{2,18},{18,2},{3,19},{19,3},{4,20},{20... | collective-permute-start | bytes 7372808 | tf_op jit(solution)/shard_map/ppermute | solution.py:82
  324.4 51.0 %all-to-all-start.6 = ((s16[4,304,1024]{2,1,0:T(8,128)(2,1)}), s16[4,304,1024]{2,1,0:T(8,128)(2,1)}, u32[]{:S(2)}, u32[]{:S(2)}) async-start(s16[4,304,1024]{2,1,0:T(8,128)(2,1)} %send.7), calls=%async_computation.6 | async-start | bytes 4980736 | tf_op jit(solution)/shard_map/all_to_all | solution.py:59
  342.3 99.6 %collective-permute-start.19 = (s16[400,768]{1,0:T(8,128)(2,1)}, s16[400,768]{1,0:T(8,128)(2,1)}, u32[]{:S(2)}, u32[]{:S(2)}) collective-permute-start(s16[400,768]{1,0:T(8,128)(2,1)} %get-tuple-element.144), channel_id=1, source_target_pairs={{0,16},{16,0},{1,17},{17,1},{2,18},{18,2},{3,19},{19,3},{4,20},{20... | collective-permute-start | bytes 1843208 | tf_op jit(solution)/shard_map/ppermute | solution.py:82
  365.1 61.7 %collective-permute-start.25 = (s16[304,1024]{1,0:T(8,128)(2,1)}, s16[304,1024]{1,0:T(8,128)(2,1)}, u32[]{:S(2)}, u32[]{:S(2)}) collective-permute-start(s16[304,1024]{1,0:T(8,128)(2,1)} %get-tuple-element.165), channel_id=1, source_target_pairs={{0,4},{1,5},{2,6},{3,7},{4,0},{5,1},{6,2},{7,3},{8,12},{9,13},{10,... | collective-permute-start | bytes 1867784 | tf_op jit(solution)/shard_map/ppermute | solution.py:70
  372.1 58.0 %collective-permute-start.26 = (s16[304,1024]{1,0:T(8,128)(2,1)}, s16[304,1024]{1,0:T(8,128)(2,1)}, u32[]{:S(2)}, u32[]{:S(2)}) collective-permute-start(s16[304,1024]{1,0:T(8,128)(2,1)} %get-tuple-element.166), channel_id=1, source_target_pairs={{0,8},{1,9},{2,10},{3,11},{4,12},{5,13},{6,14},{7,15},{8,0},{9,1},... | collective-permute-start | bytes 1867784 | tf_op jit(solution)/shard_map/ppermute | solution.py:70
  374.0 62.4 %collective-permute-start.27 = (s16[304,1024]{1,0:T(8,128)(2,1)}, s16[304,1024]{1,0:T(8,128)(2,1)}, u32[]{:S(2)}, u32[]{:S(2)}) collective-permute-start(s16[304,1024]{1,0:T(8,128)(2,1)} %get-tuple-element.167), channel_id=1, source_target_pairs={{0,12},{1,13},{2,14},{3,15},{4,8},{5,9},{6,10},{7,11},{8,4},{9,5},... | collective-permute-start | bytes 1867784 | tf_op jit(solution)/shard_map/ppermute | solution.py:70
  396.6 46.7 %collective-permute-start.21 = (s16[400,1536]{1,0:T(8,128)(2,1)}, s16[400,1536]{1,0:T(8,128)(2,1)S(1)}, u32[]{:S(2)}, u32[]{:S(2)}) collective-permute-start(s16[400,1536]{1,0:T(8,128)(2,1)} %get-tuple-element.146), channel_id=1, source_target_pairs={{0,16},{16,0},{1,17},{17,1},{2,18},{18,2},{3,19},{19,3},{4,20},{20... | collective-permute-start | bytes 3686408 | tf_op jit(solution)/shard_map/ppermute | solution.py:82
  417.8 60.0 %all-to-all-start.7 = ((s16[4,528,768]{2,1,0:T(8,128)(2,1)}), s16[4,528,768]{2,1,0:T(8,128)(2,1)}, u32[]{:S(2)}, u32[]{:S(2)}) async-start(s16[4,528,768]{2,1,0:T(8,128)(2,1)} %copy-done.2), calls=%async_computation.7 | async-start | bytes 6488064 | tf_op jit(solution)/shard_map/all_to_all | solution.py:59
  436.3 65.8 %collective-permute-start.28 = (s16[88,1024]{1,0:T(8,128)(2,1)}, s16[88,1024]{1,0:T(8,128)(2,1)S(1)}, u32[]{:S(2)}, u32[]{:S(2)}) collective-permute-start(s16[88,1024]{1,0:T(8,128)(2,1)} %get-tuple-element.168), channel_id=1, source_target_pairs={{0,4},{1,5},{2,6},{3,7},{4,0},{5,1},{6,2},{7,3},{8,12},{9,13},{10,... | collective-permute-start | bytes 540680 | tf_op jit(solution)/shard_map/ppermute | solution.py:70
  439.5 62.7 %collective-permute-start.29 = (s16[88,1024]{1,0:T(8,128)(2,1)}, s16[88,1024]{1,0:T(8,128)(2,1)S(1)}, u32[]{:S(2)}, u32[]{:S(2)}) collective-permute-start(s16[88,1024]{1,0:T(8,128)(2,1)} %get-tuple-element.169), channel_id=1, source_target_pairs={{0,8},{1,9},{2,10},{3,11},{4,12},{5,13},{6,14},{7,15},{8,0},{9,1},... | collective-permute-start | bytes 540680 | tf_op jit(solution)/shard_map/ppermute | solution.py:70
  441.8 60.3 %collective-permute-start.30 = (s16[88,1024]{1,0:T(8,128)(2,1)}, s16[88,1024]{1,0:T(8,128)(2,1)S(1)}, u32[]{:S(2)}, u32[]{:S(2)}) collective-permute-start(s16[88,1024]{1,0:T(8,128)(2,1)} %get-tuple-element.170), channel_id=1, source_target_pairs={{0,12},{1,13},{2,14},{3,15},{4,8},{5,9},{6,10},{7,11},{8,4},{9,5},... | collective-permute-start | bytes 540680 | tf_op jit(solution)/shard_map/ppermute | solution.py:70
  477.8 78.4 %all-to-all-start.8 = ((s16[4,112,3584]{2,1,0:T(8,128)(2,1)}), s16[4,112,3584]{2,1,0:T(8,128)(2,1)}, u32[]{:S(2)}, u32[]{:S(2)}) async-start(s16[4,112,3584]{2,1,0:T(8,128)(2,1)} %send.8), calls=%async_computation.8 | async-start | bytes 6422528 | tf_op jit(solution)/shard_map/all_to_all | solution.py:59
  492.8 42.2 %collective-permute-start.22 = (s16[2,136,768]{2,1,0:T(8,128)(2,1)}, s16[2,136,768]{2,1,0:T(8,128)(2,1)S(1)}, u32[]{:S(2)}, u32[]{:S(2)}) collective-permute-start(s16[2,136,768]{2,1,0:T(8,128)(2,1)} %pad_add_fusion.3), channel_id=1, source_target_pairs={{0,1},{1,2},{2,3},{3,4},{4,5},{5,6},{6,7},{7,8},{8,9},{9,10},{10,1... | collective-permute-start | bytes 1253384 | tf_op jit(solution)/shard_map/ppermute | solution.py:526
  (123 other events, 2154.4 us)
